TPU v7x, 32 devices: a whole 2x2x4 slice. The times are simulated.
32 devices in a mesh: tile: 4 (over x, core), freq: 8 (over z, y).
Axes of the slice: x: 2, y: 2, z: 4, core: 2. Of those that a mesh axis runs over, the one named last changes fastest.
Arguments:
- sky: bfloat16 [4, 512, 2, 4096], P('tile', 'freq'), may hold values from -6 to 6
- kernel: bfloat16 [4, 8, 2, 4096, 128], P('tile', 'freq'), may hold values from -0.0625 to 0.0625
- data: bfloat16 [8, 2, 128, 512], P('freq'), may hold values from -6 to 6
- block_tiles: int32 [8, 4], P('freq'), may hold values 0 or 1
- length_bin: int32 [8, 128], P('freq'), may hold values from 0 to 31
- wedge_keep: int32 [32, 512], replicated, may hold values 0 or 1
Outputs:
- gradient: float32 [4, 512, 2, 4096], P('tile', 'freq')
All inputs are finite; a program needn't handle non-finite values. No bound on the sum of `block_tiles` on one device may be relied on, other than what follows from the above.
Results may differ from a plain program's by a relative error of at most 0.0027.
Values may be sent and summed in bfloat16 or wider, within the bound.
No kernel may reach another device: no remote copies, remote signals or barrier semaphores. Data moves between devices by JAX's collectives and lax.ppermute only.
A program may use at most 128 MiB of HBM per device.

v0:
```python
import math

import jax
import jax.numpy as jnp
from jax import lax
from jax.sharding import PartitionSpec as P


def delay_tables(length):
    indices = jnp.arange(length, dtype=jnp.int32)
    product = indices[:, None] * indices[None, :] % length
    angle = product.astype(jnp.float32) * (2.0 * math.pi / length)
    return (jnp.cos(angle), jnp.sin(angle))


def real_form(kernel_pair):
    upper_half = jnp.concatenate([kernel_pair[0], kernel_pair[1]], axis=1)
    lower_half = jnp.concatenate([-kernel_pair[1], kernel_pair[0]], axis=1)
    return jnp.concatenate([upper_half, lower_half], axis=0)


def transform(values, table):
    return jnp.einsum("...c,ck->...k", values, table, precision=lax.Precision.HIGHEST)


def keep_table(own_bins, wedge_keep):
    levels = jnp.arange(wedge_keep.shape[0], dtype=jnp.int32)
    one_hot = (own_bins[:, :, None] == levels[None, None, :]).astype(jnp.float32)
    return jnp.einsum(
        "jbl,lk->jbk", one_hot, wedge_keep.astype(jnp.float32), precision=lax.Precision.HIGHEST
    )


def back_project(visibility, data, keep_mask, cosine, sine_table):
    norm_factor = 1.0 / math.sqrt(cosine.shape[0])
    real_vis = visibility[:, 0]
    imag_vis = visibility[:, 1]
    spec_real = (transform(real_vis, cosine) + transform(imag_vis, sine_table)) * norm_factor
    spec_imag = (transform(imag_vis, cosine) - transform(real_vis, sine_table)) * norm_factor
    miss_real = keep_mask * (spec_real - data[:, 0].astype(jnp.float32))
    miss_imag = keep_mask * (spec_imag - data[:, 1].astype(jnp.float32))
    back_real = (transform(miss_real, cosine) - transform(miss_imag, sine_table)) * norm_factor
    back_imag = (transform(miss_imag, cosine) + transform(miss_real, sine_table)) * norm_factor
    return jnp.stack([back_real, back_imag], axis=1).astype(jnp.bfloat16)


def body(sky, kernel, data, block_tiles, length_bin, wedge_keep):
    channels = data.shape[3]
    blocks = kernel.shape[1]
    cell_count = kernel.shape[3]
    base_count = kernel.shape[4]
    local_channels = sky.shape[1]
    tile_pos = lax.axis_index("tile")
    column = jnp.arange(block_tiles.shape[1], dtype=jnp.int32) == tile_pos
    weights = jnp.sum(jnp.where(column[None, :], block_tiles, 0), axis=1).astype(jnp.float32)
    real_forms = jax.vmap(real_form)(kernel[0])
    sky_piece = lax.all_gather(sky, "freq", axis=1, tiled=True)
    flat_rows = sky_piece[0].reshape(sky_piece.shape[1], 2 * cell_count)
    visibility = jnp.einsum(
        "nc,jcb->jbn", flat_rows, real_forms, preferred_element_type=jnp.float32
    )
    partial_vis = visibility * weights[:, None, None]
    cosine, sine_table = delay_tables(channels)
    share_rows = base_count // lax.axis_size("tile")
    visibility = lax.psum_scatter(
        partial_vis.reshape(blocks, 2, base_count, channels),
        "tile",
        scatter_dimension=2,
        tiled=True,
    )
    offset = tile_pos * share_rows
    own_data = lax.dynamic_slice_in_dim(data, offset, share_rows, 2)
    own_bins = lax.dynamic_slice_in_dim(length_bin, offset, share_rows, 1)
    own_back = back_project(
        visibility, own_data, keep_table(own_bins, wedge_keep), cosine, sine_table
    )
    back_field = lax.all_gather(own_back, "tile", axis=2, tiled=True)
    scaled = (back_field * weights[:, None, None, None].astype(jnp.bfloat16)).reshape(
        blocks, 2 * base_count, channels
    )
    partial_value = jnp.einsum(
        "jpn,jcp->nc", scaled, real_forms, preferred_element_type=jnp.float32
    )
    gradient = lax.psum_scatter(
        partial_value.reshape(lax.axis_size("freq") * local_channels, 2, cell_count),
        "freq",
        scatter_dimension=0,
        tiled=True,
    )
    return gradient[None]


def solution(mesh):
    return jax.shard_map(
        body,
        mesh=mesh,
        in_specs=(
            P("tile", "freq", None, None),
            P("tile", "freq", None, None, None),
            P("freq", None, None, None),
            P("freq", None),
            P("freq", None),
            P(),
        ),
        out_specs=P("tile", "freq", None, None),
        check_vma=False,
    )
```

profile of v0, /device:TPU:0, one launch (start us, length us, event | category | flops | bytes accessed | tf_op | source)
XLA Modules:
  0.0 528.3 jit_solution(14876942796513553346)
XLA Ops:
  6.5 0.0 copy-start
  6.5 0.0 all-gather.2.cloned.1.call-start
  6.5 0.7 all-gather.2.cloned.1.call-update
  7.3 0.0 reduce-scatter.3.cloned.1.call-start
  7.3 1.3 fusion.49
  9.3 0.0 copy-done
  9.3 0.1 fusion.48
  9.3 1.4 fusion.74
  10.7 1.7 slice_bitcast_fusion
  12.4 124.8 %all-gather.2.cloned.1.call-done = bf16[1,512,2,4096]{3,2,0,1:T(2,128)(2,1)} async-done(((bf16[1,64,2,4096]{3,2,0,1:T(2,128)(2,1)}), bf16[1,512,2,4096]{3,2,0,1:T(2,128)(2,1)}) %all-gather.2.cloned.1.call-update) | async-done | bytes 8388624 | tf_op jit(solution)/shard_map/all_gather | solution.py:57
  137.2 16.2 %copy.14 = bf16[64,8,2,4096]{3,1,2,0:T(8,128)(2,1)} copy(bf16[64,8,2,4096]{3,2,1,0:T(2,128)(2,1)} %bitcast.55) | data formatting | bytes 16777216
  153.4 7.1 %fusion.2 = f32[256,512]{1,0:T(8,128)} fusion(bf16[512,8192]{1,0:T(8,128)(2,1)} %bitcast.56, f32[]{:T(128)S(6)} %convert_element_type.54, bf16[1,4096,128]{2,1,0:T(8,128)(2,1)S(1)} %get-tuple-element.6, bf16[1,4096,128]{2,1,0:T(8,128)(2,1)S(1)} %fusion.74, bf16[1,4096,128]{2,1,0:T(8,128)(2,1)S(1)} %get-tuple-element.5), kind=kOutput, calls=%fused_computation.6 | convolution fusion | flops 2164391936 | bytes 12058628 | tf_op jit(solution)/shard_map/nc,jcb->jbn/dot_general | solution.py:59
  160.4 0.0 reduce-scatter.3.cloned.1.call-update
  160.5 0.0 reduce-scatter.5.cloned.1.call-start
  160.5 0.0 copy-done.2
  160.5 0.2 fusion.37
  160.7 14.5 %maximum_maximum_fusion = bf16[1,8192,256]{2,1,0:T(8,128)(2,1)} fusion(bf16[1,4096,128]{2,1,0:T(8,128)(2,1)S(1)} %get-tuple-element.6, bf16[1,4096,128]{2,1,0:T(8,128)(2,1)S(1)} %fusion.74, bf16[1,4096,128]{2,1,0:T(8,128)(2,1)S(1)} %get-tuple-element.5), kind=kLoop, calls=%fused_computation | loop fusion | flops 16777216 | bytes 7340032 | tf_op jit(solution)/shard_map/vmap()/concatenate | solution.py:19
  175.2 5.2 reduce-scatter.3.cloned.1.call-done
  180.4 5.5 %fusion.27 = f32[32,512]{1,0:T(8,128)S(1)} fusion(f32[1,2,32,512]{3,2,1,0:T(8,128)} %reduce-scatter.3.cloned.1.call-done), kind=kOutput, calls=%fused_computation.34 | convolution fusion | flops 104333312 | bytes 131072 | tf_op jit(solution)/shard_map/...c,ck->...k/dot_general | solution.py:23
  186.0 5.6 %fusion.12 = f32[32,512]{1,0:T(8,128)S(1)} fusion(f32[32,512]{1,0:T(8,128)S(1)} %fusion.37, f32[32,512]{1,0:T(8,128)S(1)} %fusion.27, f32[1,2,32,512]{3,2,1,0:T(8,128)} %reduce-scatter.3.cloned.1.call-done, bf16[1,2,128,512]{3,2,1,0:T(8,128)(2,1)} %param.8, s32[]{:T(128)S(6)} %add.40, s32[]{:T(128)S(6)} %select_n.29), kind=kOutput, calls=%fused_computation.18 | convolution fusion | flops 104415232 | bytes 294920 | tf_op jit(solution)/shard_map/...c,ck->...k/dot_general | solution.py:23
  191.6 4.8 fusion.25
  196.4 4.7 fusion.31
  201.1 5.6 %fusion.11 = f32[32,512]{1,0:T(8,128)S(1)} fusion(f32[32,512]{1,0:T(8,128)S(1)} %fusion.37, f32[32,512]{1,0:T(8,128)S(1)} %fusion.31, f32[1,2,32,512]{3,2,1,0:T(8,128)S(1)} %copy-done.3, bf16[1,2,128,512]{3,2,1,0:T(8,128)(2,1)} %param.8, s32[]{:T(128)S(6)} %select_n.29), kind=kOutput, calls=%fused_computation.17 | convolution fusion | flops 104415232 | bytes 294916 | tf_op jit(solution)/shard_map/...c,ck->...k/dot_general | solution.py:23
  206.6 4.7 fusion.29
  211.3 4.7 fusion.15
  216.0 4.9 fusion.16
  220.9 5.8 %all_gather.7 = bf16[1,2,128,512]{3,2,1,0:T(8,128)(2,1)S(1)} all-gather(bf16[1,2,32,512]{3,2,1,0:T(8,128)(2,1)S(1)} %pad_maximum_fusion), channel_id=1, replica_groups=mesh['tile'=4,'freq'=8] {'tile'}, dimensions={2}, use_global_device_ids=true | all-gather | bytes 327680 | tf_op jit(solution)/shard_map/all_gather | solution.py:77
  226.7 0.0 copy-done.1
  226.7 8.1 %fusion.75 = f32[512,2,4096]{2,0,1:T(8,128)} fusion(bf16[256,512,1]{1,0,2:T(8,128)(2,1)S(1)} %bitcast.61, bf16[2,4096,256]{2,1,0:T(8,128)(2,1)S(1)} %bitcast.54), kind=kOutput, calls=%fused_computation.84 | convolution fusion | flops 2147483648 | bytes 21233664 | tf_op jit(solution)/shard_map/jpn,jcp->nc/dot_general | solution.py:81
  234.8 0.0 reduce-scatter.5.cloned.1.call-update
  234.8 282.2 %reduce-scatter.5.cloned.1.call-done = f32[64,2,4096]{2,0,1:T(8,128)} async-done(((f32[512,2,4096]{2,0,1:T(8,128)}), f32[64,2,4096]{2,0,1:T(8,128)}) %reduce-scatter.5.cloned.1.call-update) | async-done | bytes 2097168 | tf_op jit(solution)/shard_map/reduce_scatter | solution.py:84
  517.0 4.5 copy.11
  (6 shorter events, 0.0 us)
Async XLA Ops:
  6.5 2.7 copy-start
  6.5 130.6 %all-gather.2.cloned.1.call-start = ((), (), s32[]{:S(2)}) async-start(), calls=%async_computation.2 | async-start | bytes 9437184 | tf_op jit(solution)/shard_map/all_gather | solution.py:57
  7.3 173.2 %reduce-scatter.3.cloned.1.call-start = ((), (), s32[]{:S(2)}) async-start(), calls=%async_computation.3 | async-start | bytes 655360 | tf_op jit(solution)/shard_map/reduce_scatter | solution.py:65
  153.4 7.1 %copy-start.2 = (s32[32,512]{1,0:T(8,128)S(1)}, s32[32,512]{1,0:T(8,128)}, u32[]{:S(2)}) copy-start(s32[32,512]{1,0:T(8,128)} %param.11) | copy-start | bytes 196612
  160.5 356.6 %reduce-scatter.5.cloned.1.call-start = ((), (), s32[]{:S(2)}) async-start(), calls=%async_computation.4 | async-start | bytes 18874368 | tf_op jit(solution)/shard_map/reduce_scatter | solution.py:84
  180.4 16.0 %copy-start.3 = (f32[1,2,32,512]{3,2,1,0:T(8,128)S(1)}, f32[1,2,32,512]{3,2,1,0:T(8,128)}, u32[]{:S(2)}) copy-start(f32[1,2,32,512]{3,2,1,0:T(8,128)} %reduce-scatter.3.cloned.1.call-done) | copy-start | bytes 393220
  201.1 25.6 %copy-start.1 = (bf16[1,8192,256]{2,1,0:T(8,128)(2,1)S(1)}, bf16[1,8192,256]{2,1,0:T(8,128)(2,1)}, u32[]{:S(2)}) copy-start(bf16[1,8192,256]{2,1,0:T(8,128)(2,1)} %maximum_maximum_fusion) | copy-start | bytes 12582916
Sparse Core Ops, SparseCore 0:
  9.5 127.6 all-gather.1
  160.6 19.8 reduce-scatter.2
  235.0 282.0 reduce-scatter.4
where the time goes:
time: 537 us; the launch traced here: 528 us
  waiting for transfers between devices  413 us (77%)
  matrix products  55.7 us (10%)
  local copies, waits for them, and re-layouts  22.5 us (4%)
  other arithmetic  17.2 us (3%)
  between operations  14.1 us (3%)
  blocking collectives  5.79 us (1%)
    reduce_scatter x1, waiting for transfers between devices, body(): lax.psum_scatter(partial_value.reshape(lax.axis_size('freq') * local_chan...  282 us
    all_gather x1, waiting for transfers between devices, body(): sky_piece = lax.all_gather(sky, 'freq', axis=1, tiled=True)  125 us
    dot_general x8, matrix products, transform(): jnp.einsum('...c,ck->...k', values, table, precision=lax.Precision.HIGHEST)  40.3 us
    unnamed x9, local copies, waits for them, and re-layouts  16.2 us
    concatenate x1, other arithmetic, real_form(): return jnp.concatenate([upper_half, lower_half], axis=0)  14.5 us
  transfers between devices with their start and end apart: 3, of which 3 were waited for; matrix products, arithmetic and copies ran while one was open for 4% of the time, Pallas kernels for 0%

commit v1 on v0

v1 whole, which is shorter than its diff:
```python
import math

import jax
import jax.numpy as jnp
from jax import lax
from jax.sharding import Mesh, PartitionSpec as P

SWAP = [(0, 1), (1, 0)]
ENDS = [(0, 1), (1, 0), (2, 3), (3, 2)]
MIDS = [(0, 0), (1, 2), (2, 1), (3, 3)]


def xor_chunks(rows, hi, lo):
    planes, count, cells = rows.shape
    rows = rows.reshape(planes, 2, 2, count // 4, cells)
    rows = jnp.where(hi == 1, rows[:, ::-1], rows)
    rows = jnp.where(lo == 1, rows[:, :, ::-1], rows)
    return rows.reshape(planes * count, cells)


def project(kernel_rows, sky_rows):
    out = lax.dot_general(
        kernel_rows, sky_rows, (((1,), (1,)), ((), ())), preferred_element_type=jnp.float32
    )
    base, chans = out.shape[0] // 2, out.shape[1] // 2
    real = out[:base, :chans] - out[base:, chans:]
    imag = out[:base, chans:] + out[base:, :chans]
    return jnp.stack([real, imag])


def adjoint(field, kernel_rows):
    total = 0.0
    for blk in range(2):
        real, imag = field[blk][0], field[blk][1]
        lhs = jnp.concatenate(
            [jnp.concatenate([real, imag], 1), jnp.concatenate([imag, -real], 1)], 0
        )
        total = total + lax.dot_general(
            lhs, kernel_rows[blk], (((0,), (0,)), ((), ())), preferred_element_type=jnp.float32
        )
    return total


def tables(channels, length):
    product = channels[:, None] * jnp.arange(length, dtype=jnp.int32)[None, :] % length
    angle = product.astype(jnp.float32) * (2.0 * math.pi / length)
    return jnp.cos(angle), jnp.sin(angle)


def mm(a, b):
    return jnp.einsum("bc,ck->bk", a, b, precision=lax.Precision.HIGHEST)


def mmt(a, b):
    return jnp.einsum("bk,ck->bc", a, b, precision=lax.Precision.HIGHEST)


def body(sky, kernel, data, block_tiles, length_bin, wedge_keep):
    length = data.shape[3]
    local, cells = sky.shape[1], sky.shape[3]
    base = kernel.shape[4]
    hi, lo = lax.axis_index("th"), lax.axis_index("tl")
    zpos, ypos = lax.axis_index("outer"), lax.axis_index("inner")
    depth = lax.axis_size("outer")
    tile_pos = hi * 2 + lo
    chunk = base // 4

    column = jnp.arange(block_tiles.shape[1], dtype=jnp.int32) == tile_pos
    weight = jnp.sum(jnp.where(column, block_tiles[0], 0)).astype(jnp.bfloat16)

    own_sky = sky[0].transpose(1, 0, 2).reshape(2 * local, cells)
    own_rows = xor_chunks((kernel[0, 0] * weight).transpose(0, 2, 1), hi, lo)
    kernels = [own_rows, lax.ppermute(own_rows, "inner", SWAP)]

    chain = depth == 4
    if chain:
        is_mid = (zpos == 1) | (zpos == 2)
        e1 = lax.ppermute(own_sky, "outer", ENDS)
        e2 = lax.ppermute(own_sky, "outer", MIDS)
        f1 = lax.ppermute(e2, "outer", ENDS)
        f2 = lax.ppermute(e1, "outer", MIDS)
        g1 = lax.ppermute(f2, "outer", ENDS)
        order = jnp.array([[0, 1, 2, 3], [1, 0, 2, 3], [2, 3, 1, 0], [3, 2, 1, 0]], jnp.int32)[zpos]
        vis = []
        for rows in kernels:
            parts = [
                project(rows, own_sky),
                project(rows, e1),
                jnp.where(is_mid, project(rows, e2), project(rows, f1)),
                jnp.where(is_mid, project(rows, f2), project(rows, g1)),
            ]
            vis.append(jnp.concatenate(parts, axis=2))
    else:
        every = lax.all_gather(own_sky, "outer")
        order = jnp.arange(depth, dtype=jnp.int32)
        vis = [
            jnp.concatenate([project(rows, every[s]) for s in range(depth)], axis=2)
            for rows in kernels
        ]

    def channels(half):
        place = (order[:, None] * 2 + half) * local + jnp.arange(local, dtype=jnp.int32)[None, :]
        return place.reshape(-1)

    own_cos, own_sin = tables(channels(ypos), length)
    far_cos, far_sin = tables(channels(1 - ypos), length)

    count = vis[0].shape[2]
    vis = jnp.stack(vis).reshape(2, 2, 2, 2, chunk, count)
    vis = vis[:, :, :, 0] + lax.ppermute(vis[:, :, :, 1], "tl", SWAP)
    diag = [(0, 3), (1, 2), (2, 1), (3, 0)]
    from_x = lax.ppermute(vis[0, :, 1], "th", SWAP)
    from_y = lax.ppermute(vis[1, :, 0], "inner", SWAP)
    from_d = lax.ppermute(vis[1, :, 1], ("th", "inner"), diag)
    own_vis = vis[0, :, 0] + from_x
    far_vis = from_y + from_d

    norm = 1.0 / math.sqrt(length)
    own_data = lax.dynamic_slice_in_dim(data[0], tile_pos * chunk, chunk, 1).astype(jnp.float32)
    own_bins = lax.dynamic_slice_in_dim(length_bin[0], tile_pos * chunk, chunk, 0)
    keep = wedge_keep[own_bins].astype(jnp.float32)
    cos_sum = [mm(own_vis[p], own_cos) + mm(far_vis[p], far_cos) for p in range(2)]
    sin_sum = [mm(own_vis[p], own_sin) + mm(far_vis[p], far_sin) for p in range(2)]
    miss_real = keep * ((cos_sum[0] + sin_sum[1]) * norm - own_data[0])
    miss_imag = keep * ((cos_sum[1] - sin_sum[0]) * norm - own_data[1])

    def back(cosine, sine):
        real = (mmt(miss_real, cosine) - mmt(miss_imag, sine)) * norm
        imag = (mmt(miss_imag, cosine) + mmt(miss_real, sine)) * norm
        return jnp.stack([real, imag]).astype(jnp.bfloat16)

    own_back, far_back = back(own_cos, own_sin), back(far_cos, far_sin)
    back_x = lax.ppermute(own_back, "th", SWAP)
    back_y = lax.ppermute(far_back, "inner", SWAP)
    back_d = lax.ppermute(far_back, ("th", "inner"), diag)
    half = jnp.stack([jnp.stack([own_back, back_x], 1), jnp.stack([back_y, back_d], 1)])
    other = lax.ppermute(half, "tl", SWAP)
    field = jnp.stack([half, other], 3).reshape(2, 2, base, count)

    def update(slot):
        return adjoint(field[..., slot * local : (slot + 1) * local], kernels)

    if chain:
        low = jnp.bfloat16
        near = lax.ppermute(update(3).astype(low), "outer", ENDS)
        sums3 = (update(3) + near.astype(jnp.float32)).astype(low)
        far3 = lax.ppermute(sums3, "outer", MIDS)
        near2 = lax.ppermute(update(2).astype(low), "outer", ENDS)
        sums2 = (update(2) + near2.astype(jnp.float32)).astype(low)
        far2 = lax.ppermute(sums2, "outer", MIDS)
        zero = jnp.zeros((), jnp.float32)
        last = (update(1) + jnp.where(is_mid, far3.astype(jnp.float32), zero)).astype(low)
        near1 = lax.ppermute(last, "outer", ENDS)
        gradient = update(0) + near1.astype(jnp.float32)
        gradient = gradient + jnp.where(is_mid, far2.astype(jnp.float32), zero)
    else:
        every = jnp.concatenate([update(s) for s in range(depth)], 0)
        gradient = lax.psum_scatter(every, "outer", scatter_dimension=0, tiled=True)
    return gradient.reshape(2, local, cells).transpose(1, 0, 2)[None]


def solution(mesh):
    tiles, freqs = mesh.shape["tile"], mesh.shape["freq"]
    fine = Mesh(mesh.devices.reshape(tiles // 2, 2, freqs // 2, 2), ("th", "tl", "outer", "inner"))
    tile, freq = ("th", "tl"), ("outer", "inner")
    return jax.shard_map(
        body,
        mesh=fine,
        in_specs=(
            P(tile, freq, None, None),
            P(tile, freq, None, None, None),
            P(freq, None, None, None),
            P(freq, None),
            P(freq, None),
            P(),
        ),
        out_specs=P(tile, freq, None, None),
        check_vma=False,
    )
```

time: 537 us -> 266 us (0.50)
  waiting for transfers between devices: 413 us -> 117 us
  starting transfers between devices: 0.08 us -> 32.8 us
  matrix products: 55.7 us -> 78.4 us
  between operations: 14.1 us -> 1.67 us
  other arithmetic: 17.2 us -> 7.51 us
  blocking collectives: 5.79 us -> 0 us
    reduce_scatter x2 -> x0, waiting for transfers between devices: 287 us -> none  [the longest x1 282 us: body(): lax.psum_scatter(partial_value.reshape(lax.axis_size('freq') * local_chan...]
    all_gather x1 -> x0, waiting for transfers between devices: 125 us -> none  [body(): sky_piece = lax.all_gather(sky, 'freq', axis=1, tiled=True)]
    ppermute x0 -> x19, waiting for transfers between devices: none -> 117 us  [the longest x1 21.4 us: body(): near1 = lax.ppermute(last, 'outer', ENDS)]
    ppermute x0 -> x19, starting transfers between devices: none -> 32.8 us  [the longest x1 9.96 us: body(): f2 = lax.ppermute(e1, 'outer', MIDS)]
    dot_general x11 -> x36, matrix products: 55.7 us -> 78.4 us  [the longest x12 27 us: project(): lax.dot_general(kernel_rows, sky_rows, (((1,), (1,)), ((), ())), preferre...]
    concatenate x1 -> x0, other arithmetic: 14.5 us -> none  [real_form(): return jnp.concatenate([upper_half, lower_half], axis=0)]
    unnamed x9 -> x34, local copies, waits for them, and re-layouts: 16.2 us -> 4.85 us
    add x0 -> x14, local copies, waits for them, and re-layouts: none -> 8.5 us  [the longest x12 8.34 us: project(): imag = out[:base, chans:] + out[base:, :chans]]
  transfers between devices with their start and end apart: 3 -> 19, of which waited for: 3 -> 10; matrix products, arithmetic and copies ran while one was open for 4% -> 19% of each run, Pallas kernels for 0% -> 0%
where the time goes in v1:
time: 266 us; the launch traced here: 262 us
  waiting for transfers between devices  117 us (44%)
  matrix products  78.4 us (29%)
  starting transfers between devices  32.8 us (12%)
  local copies, waits for them, and re-layouts  24.1 us (9%)
  other arithmetic  7.51 us (3%)
    dot_general x12, matrix products, project(): lax.dot_general(kernel_rows, sky_rows, (((1,), (1,)), ((), ())), preferre...  27 us
    ppermute x1, waiting for transfers between devices, body(): near1 = lax.ppermute(last, 'outer', ENDS)  21.4 us
    ppermute x1, waiting for transfers between devices, body(): near = lax.ppermute(update(3).astype(low), 'outer', ENDS)  21.1 us
    dot_general x8, matrix products, mmt(): return jnp.einsum('bk,ck->bc', a, b, precision=lax.Precision.HIGHEST)  20.5 us
    ppermute x1, waiting for transfers between devices, body(): near2 = lax.ppermute(update(2).astype(low), 'outer', ENDS)  20 us
    dot_general x8, matrix products, mm(): return jnp.einsum('bc,ck->bk', a, b, precision=lax.Precision.HIGHEST)  19.2 us
    ppermute x1, waiting for transfers between devices, body(): f1 = lax.ppermute(e2, 'outer', ENDS)  18.8 us
    ppermute x1, waiting for transfers between devices, body(): g1 = lax.ppermute(f2, 'outer', ENDS)  15.1 us
  transfers between devices with their start and end apart: 19, of which 10 were waited for; matrix products, arithmetic and copies ran while one was open for 19% of the time, Pallas kernels for 0%

profile of v1, /device:TPU:0, one launch (start us, length us, event | category | flops | bytes accessed | tf_op | source)
XLA Modules:
  0.0 261.6 jit_solution(9193857839487541684)
XLA Ops:
  1.9 3.1 %collective-permute-start = (bf16[128,4096]{1,0:T(8,128)(2,1)S(1)}, bf16[128,4096]{1,0:T(8,128)(2,1)}, u32[]{:S(2)}, u32[]{:S(2)}) collective-permute-start(bf16[128,4096]{1,0:T(8,128)(2,1)S(1)} %bitcast.221), channel_id=1, source_target_pairs={{0,2},{2,0},{4,6},{6,4},{1,3},{3,1},{5,7},{7,5},{8,10},{10,8},{12,... | collective-permute-start | bytes 3145736 | tf_op jit(solution)/shard_map/ppermute | solution.py:78
  7.9 2.9 %copy.13 = bf16[1,1,2,4096,128]{3,4,2,1,0:T(8,128)(2,1)S(1)} copy(bf16[1,1,2,4096,128]{4,3,2,1,0:T(8,128)(2,1)} %param.8) | data formatting | bytes 4194304 | tf_op args[1]
  15.2 13.0 %collective-permute-done = bf16[128,4096]{1,0:T(8,128)(2,1)} collective-permute-done((bf16[128,4096]{1,0:T(8,128)(2,1)S(1)}, bf16[128,4096]{1,0:T(8,128)(2,1)}, u32[]{:S(2)}, u32[]{:S(2)}) %collective-permute-start) | collective-permute-done | bytes 1048608 | tf_op jit(solution)/shard_map/ppermute | solution.py:78
  28.2 10.0 %collective-permute-start.3 = (bf16[128,4096]{1,0:T(8,128)(2,1)}, bf16[128,4096]{1,0:T(8,128)(2,1)}, u32[]{:S(2)}, u32[]{:S(2)}) collective-permute-start(bf16[128,4096]{1,0:T(8,128)(2,1)} %collective-permute-done), channel_id=1, source_target_pairs={{0,0},{2,4},{4,2},{6,6},{1,1},{3,5},{5,3},{7,7},{8,8},{10,12},{12,... | collective-permute-start | bytes 3145736 | tf_op jit(solution)/shard_map/ppermute | solution.py:81
  47.6 18.8 %collective-permute-done.2 = bf16[128,4096]{1,0:T(8,128)(2,1)} collective-permute-done((bf16[128,4096]{1,0:T(8,128)(2,1)}, bf16[128,4096]{1,0:T(8,128)(2,1)}, u32[]{:S(2)}, u32[]{:S(2)}) %collective-permute-start.2) | collective-permute-done | bytes 1048608 | tf_op jit(solution)/shard_map/ppermute | solution.py:80
  69.9 2.7 %fusion.221 = f32[256,128]{0,1:T(8,128)S(1)} fusion(bf16[256,4096]{1,0:T(8,128)(2,1)} %collective-permute-done.5, bf16[128,4096]{1,0:T(8,128)(2,1)} %collective-permute-done.3), kind=kOutput, calls=%fused_computation.304 | convolution fusion | flops 268435456 | bytes 3276800 | tf_op jit(solution)/shard_map/dot_general | solution.py:22
  74.1 2.7 %fusion.220 = f32[256,128]{0,1:T(8,128)S(1)} fusion(bf16[256,4096]{1,0:T(8,128)(2,1)} %collective-permute-done.5, bf16[128,4096]{1,0:T(8,128)(2,1)} %collective-permute-done.2), kind=kOutput, calls=%fused_computation.303 | convolution fusion | flops 268435456 | bytes 3276800 | tf_op jit(solution)/shard_map/dot_general | solution.py:22
  78.3 2.7 %fusion.219 = f32[256,128]{0,1:T(8,128)S(1)} fusion(bf16[256,4096]{1,0:T(8,128)(2,1)} %collective-permute-done.5, bf16[128,4096]{1,0:T(8,128)(2,1)} %collective-permute-done.1), kind=kOutput, calls=%fused_computation.302 | convolution fusion | flops 268435456 | bytes 3276800 | tf_op jit(solution)/shard_map/dot_general | solution.py:22
  82.7 2.7 %fusion.218 = f32[256,128]{0,1:T(8,128)S(1)} fusion(bf16[256,4096]{1,0:T(8,128)(2,1)} %collective-permute-done.5, bf16[128,4096]{1,0:T(8,128)(2,1)} %collective-permute-done), kind=kOutput, calls=%fused_computation.301 | convolution fusion | flops 268435456 | bytes 3276800 | tf_op jit(solution)/shard_map/dot_general | solution.py:22
  88.4 2.4 fusion.217
  91.0 15.1 %collective-permute-done.4 = bf16[128,4096]{1,0:T(8,128)(2,1)} collective-permute-done((bf16[128,4096]{1,0:T(8,128)(2,1)}, bf16[128,4096]{1,0:T(8,128)(2,1)}, u32[]{:S(2)}, u32[]{:S(2)}) %collective-permute-start.4) | collective-permute-done | bytes 1048608 | tf_op jit(solution)/shard_map/ppermute | solution.py:82
  109.2 2.8 %fusion.222 = f32[256,128]{0,1:T(8,128)S(1)} fusion(bf16[256,4096]{1,0:T(8,128)(2,1)} %collective-permute-done.5, bf16[128,4096]{1,0:T(8,128)(2,1)} %collective-permute-done.4), kind=kOutput, calls=%fused_computation.305 | convolution fusion | flops 268435456 | bytes 3276800 | tf_op jit(solution)/shard_map/dot_general | solution.py:22
  128.1 2.5 fusion.43
  130.7 2.4 fusion.47
  135.5 2.4 convolution_add_fusion.6
  140.3 2.7 %fusion.56 = f32[32,256]{1,0:T(8,128)S(1)} fusion(f32[32,512]{1,0:T(8,128)S(1)} %fusion.7, s32[256]{0:T(256)S(1)} %add.216), kind=kOutput, calls=%fused_computation.75 | convolution fusion | flops 52166656 | bytes 99328 | tf_op jit(solution)/shard_map/bk,ck->bc/dot_general | solution.py:55
  142.9 2.5 fusion.39
  150.2 2.5 fusion.53
  152.7 2.5 fusion.37
  155.2 2.9 %fusion.20 = bf16[1,32,256]{2,1,0:T(8,128)(2,1)S(1)} fusion(f32[32,256]{1,0:T(8,128)S(1)} %fusion.39, f32[32,512]{1,0:T(8,128)S(1)} %fusion.11, s32[256]{0:T(256)S(1)} %add.224), kind=kOutput, calls=%fused_computation.38 | convolution fusion | flops 52191232 | bytes 115712 | tf_op jit(solution)/shard_map/bk,ck->bc/dot_general | solution.py:55
  158.1 2.5 fusion.21
  161.9 2.4 collective-permute-start.12
  164.3 2.5 fusion.19
  166.8 2.5 fusion.18
  169.4 3.9 %collective-permute-done.10 = bf16[2,32,256]{2,1,0:T(8,128)(2,1)S(1)} collective-permute-done((bf16[2,32,256]{2,1,0:T(8,128)(2,1)S(1)}, bf16[2,32,256]{2,1,0:T(8,128)(2,1)S(1)}, u32[]{:S(2)}, u32[]{:S(2)}) %collective-permute-start.10) | collective-permute-done | bytes 32800 | tf_op jit(solution)/shard_map/ppermute | solution.py:133
  182.8 21.1 %collective-permute-done.14 = bf16[128,4096]{1,0:T(8,128)(2,1)S(1)} collective-permute-done((bf16[128,4096]{1,0:T(8,128)(2,1)S(1)}, bf16[128,4096]{1,0:T(8,128)(2,1)S(1)}, u32[]{:S(2)}, u32[]{:S(2)}) %collective-permute-start.14) | collective-permute-done | bytes 1048608 | tf_op jit(solution)/shard_map/ppermute | solution.py:145
  205.6 20.0 %collective-permute-done.17 = bf16[128,4096]{1,0:T(8,128)(2,1)S(1)} collective-permute-done((bf16[128,4096]{1,0:T(8,128)(2,1)S(1)}, bf16[128,4096]{1,0:T(8,128)(2,1)S(1)}, u32[]{:S(2)}, u32[]{:S(2)}) %collective-permute-start.17) | collective-permute-done | bytes 1048608 | tf_op jit(solution)/shard_map/ppermute | solution.py:148
  226.6 2.4 fusion.3
  229.0 4.9 %collective-permute-start.16 = (bf16[128,4096]{1,0:T(8,128)(2,1)S(1)}, bf16[128,4096]{1,0:T(8,128)(2,1)S(1)}, u32[]{:S(2)}, u32[]{:S(2)}) collective-permute-start(bf16[128,4096]{1,0:T(8,128)(2,1)S(1)} %fusion.3), channel_id=1, source_target_pairs={{0,2},{2,0},{4,6},{6,4},{1,3},{3,1},{5,7},{7,5},{8,10},{10,8},{12,... | collective-permute-start | bytes 3145736 | tf_op jit(solution)/shard_map/ppermute | solution.py:153
  234.5 21.4 %collective-permute-done.16 = bf16[128,4096]{1,0:T(8,128)(2,1)S(1)} collective-permute-done((bf16[128,4096]{1,0:T(8,128)(2,1)S(1)}, bf16[128,4096]{1,0:T(8,128)(2,1)S(1)}, u32[]{:S(2)}, u32[]{:S(2)}) %collective-permute-start.16) | collective-permute-done | bytes 1048608 | tf_op jit(solution)/shard_map/ppermute | solution.py:153
  255.8 2.6 fusion.2
  258.4 2.9 %copy.49 = f32[2,64,4096]{2,0,1:T(2,128)} copy(f32[2,64,4096]{2,1,0:T(8,128)S(1)} %bitcast.226) | data formatting | bytes 4194304 | tf_op jit(solution)/shard_map/reshape | solution.py:159
  (145 shorter events, 71.6 us)
Async XLA Ops:
  0.0 118.2 %copy-start = (s32[32,512]{1,0:T(8,128)S(1)}, s32[32,512]{1,0:T(8,128)}, u32[]{:S(2)}) copy-start(s32[32,512]{1,0:T(8,128)} %param.12) | copy-start | bytes 196612
  1.9 26.4 %collective-permute-start = (bf16[128,4096]{1,0:T(8,128)(2,1)S(1)}, bf16[128,4096]{1,0:T(8,128)(2,1)}, u32[]{:S(2)}, u32[]{:S(2)}) collective-permute-start(bf16[128,4096]{1,0:T(8,128)(2,1)S(1)} %bitcast.221), channel_id=1, source_target_pairs={{0,2},{2,0},{4,6},{6,4},{1,3},{3,1},{5,7},{7,5},{8,10},{10,8},{12,... | collective-permute-start | bytes 3145736 | tf_op jit(solution)/shard_map/ppermute | solution.py:78
  4.9 33.2 %collective-permute-start.1 = (bf16[128,4096]{1,0:T(8,128)(2,1)S(1)}, bf16[128,4096]{1,0:T(8,128)(2,1)}, u32[]{:S(2)}, u32[]{:S(2)}) collective-permute-start(bf16[128,4096]{1,0:T(8,128)(2,1)S(1)} %bitcast.222), channel_id=1, source_target_pairs={{0,0},{2,4},{4,2},{6,6},{1,1},{3,5},{5,3},{7,7},{8,8},{10,12},{12,... | collective-permute-start | bytes 3145736 | tf_op jit(solution)/shard_map/ppermute | solution.py:79
  11.9 58.0 %collective-permute-start.5 = (bf16[256,4096]{1,0:T(8,128)(2,1)S(1)}, bf16[256,4096]{1,0:T(8,128)(2,1)}, u32[]{:S(2)}, u32[]{:S(2)}) collective-permute-start(bf16[256,4096]{1,0:T(8,128)(2,1)S(1)} %bitcast.210), channel_id=1, source_target_pairs={{0,1},{1,0},{2,3},{3,2},{4,5},{5,4},{6,7},{7,6},{8,9},{9,8},{10,11... | collective-permute-start | bytes 6291464 | tf_op jit(solution)/shard_map/ppermute | solution.py:73
  28.2 15.8 %collective-permute-start.3 = (bf16[128,4096]{1,0:T(8,128)(2,1)}, bf16[128,4096]{1,0:T(8,128)(2,1)}, u32[]{:S(2)}, u32[]{:S(2)}) collective-permute-start(bf16[128,4096]{1,0:T(8,128)(2,1)} %collective-permute-done), channel_id=1, source_target_pairs={{0,0},{2,4},{4,2},{6,6},{1,1},{3,5},{5,3},{7,7},{8,8},{10,12},{12,... | collective-permute-start | bytes 3145736 | tf_op jit(solution)/shard_map/ppermute | solution.py:81
  41.7 24.7 %collective-permute-start.2 = (bf16[128,4096]{1,0:T(8,128)(2,1)}, bf16[128,4096]{1,0:T(8,128)(2,1)}, u32[]{:S(2)}, u32[]{:S(2)}) collective-permute-start(bf16[128,4096]{1,0:T(8,128)(2,1)} %collective-permute-done.1), channel_id=1, source_target_pairs={{0,2},{2,0},{4,6},{6,4},{1,3},{3,1},{5,7},{7,5},{8,10},{10,8},{12,... | collective-permute-start | bytes 3145736 | tf_op jit(solution)/shard_map/ppermute | solution.py:80
  82.4 23.7 %collective-permute-start.4 = (bf16[128,4096]{1,0:T(8,128)(2,1)}, bf16[128,4096]{1,0:T(8,128)(2,1)}, u32[]{:S(2)}, u32[]{:S(2)}) collective-permute-start(bf16[128,4096]{1,0:T(8,128)(2,1)} %collective-permute-done.3), channel_id=1, source_target_pairs={{0,2},{2,0},{4,6},{6,4},{1,3},{3,1},{5,7},{7,5},{8,10},{10,8},{12,... | collective-permute-start | bytes 3145736 | tf_op jit(solution)/shard_map/ppermute | solution.py:82
  108.2 7.3 %copy-start.2 = (f32[128,64]{1,0:T(8,128)S(1)}, f32[128,64]{1,0:T(8,128)}, u32[]{:S(2)}) copy-start(f32[128,64]{1,0:T(8,128)} %copy.19) | copy-start | bytes 98308
  108.2 7.3 %copy-start.3 = (f32[128,64]{1,0:T(8,128)S(1)}, f32[128,64]{1,0:T(8,128)}, u32[]{:S(2)}) copy-start(f32[128,64]{1,0:T(8,128)} %copy.20) | copy-start | bytes 98308
  108.2 7.3 %copy-start.4 = (f32[128,64]{1,0:T(8,128)S(1)}, f32[128,64]{1,0:T(8,128)}, u32[]{:S(2)}) copy-start(f32[128,64]{1,0:T(8,128)} %copy.23) | copy-start | bytes 98308
  108.3 7.3 %copy-start.5 = (f32[128,64]{1,0:T(8,128)S(1)}, f32[128,64]{1,0:T(8,128)}, u32[]{:S(2)}) copy-start(f32[128,64]{1,0:T(8,128)} %copy.24) | copy-start | bytes 98308
  108.3 7.3 %copy-start.6 = (f32[128,64]{1,0:T(8,128)S(1)}, f32[128,64]{1,0:T(8,128)}, u32[]{:S(2)}) copy-start(f32[128,64]{1,0:T(8,128)} %copy.21) | copy-start | bytes 98308
  109.1 7.4 %copy-start.8 = (f32[128,64]{1,0:T(8,128)S(1)}, f32[128,64]{1,0:T(8,128)}, u32[]{:S(2)}) copy-start(f32[128,64]{1,0:T(8,128)} %copy.35) | copy-start | bytes 98308
  109.1 7.4 %copy-start.9 = (f32[128,64]{1,0:T(8,128)S(1)}, f32[128,64]{1,0:T(8,128)}, u32[]{:S(2)}) copy-start(f32[128,64]{1,0:T(8,128)} %copy.36) | copy-start | bytes 98308
  109.1 7.4 %copy-start.10 = (f32[128,64]{1,0:T(8,128)S(1)}, f32[128,64]{1,0:T(8,128)}, u32[]{:S(2)}) copy-start(f32[128,64]{1,0:T(8,128)} %copy.33) | copy-start | bytes 98308
  109.1 7.4 %copy-start.11 = (f32[128,64]{1,0:T(8,128)S(1)}, f32[128,64]{1,0:T(8,128)}, u32[]{:S(2)}) copy-start(f32[128,64]{1,0:T(8,128)} %copy.34) | copy-start | bytes 98308
  109.1 7.4 %copy-start.12 = (f32[128,64]{1,0:T(8,128)S(1)}, f32[128,64]{1,0:T(8,128)}, u32[]{:S(2)}) copy-start(f32[128,64]{1,0:T(8,128)} %copy.31) | copy-start | bytes 98308
  109.2 7.4 %copy-start.13 = (f32[128,64]{1,0:T(8,128)S(1)}, f32[128,64]{1,0:T(8,128)}, u32[]{:S(2)}) copy-start(f32[128,64]{1,0:T(8,128)} %copy.32) | copy-start | bytes 98308
  109.2 8.3 %copy-start.1 = (f32[128,64]{1,0:T(8,128)S(1)}, f32[128,64]{1,0:T(8,128)}, u32[]{:S(2)}) copy-start(f32[128,64]{1,0:T(8,128)} %copy.30) | copy-start | bytes 98308
  117.8 1.6 collective-permute-start.6
  119.4 4.5 %collective-permute-start.8 = (f32[2,32,256]{2,1,0:T(8,128)S(1)}, f32[2,32,256]{2,1,0:T(8,128)S(1)}, u32[]{:S(2)}, u32[]{:S(2)}) collective-permute-start(f32[2,32,256]{2,1,0:T(8,128)S(1)} %get-tuple-element.31), channel_id=1, source_target_pairs={{0,1},{1,0},{2,3},{3,2},{4,5},{5,4},{6,7},{7,6},{8,9},{9,8},{10,11... | collective-permute-start | bytes 196616 | tf_op jit(solution)/shard_map/ppermute | solution.py:113
  120.6 5.2 %collective-permute-start.9 = (f32[2,32,256]{2,1,0:T(8,128)S(1)}, f32[2,32,256]{2,1,0:T(8,128)S(1)}, u32[]{:S(2)}, u32[]{:S(2)}) collective-permute-start(f32[2,32,256]{2,1,0:T(8,128)S(1)} %get-tuple-element.30), channel_id=1, source_target_pairs={{0,17},{1,16},{16,1},{17,0},{2,19},{3,18},{18,3},{19,2},{4,21},{5,... | collective-permute-start | bytes 196616 | tf_op jit(solution)/shard_map/ppermute | solution.py:114
  122.9 12.6 %collective-permute-start.7 = (f32[2,32,256]{2,1,0:T(8,128)S(1)}, f32[2,32,256]{2,1,0:T(8,128)S(1)}, u32[]{:S(2)}, u32[]{:S(2)}) collective-permute-start(f32[2,32,256]{2,1,0:T(8,128)S(1)} %get-tuple-element.29), channel_id=1, source_target_pairs={{0,16},{16,0},{1,17},{17,1},{2,18},{18,2},{3,19},{19,3},{4,20},{20... | collective-permute-start | bytes 196616 | tf_op jit(solution)/shard_map/ppermute | solution.py:112
  160.6 12.7 %collective-permute-start.11 = (bf16[2,32,256]{2,1,0:T(8,128)(2,1)S(1)}, bf16[2,32,256]{2,1,0:T(8,128)(2,1)S(1)}, u32[]{:S(2)}, u32[]{:S(2)}) collective-permute-start(bf16[2,32,256]{2,1,0:T(8,128)(2,1)S(1)} %pad_maximum_fusion.3), channel_id=1, source_target_pairs={{0,1},{1,0},{2,3},{3,2},{4,5},{5,4},{6,7},{7,6},{8,9},{9,8},{10,11... | collective-permute-start | bytes 98312 | tf_op jit(solution)/shard_map/ppermute | solution.py:134
  161.9 11.4 %collective-permute-start.12 = (bf16[2,32,256]{2,1,0:T(8,128)(2,1)S(1)}, bf16[2,32,256]{2,1,0:T(8,128)(2,1)S(1)}, u32[]{:S(2)}, u32[]{:S(2)}) collective-permute-start(bf16[2,32,256]{2,1,0:T(8,128)(2,1)S(1)} %pad_maximum_fusion.3), channel_id=1, source_target_pairs={{0,17},{1,16},{16,1},{17,0},{2,19},{3,18},{18,3},{19,2},{4,21},{5,... | collective-permute-start | bytes 98312 | tf_op jit(solution)/shard_map/ppermute | solution.py:135
  169.3 4.0 %collective-permute-start.10 = (bf16[2,32,256]{2,1,0:T(8,128)(2,1)S(1)}, bf16[2,32,256]{2,1,0:T(8,128)(2,1)S(1)}, u32[]{:S(2)}, u32[]{:S(2)}) collective-permute-start(bf16[2,32,256]{2,1,0:T(8,128)(2,1)S(1)} %pad_maximum_fusion.2), channel_id=1, source_target_pairs={{0,16},{16,0},{1,17},{17,1},{2,18},{18,2},{3,19},{19,3},{4,20},{20... | collective-permute-start | bytes 98312 | tf_op jit(solution)/shard_map/ppermute | solution.py:133
  173.4 1.4 collective-permute-start.13
  177.9 26.1 %collective-permute-start.14 = (bf16[128,4096]{1,0:T(8,128)(2,1)S(1)}, bf16[128,4096]{1,0:T(8,128)(2,1)S(1)}, u32[]{:S(2)}, u32[]{:S(2)}) collective-permute-start(bf16[128,4096]{1,0:T(8,128)(2,1)S(1)} %get-tuple-element.62), channel_id=1, source_target_pairs={{0,2},{2,0},{4,6},{6,4},{1,3},{3,1},{5,7},{7,5},{8,10},{10,8},{12,... | collective-permute-start | bytes 3145736 | tf_op jit(solution)/shard_map/ppermute | solution.py:145
  181.3 44.4 %collective-permute-start.17 = (bf16[128,4096]{1,0:T(8,128)(2,1)S(1)}, bf16[128,4096]{1,0:T(8,128)(2,1)S(1)}, u32[]{:S(2)}, u32[]{:S(2)}) collective-permute-start(bf16[128,4096]{1,0:T(8,128)(2,1)S(1)} %get-tuple-element.60), channel_id=1, source_target_pairs={{0,2},{2,0},{4,6},{6,4},{1,3},{3,1},{5,7},{7,5},{8,10},{10,8},{12,... | collective-permute-start | bytes 3145736 | tf_op jit(solution)/shard_map/ppermute | solution.py:148
  204.1 22.4 %collective-permute-start.15 = (bf16[128,4096]{1,0:T(8,128)(2,1)S(1)}, bf16[128,4096]{1,0:T(8,128)(2,1)S(1)}, u32[]{:S(2)}, u32[]{:S(2)}) collective-permute-start(bf16[128,4096]{1,0:T(8,128)(2,1)S(1)} %add_convert_fusion.1), channel_id=1, source_target_pairs={{0,0},{2,4},{4,2},{6,6},{1,1},{3,5},{5,3},{7,7},{8,8},{10,12},{12,... | collective-permute-start | bytes 3145736 | tf_op jit(solution)/shard_map/ppermute | solution.py:147
  225.8 8.6 %collective-permute-start.18 = (bf16[128,4096]{1,0:T(8,128)(2,1)S(1)}, bf16[128,4096]{1,0:T(8,128)(2,1)S(1)}, u32[]{:S(2)}, u32[]{:S(2)}) collective-permute-start(bf16[128,4096]{1,0:T(8,128)(2,1)S(1)} %add_convert_fusion), channel_id=1, source_target_pairs={{0,0},{2,4},{4,2},{6,6},{1,1},{3,5},{5,3},{7,7},{8,8},{10,12},{12,... | collective-permute-start | bytes 3145736 | tf_op jit(solution)/shard_map/ppermute | solution.py:150
  229.0 26.9 %collective-permute-start.16 = (bf16[128,4096]{1,0:T(8,128)(2,1)S(1)}, bf16[128,4096]{1,0:T(8,128)(2,1)S(1)}, u32[]{:S(2)}, u32[]{:S(2)}) collective-permute-start(bf16[128,4096]{1,0:T(8,128)(2,1)S(1)} %fusion.3), channel_id=1, source_target_pairs={{0,2},{2,0},{4,6},{6,4},{1,3},{3,1},{5,7},{7,5},{8,10},{10,8},{12,... | collective-permute-start | bytes 3145736 | tf_op jit(solution)/shard_map/ppermute | solution.py:153
  (3 other events, 20.1 us)

commit v2 on v1

--- a/solution.py
+++ b/solution.py
@@ -1,13 +1,21 @@
+import functools
 import math
 
 import jax
 import jax.numpy as jnp
 from jax import lax
+from jax.experimental import pallas as pl
+from jax.experimental.pallas import tpu as pltpu
 from jax.sharding import Mesh, PartitionSpec as P
 
 SWAP = [(0, 1), (1, 0)]
 ENDS = [(0, 1), (1, 0), (2, 3), (3, 2)]
 MIDS = [(0, 0), (1, 2), (2, 1), (3, 3)]
+DIAG = [(0, 3), (1, 2), (2, 1), (3, 0)]
+LANES = 128
+STEPS = 4
+VMEM_LIMIT = 40 * 2**20
+NT = (((1,), (1,)), ((), ()))
 
 
 def xor_chunks(rows, hi, lo):
@@ -55,7 +63,7 @@
     return jnp.einsum("bk,ck->bc", a, b, precision=lax.Precision.HIGHEST)
 
 
-def body(sky, kernel, data, block_tiles, length_bin, wedge_keep):
+def any_body(sky, kernel, data, block_tiles, length_bin, wedge_keep):
     length = data.shape[3]
     local, cells = sky.shape[1], sky.shape[3]
     base = kernel.shape[4]
@@ -72,31 +80,12 @@
     own_rows = xor_chunks((kernel[0, 0] * weight).transpose(0, 2, 1), hi, lo)
     kernels = [own_rows, lax.ppermute(own_rows, "inner", SWAP)]
 
-    chain = depth == 4
-    if chain:
-        is_mid = (zpos == 1) | (zpos == 2)
-        e1 = lax.ppermute(own_sky, "outer", ENDS)
-        e2 = lax.ppermute(own_sky, "outer", MIDS)
-        f1 = lax.ppermute(e2, "outer", ENDS)
-        f2 = lax.ppermute(e1, "outer", MIDS)
-        g1 = lax.ppermute(f2, "outer", ENDS)
-        order = jnp.array([[0, 1, 2, 3], [1, 0, 2, 3], [2, 3, 1, 0], [3, 2, 1, 0]], jnp.int32)[zpos]
-        vis = []
-        for rows in kernels:
-            parts = [
-                project(rows, own_sky),
-                project(rows, e1),
-                jnp.where(is_mid, project(rows, e2), project(rows, f1)),
-                jnp.where(is_mid, project(rows, f2), project(rows, g1)),
-            ]
-            vis.append(jnp.concatenate(parts, axis=2))
-    else:
-        every = lax.all_gather(own_sky, "outer")
-        order = jnp.arange(depth, dtype=jnp.int32)
-        vis = [
-            jnp.concatenate([project(rows, every[s]) for s in range(depth)], axis=2)
-            for rows in kernels
-        ]
+    every = lax.all_gather(own_sky, "outer")
+    order = jnp.arange(depth, dtype=jnp.int32)
+    vis = [
+        jnp.concatenate([project(rows, every[s]) for s in range(depth)], axis=2)
+        for rows in kernels
+    ]
 
     def channels(half):
         place = (order[:, None] * 2 + half) * local + jnp.arange(local, dtype=jnp.int32)[None, :]
@@ -108,10 +97,9 @@
     count = vis[0].shape[2]
     vis = jnp.stack(vis).reshape(2, 2, 2, 2, chunk, count)
     vis = vis[:, :, :, 0] + lax.ppermute(vis[:, :, :, 1], "tl", SWAP)
-    diag = [(0, 3), (1, 2), (2, 1), (3, 0)]
     from_x = lax.ppermute(vis[0, :, 1], "th", SWAP)
     from_y = lax.ppermute(vis[1, :, 0], "inner", SWAP)
-    from_d = lax.ppermute(vis[1, :, 1], ("th", "inner"), diag)
+    from_d = lax.ppermute(vis[1, :, 1], ("th", "inner"), DIAG)
     own_vis = vis[0, :, 0] + from_x
     far_vis = from_y + from_d
 
@@ -132,7 +120,7 @@
     own_back, far_back = back(own_cos, own_sin), back(far_cos, far_sin)
     back_x = lax.ppermute(own_back, "th", SWAP)
     back_y = lax.ppermute(far_back, "inner", SWAP)
-    back_d = lax.ppermute(far_back, ("th", "inner"), diag)
+    back_d = lax.ppermute(far_back, ("th", "inner"), DIAG)
     half = jnp.stack([jnp.stack([own_back, back_x], 1), jnp.stack([back_y, back_d], 1)])
     other = lax.ppermute(half, "tl", SWAP)
     field = jnp.stack([half, other], 3).reshape(2, 2, base, count)
@@ -140,23 +128,285 @@
     def update(slot):
         return adjoint(field[..., slot * local : (slot + 1) * local], kernels)
 
-    if chain:
-        low = jnp.bfloat16
-        near = lax.ppermute(update(3).astype(low), "outer", ENDS)
-        sums3 = (update(3) + near.astype(jnp.float32)).astype(low)
-        far3 = lax.ppermute(sums3, "outer", MIDS)
-        near2 = lax.ppermute(update(2).astype(low), "outer", ENDS)
-        sums2 = (update(2) + near2.astype(jnp.float32)).astype(low)
-        far2 = lax.ppermute(sums2, "outer", MIDS)
-        zero = jnp.zeros((), jnp.float32)
-        last = (update(1) + jnp.where(is_mid, far3.astype(jnp.float32), zero)).astype(low)
-        near1 = lax.ppermute(last, "outer", ENDS)
-        gradient = update(0) + near1.astype(jnp.float32)
-        gradient = gradient + jnp.where(is_mid, far2.astype(jnp.float32), zero)
-    else:
-        every = jnp.concatenate([update(s) for s in range(depth)], 0)
-        gradient = lax.psum_scatter(every, "outer", scatter_dimension=0, tiled=True)
+    every = jnp.concatenate([update(s) for s in range(depth)], 0)
+    gradient = lax.psum_scatter(every, "outer", scatter_dimension=0, tiled=True)
     return gradient.reshape(2, local, cells).transpose(1, 0, 2)[None]
+
+
+def wide(tiles):
+    return jnp.concatenate([tiles[t] for t in range(tiles.shape[0])], axis=1)
+
+
+def forward_kernel(
+    place, own_k, far_k, slot0, slot1, mid2, mid3, end2, end3, out, total
+):
+    step = pl.program_id(0)
+    is_mid = place[0] == 1
+
+    @pl.when(step == 0)
+    def _():
+        total[...] = jnp.zeros_like(total)
+
+    rows = jnp.concatenate(
+        [
+            wide(slot0[...]),
+            wide(slot1[...]),
+            wide(jnp.where(is_mid, mid2[...], end2[...])),
+            wide(jnp.where(is_mid, mid3[...], end3[...])),
+        ],
+        axis=0,
+    )
+    for blk, part in enumerate((own_k, far_k)):
+        pair = jnp.concatenate([part[0], part[1]], axis=1)
+        total[blk] += jnp.dot(rows, pair, preferred_element_type=jnp.float32)
+
+    @pl.when(step == STEPS - 1)
+    def _():
+        store_visibility(place, total, out)
+
+
+def store_visibility(place, total, out):
+    base = total.shape[2] // 2
+    local = total.shape[1] // 8
+    chunk = base // 4
+    for blk in range(2):
+        for two in range(2):
+            planes = [[], []]
+            for slot in (2 * two, 2 * two + 1):
+                own = total[blk, slot * 2 * local : (slot + 1) * 2 * local, :]
+                planes[0].append(own[:local, :base] - own[local:, base:])
+                planes[1].append(own[local:, :base] + own[:local, base:])
+            for p in range(2):
+                turned = jnp.concatenate(planes[p], axis=0).T
+                for n in range(4):
+                    m = ((n & 1) ^ place[2]) * 2 + ((n >> 1) ^ place[1])
+                    out[m, blk, p, :, two * 2 * local : (two + 1) * 2 * local] = turned[
+                        n * chunk : (n + 1) * chunk
+                    ]
+
+
+def forward(place, own_k, far_k, slots, chunk):
+    count, rows, _ = slots[0].shape
+    tiles = count // STEPS
+    base = own_k.shape[2]
+    k_spec = pl.BlockSpec((2, tiles * LANES, base), lambda i: (0, i, 0))
+    s_spec = pl.BlockSpec((tiles, rows, LANES), lambda i: (i, 0, 0))
+    shape = (4, 2, 2, chunk, rows * 2)
+    return pl.pallas_call(
+        forward_kernel,
+        grid=(STEPS,),
+        in_specs=[pl.BlockSpec(memory_space=pltpu.SMEM), k_spec, k_spec] + [s_spec] * 6,
+        out_specs=pl.BlockSpec(shape, lambda i: (0,) * 5),
+        out_shape=jax.ShapeDtypeStruct(shape, jnp.float32),
+        scratch_shapes=[pltpu.VMEM((2, 4 * rows, 2 * base), jnp.float32)],
+        compiler_params=pltpu.CompilerParams(vmem_limit_bytes=VMEM_LIMIT),
+        cost_estimate=pl.CostEstimate(
+            flops=16 * rows * count * LANES * 2 * base, bytes_accessed=10 * 2**20, transcendentals=0
+        ),
+        name="forward",
+    )(place, own_k, far_k, *slots)
+
+
+def split(value):
+    high = value.astype(jnp.bfloat16)
+    return high, (value - high.astype(jnp.float32)).astype(jnp.bfloat16)
+
+
+def times(value, high, low, dims):
+    rows = value.shape[0]
+    upper, lower = split(value)
+    both = lax.dot_general(
+        jnp.concatenate([upper, lower], axis=0), high, dims, preferred_element_type=jnp.float32
+    )
+    rest = lax.dot_general(upper, low, dims, preferred_element_type=jnp.float32)
+    return both[:rows] + both[rows:] + rest
+
+
+def delay_kernel(vis0, from_x, from_y, from_d, data, keep, ch, cl, sh, sl, own_out, far_out):
+    length = keep.shape[1]
+    chunk = keep.shape[0]
+    half = length // 2
+    norm = 1.0 / math.sqrt(length)
+    nn = (((1,), (0,)), ((), ()))
+    own = vis0[...] + from_x[...]
+    far = from_y[...] + from_d[...]
+    rows = jnp.concatenate(
+        [jnp.concatenate([own[p], far[p]], axis=1) for p in range(2)], axis=0
+    )
+    cos_sum = times(rows, ch[...], cl[...], nn)
+    sin_sum = times(rows, sh[...], sl[...], nn)
+    kept = keep[...]
+    real = kept * ((cos_sum[:chunk] + sin_sum[chunk:]) * norm - data[0])
+    imag = kept * ((cos_sum[chunk:] - sin_sum[:chunk]) * norm - data[1])
+    miss = jnp.concatenate([real, imag], axis=0)
+    cos_back = times(miss, ch[...], cl[...], NT)
+    sin_back = times(miss, sh[...], sl[...], NT)
+    back_real = ((cos_back[:chunk] - sin_back[chunk:]) * norm).astype(jnp.bfloat16)
+    back_imag = ((cos_back[chunk:] + sin_back[:chunk]) * norm).astype(jnp.bfloat16)
+    own_out[0] = back_real[:, :half]
+    own_out[1] = back_imag[:, :half]
+    far_out[0] = back_real[:, half:]
+    far_out[1] = back_imag[:, half:]
+
+
+def delay(*parts):
+    shape = jax.ShapeDtypeStruct(parts[0].shape, jnp.bfloat16)
+    length = parts[5].shape[1]
+    return pl.pallas_call(
+        delay_kernel,
+        out_shape=(shape, shape),
+        compiler_params=pltpu.CompilerParams(vmem_limit_bytes=VMEM_LIMIT),
+        cost_estimate=pl.CostEstimate(
+            flops=24 * parts[5].shape[0] * length * length,
+            bytes_accessed=8 * length * length,
+            transcendentals=0,
+        ),
+        name="delay",
+    )(*parts)
+
+
+def turn_field(place, half, other, slots, out):
+    chunk, wide_c = half.shape[3], half.shape[4]
+    local = wide_c // 4
+    base = 4 * chunk
+    for blk in range(2):
+        for two in sorted({s // 2 for s in slots}):
+            turned = []
+            for p in range(2):
+                rows = []
+                for n in range(4):
+                    hi, lo = (n >> 1) ^ place[1], (n & 1) ^ place[2]
+                    lanes = slice(two * 2 * local, (two + 1) * 2 * local)
+                    near = half[hi, blk, p, :, lanes].astype(jnp.float32)
+                    away = other[hi, blk, p, :, lanes].astype(jnp.float32)
+                    rows.append(jnp.where(lo == 0, near, away))
+                turned.append(jnp.concatenate(rows, axis=0).T)
+            for s in slots:
+                if s // 2 != two:
+                    continue
+                low = (s % 2) * local
+                real = turned[0][low : low + local].astype(jnp.bfloat16)
+                imag = turned[1][low : low + local].astype(jnp.bfloat16)
+                at = blk * 2 * base
+                i = slots.index(s)
+                out[i * 2 * local : i * 2 * local + local, at : at + base] = real
+                out[i * 2 * local : i * 2 * local + local, at + base : at + 2 * base] = imag
+                out[i * 2 * local + local : (i + 1) * 2 * local, at : at + base] = imag
+                out[i * 2 * local + local : (i + 1) * 2 * local, at + base : at + 2 * base] = -real
+
+
+def adjoint_kernel(slots, place, half, other, own_k, far_k, *rest):
+    outs, field = rest[:-1], rest[-1]
+
+    @pl.when(pl.program_id(0) == 0)
+    def _():
+        turn_field(place, half, other, slots, field)
+
+    cells = jnp.concatenate([own_k[0], own_k[1], far_k[0], far_k[1]], axis=1)
+    sums = lax.dot_general(field[...], cells, NT, preferred_element_type=jnp.float32)
+    rows = sums.shape[0] // len(slots)
+    for i in range(len(slots)):
+        for t in range(outs[i].shape[0]):
+            outs[i][t] = sums[i * rows : (i + 1) * rows, t * LANES : (t + 1) * LANES]
+
+
+def adjoint_parts(place, half, other, own_k, far_k, slots):
+    base = own_k.shape[2]
+    count = own_k.shape[1] // LANES
+    tiles = count // STEPS
+    rows = half.shape[4] // 2
+    k_spec = pl.BlockSpec((2, tiles * LANES, base), lambda i: (0, i, 0))
+    f_spec = pl.BlockSpec(half.shape, lambda i: (0,) * 5)
+    return pl.pallas_call(
+        functools.partial(adjoint_kernel, slots),
+        grid=(STEPS,),
+        in_specs=[pl.BlockSpec(memory_space=pltpu.SMEM), f_spec, f_spec, k_spec, k_spec],
+        out_specs=[pl.BlockSpec((tiles, rows, LANES), lambda i: (i, 0, 0))] * len(slots),
+        out_shape=[jax.ShapeDtypeStruct((count, rows, LANES), jnp.float32)] * len(slots),
+        scratch_shapes=[pltpu.VMEM((rows * len(slots), 4 * base), jnp.bfloat16)],
+        compiler_params=pltpu.CompilerParams(vmem_limit_bytes=VMEM_LIMIT),
+        cost_estimate=pl.CostEstimate(
+            flops=8 * rows * len(slots) * count * LANES * base,
+            bytes_accessed=(4 + 2 * len(slots)) * 2**20,
+            transcendentals=0,
+        ),
+        name="adjoint",
+    )(place, half, other, own_k, far_k)
+
+
+def table_parts(value):
+    high = lax.reduce_precision(value, 8, 7)
+    return high.astype(jnp.bfloat16), (value - high).astype(jnp.bfloat16)
+
+
+def line_body(sky, kernel, data, block_tiles, length_bin, wedge_keep):
+    length = data.shape[3]
+    local, cells = sky.shape[1], sky.shape[3]
+    base = kernel.shape[4]
+    hi, lo = lax.axis_index("th"), lax.axis_index("tl")
+    zpos, ypos = lax.axis_index("outer"), lax.axis_index("inner")
+    tile_pos = hi * 2 + lo
+    chunk = base // 4
+    is_mid = (zpos == 1) | (zpos == 2)
+    place = jnp.stack([is_mid.astype(jnp.int32), hi, lo])
+
+    own_sky = sky[0].reshape(local, 2, cells // LANES, LANES).transpose(2, 1, 0, 3)
+    own_sky = own_sky.reshape(cells // LANES, 2 * local, LANES)
+    column = jnp.arange(block_tiles.shape[1], dtype=jnp.int32) == tile_pos
+    weight = jnp.sum(jnp.where(column, block_tiles[0], 0)).astype(jnp.bfloat16)
+
+    e1 = lax.ppermute(own_sky, "outer", ENDS)
+    e2 = lax.ppermute(own_sky, "outer", MIDS)
+    own_k = kernel[0, 0] * weight
+    far_k = lax.ppermute(own_k, "inner", SWAP)
+    f2 = lax.ppermute(e1, "outer", MIDS)
+    f1 = lax.ppermute(e2, "outer", ENDS)
+    g1 = lax.ppermute(f2, "outer", ENDS)
+
+    order = jnp.array([[0, 1, 2, 3], [1, 0, 2, 3], [2, 3, 1, 0], [3, 2, 1, 0]], jnp.int32)[zpos]
+    halves = jnp.stack([ypos, 1 - ypos])
+    place_of = (order[None, :, None] * 2 + halves[:, None, None]) * local
+    place_of = place_of + jnp.arange(local, dtype=jnp.int32)
+    cosine, sine = tables(place_of.reshape(-1), length)
+    parts = table_parts(cosine) + table_parts(sine)
+    own_data = lax.dynamic_slice_in_dim(data[0], tile_pos * chunk, chunk, 1).astype(jnp.float32)
+    own_bins = lax.dynamic_slice_in_dim(length_bin[0], tile_pos * chunk, chunk, 0)
+    keep = wedge_keep[own_bins].astype(jnp.float32)
+
+    vis = forward(place, own_k, far_k, (own_sky, e1, e2, f2, f1, g1), chunk)
+    vis = vis[:2] + lax.ppermute(vis[2:], "tl", SWAP)
+    from_x = lax.ppermute(vis[1, 0], "th", SWAP)
+    from_y = lax.ppermute(vis[0, 1], "inner", SWAP)
+    from_d = lax.ppermute(vis[1, 1], ("th", "inner"), DIAG)
+    own_back, far_back = delay(vis[0, 0], from_x, from_y, from_d, own_data, keep, *parts)
+    back_x = lax.ppermute(own_back, "th", SWAP)
+    back_y = lax.ppermute(far_back, "inner", SWAP)
+    back_d = lax.ppermute(far_back, ("th", "inner"), DIAG)
+    half = jnp.stack([jnp.stack([own_back, back_y]), jnp.stack([back_x, back_d])])
+    other = lax.ppermute(half, "tl", SWAP)
+
+    (part3,) = adjoint_parts(place, half, other, own_k, far_k, (3,))
+    (part2,) = adjoint_parts(place, half, other, own_k, far_k, (2,))
+    part1, part0 = adjoint_parts(place, half, other, own_k, far_k, (1, 0))
+    low = jnp.bfloat16
+    near3 = lax.ppermute(part3.astype(low), "outer", ENDS)
+    far3 = lax.ppermute((part3 + near3.astype(jnp.float32)).astype(low), "outer", MIDS)
+    near2 = lax.ppermute(part2.astype(low), "outer", ENDS)
+    far2 = lax.ppermute((part2 + near2.astype(jnp.float32)).astype(low), "outer", MIDS)
+    zero = jnp.zeros((), jnp.float32)
+    last = (part1 + jnp.where(is_mid, far3.astype(jnp.float32), zero)).astype(low)
+    near1 = lax.ppermute(last, "outer", ENDS)
+    gradient = part0 + near1.astype(jnp.float32)
+    gradient = gradient + jnp.where(is_mid, far2.astype(jnp.float32), zero)
+    gradient = gradient.reshape(cells // LANES, 2, local, LANES).transpose(2, 1, 0, 3)
+    return gradient.reshape(1, local, 2, cells)
+
+
+def body(sky, kernel, *rest):
+    local, cells = sky.shape[1], sky.shape[3]
+    line = lax.axis_size("outer") == 4 and 2 * local == LANES and kernel.shape[4] == LANES
+    chosen = line_body if line and cells % (STEPS * LANES) == 0 else any_body
+    return chosen(sky, kernel, *rest)
 
 
 def solution(mesh):

time: 266 us -> 198 us (0.74); the launches traced: 262 us -> 197 us
  matrix products: 78.4 us -> 0 us
  Pallas kernels: 0 us -> 18.3 us
  local copies, waits for them, and re-layouts: 24.1 us -> 6.66 us
  starting transfers between devices: 32.8 us -> 49.5 us
  waiting for transfers between devices: 117 us -> 110 us
  other arithmetic: 7.51 us -> 11.3 us
    dot_general x36 -> x0, matrix products: 78.4 us -> none  [the longest x12 27 us: project(): lax.dot_general(kernel_rows, sky_rows, (((1,), (1,)), ((), ())), preferre...]
    pallas_call x0 -> x5, Pallas kernels: none -> 18.3 us  [the longest x3 11.5 us: adjoint_parts(): pl.pallas_call(functools.partial(adjoint_kernel, slots), grid=(STEPS,), i...]
    ppermute x19, starting transfers between devices: 32.8 us -> 49.5 us  [the longest x1 18.5 us: line_body(): g1 = lax.ppermute(f2, 'outer', ENDS)]
    add x14 -> x1, local copies, waits for them, and re-layouts: 8.5 us -> 0.08 us  [line_body(): place_of = place_of + jnp.arange(local, dtype=jnp.int32)]
    sub x12 -> x0, local copies, waits for them, and re-layouts: 7.06 us -> none  [project(): real = out[:base, :chans] - out[base:, chans:]]
    ppermute x19, waiting for transfers between devices: 117 us -> 110 us  [the longest x1 22.2 us: line_body(): near1 = lax.ppermute(last, 'outer', ENDS)]
    convert_element_type x3 -> x8, other arithmetic: 1.26 us -> 7.22 us  [the longest x1 5.04 us: table_parts(): return (high.astype(jnp.bfloat16), (value - high).astype(jnp.bfloat16))]
    unnamed x34 -> x6, local copies, waits for them, and re-layouts: 4.85 us -> 0.01 us
  transfers between devices with their start and end apart: 19 -> 19, of which waited for: 10 -> 12; matrix products, arithmetic and copies ran while one was open for 19% -> 6% of each run, Pallas kernels for 0% -> 4%
where the time goes in v2:
time: 198 us; the launch traced here: 197 us
  waiting for transfers between devices  110 us (56%)
  starting transfers between devices  49.5 us (25%)
  Pallas kernels  18.3 us (9%)
  other arithmetic  11.3 us (6%)
  local copies, waits for them, and re-layouts  6.66 us (3%)
    ppermute x1, waiting for transfers between devices, line_body(): near1 = lax.ppermute(last, 'outer', ENDS)  22.2 us
    ppermute x1, waiting for transfers between devices, line_body(): g1 = lax.ppermute(f2, 'outer', ENDS)  20.7 us
    ppermute x1, waiting for transfers between devices, line_body(): near3 = lax.ppermute(part3.astype(low), 'outer', ENDS)  19.9 us
    ppermute x1, starting transfers between devices, line_body(): g1 = lax.ppermute(f2, 'outer', ENDS)  18.5 us
    ppermute x1, waiting for transfers between devices, line_body(): e1 = lax.ppermute(own_sky, 'outer', ENDS)  17 us
    ppermute x1, waiting for transfers between devices, line_body(): near2 = lax.ppermute(part2.astype(low), 'outer', ENDS)  16.8 us
    pallas_call x3, Pallas kernels, adjoint_parts(): pl.pallas_call(functools.partial(adjoint_kernel, slots), grid=(STEPS,), i...  11.5 us
    ppermute x1, starting transfers between devices, line_body(): f2 = lax.ppermute(e1, 'outer', MIDS)  9.43 us
  transfers between devices with their start and end apart: 19, of which 12 were waited for; matrix products, arithmetic and copies ran while one was open for 6% of the time, Pallas kernels for 4%

profile of v2, /device:TPU:0, one launch (start us, length us, event | category | flops | bytes accessed | tf_op | source)
XLA Modules:
  0.0 196.7 jit_solution(18244254017451193008)
XLA Ops:
  0.0 1.9 reshape_squeeze.3
  2.6 3.1 %collective-permute-start.1 = (bf16[32,128,128]{2,1,0:T(8,128)(2,1)S(1)}, bf16[32,128,128]{2,1,0:T(8,128)(2,1)}, u32[]{:S(2)}, u32[]{:S(2)}) collective-permute-start(bf16[32,128,128]{2,1,0:T(8,128)(2,1)S(1)} %bitcast.46), channel_id=1, source_target_pairs={{0,2},{2,0},{4,6},{6,4},{1,3},{3,1},{5,7},{7,5},{8,10},{10,8},{12,... | collective-permute-start | bytes 3145736 | tf_op jit(solution)/shard_map/ppermute | solution.py:358
  5.7 1.6 collective-permute-start.2
  8.6 1.7 multiply_bitcast_fusion.own_k
  10.4 1.6 collective-permute-start
  12.0 17.0 %collective-permute-done.1.slot1 = bf16[32,128,128]{2,1,0:T(8,128)(2,1)} collective-permute-done((bf16[32,128,128]{2,1,0:T(8,128)(2,1)S(1)}, bf16[32,128,128]{2,1,0:T(8,128)(2,1)}, u32[]{:S(2)}, u32[]{:S(2)}) %collective-permute-start.1) | collective-permute-done | bytes 1048608 | tf_op jit(solution)/shard_map/ppermute | solution.py:358
  29.0 9.4 %collective-permute-start.3 = (bf16[32,128,128]{2,1,0:T(8,128)(2,1)}, bf16[32,128,128]{2,1,0:T(8,128)(2,1)}, u32[]{:S(2)}, u32[]{:S(2)}) collective-permute-start(bf16[32,128,128]{2,1,0:T(8,128)(2,1)} %collective-permute-done.1.slot1), channel_id=1, source_target_pairs={{0,0},{2,4},{4,2},{6,6},{1,1},{3,5},{5,3},{7,7},{8,8},{10,12},{12,... | collective-permute-start | bytes 3145736 | tf_op jit(solution)/shard_map/ppermute | solution.py:362
  38.4 18.5 %collective-permute-start.5 = (bf16[32,128,128]{2,1,0:T(8,128)(2,1)}, bf16[32,128,128]{2,1,0:T(8,128)(2,1)}, u32[]{:S(2)}, u32[]{:S(2)}) collective-permute-start(bf16[32,128,128]{2,1,0:T(8,128)(2,1)} %collective-permute-done.3.mid3), channel_id=1, source_target_pairs={{0,2},{2,0},{4,6},{6,4},{1,3},{3,1},{5,7},{7,5},{8,10},{10,8},{12,... | collective-permute-start | bytes 3145736 | tf_op jit(solution)/shard_map/ppermute | solution.py:364
  58.7 6.1 %collective-permute-done.4.end2 = bf16[32,128,128]{2,1,0:T(8,128)(2,1)} collective-permute-done((bf16[32,128,128]{2,1,0:T(8,128)(2,1)}, bf16[32,128,128]{2,1,0:T(8,128)(2,1)}, u32[]{:S(2)}, u32[]{:S(2)}) %collective-permute-start.4) | collective-permute-done | bytes 1048608 | tf_op jit(solution)/shard_map/ppermute | solution.py:363
  64.8 20.7 %collective-permute-done.5.end3 = bf16[32,128,128]{2,1,0:T(8,128)(2,1)} collective-permute-done((bf16[32,128,128]{2,1,0:T(8,128)(2,1)}, bf16[32,128,128]{2,1,0:T(8,128)(2,1)}, u32[]{:S(2)}, u32[]{:S(2)}) %collective-permute-start.5) | collective-permute-done | bytes 1048608 | tf_op jit(solution)/shard_map/ppermute | solution.py:364
  85.5 5.6 %forward.1 = f32[4,2,2,32,256]{4,3,2,1,0:T(8,128)S(1)} custom-call(s32[3]{0:T(128)S(1)} %pad_add_fusion.place, bf16[2,4096,128]{2,1,0:T(8,128)(2,1)S(1)} %multiply_bitcast_fusion.own_k, bf16[2,4096,128]{2,1,0:T(8,128)(2,1)} %collective-permute-done.far_k, bf16[32,128,128]{2,1,0:T(8,128)(2,1)S(1)} %bitcast.48, ...), custom_call_target="tpu_custom_call" | custom-call | flops 2147483648 | bytes 10485760 | tf_op jit(solution)/shard_map/forward/pallas_call | solution.py:195
  91.2 5.0 %fusion.1 = (bf16[512,512]{1,0:T(8,128)(2,1)S(1)}, bf16[512,512]{1,0:T(8,128)(2,1)S(1)}, bf16[512,512]{1,0:T(8,128)(2,1)S(1)}, bf16[512,512]{1,0:T(8,128)(2,1)S(1)}) fusion(s32[512]{0:T(512)S(1)} %add.97), kind=kLoop, calls=%fused_computation.14 | loop fusion | flops 5767168 | bytes 2099200 | tf_op jit(solution)/shard_map/convert_element_type | solution.py:339
  96.4 1.4 collective-permute-start.7
  97.8 1.5 collective-permute-start.8
  99.9 0.8 bitcast_convert_fusion.data
  100.9 1.1 collective-permute-done.8.from_y
  102.0 2.4 %collective-permute-done.9.from_d = f32[2,32,256]{2,1,0:T(8,128)S(1)} collective-permute-done((f32[2,32,256]{2,1,0:T(8,128)S(1)}, f32[2,32,256]{2,1,0:T(8,128)S(1)}, u32[]{:S(2)}, u32[]{:S(2)}) %collective-permute-start.9) | collective-permute-done | bytes 65568 | tf_op jit(solution)/shard_map/ppermute | solution.py:380
  104.4 1.2 delay.1
  106.2 1.5 collective-permute-start.12
  107.7 1.5 collective-permute-start.11
  109.6 2.0 %collective-permute-done.11 = bf16[2,32,256]{2,1,0:T(8,128)(2,1)S(1)} collective-permute-done((bf16[2,32,256]{2,1,0:T(8,128)(2,1)S(1)}, bf16[2,32,256]{2,1,0:T(8,128)(2,1)S(1)}, u32[]{:S(2)}, u32[]{:S(2)}) %collective-permute-start.11) | collective-permute-done | bytes 32800 | tf_op jit(solution)/shard_map/ppermute | solution.py:382
  111.7 1.3 collective-permute-done.13.other
  113.0 3.8 %adjoint.4 = f32[32,128,128]{2,1,0:T(8,128)S(1)} custom-call(s32[3]{0:T(128)S(1)} %pad_add_fusion.place, bf16[2,2,2,32,256]{4,3,2,1,0:T(8,128)(2,1)S(1)} %pad_maximum_fusion.half, bf16[2,2,2,32,256]{4,3,2,1,0:T(8,128)(2,1)S(1)} %collective-permute-done.13.other, bf16[2,4096,128]{2,1,0:T(8,128)(2,1)S(1)} %multiply_bitcast_fusion.own_k, ...), custom_call_target="tpu_custom_call" | custom-call | flops 536870912 | bytes 6291456 | tf_op jit(solution)/shard_map/adjoint/pallas_call | solution.py:320
  117.4 3.8 %adjoint.5 = f32[32,128,128]{2,1,0:T(8,128)S(1)} custom-call(s32[3]{0:T(128)S(1)} %pad_add_fusion.place, bf16[2,2,2,32,256]{4,3,2,1,0:T(8,128)(2,1)S(1)} %pad_maximum_fusion.half, bf16[2,2,2,32,256]{4,3,2,1,0:T(8,128)(2,1)S(1)} %collective-permute-done.13.other, bf16[2,4096,128]{2,1,0:T(8,128)(2,1)S(1)} %multiply_bitcast_fusion.own_k, ...), custom_call_target="tpu_custom_call" | custom-call | flops 536870912 | bytes 6291456 | tf_op jit(solution)/shard_map/adjoint/pallas_call | solution.py:320
  121.4 1.8 collective-permute-start.17
  123.2 19.9 %collective-permute-done.14 = bf16[32,128,128]{2,1,0:T(8,128)(2,1)S(1)} collective-permute-done((bf16[32,128,128]{2,1,0:T(8,128)(2,1)S(1)}, bf16[32,128,128]{2,1,0:T(8,128)(2,1)S(1)}, u32[]{:S(2)}, u32[]{:S(2)}) %collective-permute-start.14) | collective-permute-done | bytes 1048608 | tf_op jit(solution)/shard_map/ppermute | solution.py:392
  144.2 3.9 %adjoint.3 = (f32[32,128,128]{2,1,0:T(8,128)S(1)}, f32[32,128,128]{2,1,0:T(8,128)S(1)}) custom-call(s32[3]{0:T(128)S(1)} %pad_add_fusion.place, bf16[2,2,2,32,256]{4,3,2,1,0:T(8,128)(2,1)S(1)} %pad_maximum_fusion.half, bf16[2,2,2,32,256]{4,3,2,1,0:T(8,128)(2,1)S(1)} %collective-permute-done.13.other, bf16[2,4096,128]{2,1,0:T(8,128)(2,1)S(1)} %multiply_bitcast_fusion.own_k, ...), custom_call_target="tpu_custom_call" | custom-call | flops 1073741824 | bytes 8388608 | tf_op jit(solution)/shard_map/adjoint/pallas_call | solution.py:320
  148.1 16.8 %collective-permute-done.17 = bf16[32,128,128]{2,1,0:T(8,128)(2,1)S(1)} collective-permute-done((bf16[32,128,128]{2,1,0:T(8,128)(2,1)S(1)}, bf16[32,128,128]{2,1,0:T(8,128)(2,1)S(1)}, u32[]{:S(2)}, u32[]{:S(2)}) %collective-permute-start.17) | collective-permute-done | bytes 1048608 | tf_op jit(solution)/shard_map/ppermute | solution.py:394
  166.3 4.4 %collective-permute-start.16 = (bf16[32,128,128]{2,1,0:T(8,128)(2,1)S(1)}, bf16[32,128,128]{2,1,0:T(8,128)(2,1)S(1)}, u32[]{:S(2)}, u32[]{:S(2)}) collective-permute-start(bf16[32,128,128]{2,1,0:T(8,128)(2,1)S(1)} %add_convert_fusion.1), channel_id=1, source_target_pairs={{0,2},{2,0},{4,6},{6,4},{1,3},{3,1},{5,7},{7,5},{8,10},{10,8},{12,... | collective-permute-start | bytes 3145736 | tf_op jit(solution)/shard_map/ppermute | solution.py:398
  170.6 22.2 %collective-permute-done.16 = bf16[32,128,128]{2,1,0:T(8,128)(2,1)S(1)} collective-permute-done((bf16[32,128,128]{2,1,0:T(8,128)(2,1)S(1)}, bf16[32,128,128]{2,1,0:T(8,128)(2,1)S(1)}, u32[]{:S(2)}, u32[]{:S(2)}) %collective-permute-start.16) | collective-permute-done | bytes 1048608 | tf_op jit(solution)/shard_map/ppermute | solution.py:398
  193.3 1.2 copy.9
  194.6 2.1 %reshape.103 = f32[1,64,2,4096]{3,2,1,0:T(2,128)} reshape(f32[64,2,32,128]{3,2,1,0:T(8,128)S(1)} %copy.9) | data formatting | bytes 4194304 | tf_op jit(solution)/shard_map/reshape | solution.py:402
  (47 shorter events, 8.8 us)
Async XLA Ops:
  0.0 57.0 %copy-start = (s32[32,512]{1,0:T(8,128)S(1)}, s32[32,512]{1,0:T(8,128)}, u32[]{:S(2)}) copy-start(s32[32,512]{1,0:T(8,128)} %param.12) | copy-start | bytes 196612
  0.0 7.3 %copy-start.1 = (s32[1,4]{1,0:T(1,128)S(1)}, s32[1,4]{1,0:T(1,128)}, u32[]{:S(2)}) copy-start(s32[1,4]{1,0:T(1,128)} %param.10) | copy-start | bytes 52
  2.6 26.4 %collective-permute-start.1 = (bf16[32,128,128]{2,1,0:T(8,128)(2,1)S(1)}, bf16[32,128,128]{2,1,0:T(8,128)(2,1)}, u32[]{:S(2)}, u32[]{:S(2)}) collective-permute-start(bf16[32,128,128]{2,1,0:T(8,128)(2,1)S(1)} %bitcast.46), channel_id=1, source_target_pairs={{0,2},{2,0},{4,6},{6,4},{1,3},{3,1},{5,7},{7,5},{8,10},{10,8},{12,... | collective-permute-start | bytes 3145736 | tf_op jit(solution)/shard_map/ppermute | solution.py:358
  5.7 32.7 %collective-permute-start.2 = (bf16[32,128,128]{2,1,0:T(8,128)(2,1)S(1)}, bf16[32,128,128]{2,1,0:T(8,128)(2,1)}, u32[]{:S(2)}, u32[]{:S(2)}) collective-permute-start(bf16[32,128,128]{2,1,0:T(8,128)(2,1)S(1)} %bitcast.47), channel_id=1, source_target_pairs={{0,0},{2,4},{4,2},{6,6},{1,1},{3,5},{5,3},{7,7},{8,8},{10,12},{12,... | collective-permute-start | bytes 3145736 | tf_op jit(solution)/shard_map/ppermute | solution.py:359
  8.6 48.3 %copy-start.2 = (s32[1,128]{1,0:T(1,128)S(1)}, s32[1,128]{1,0:T(1,128)}, u32[]{:S(2)}) copy-start(s32[1,128]{1,0:T(1,128)} %param.11) | copy-start | bytes 1540
  10.4 48.3 %collective-permute-start = (bf16[2,4096,128]{2,1,0:T(8,128)(2,1)S(1)}, bf16[2,4096,128]{2,1,0:T(8,128)(2,1)}, u32[]{:S(2)}, u32[]{:S(2)}) collective-permute-start(bf16[2,4096,128]{2,1,0:T(8,128)(2,1)S(1)} %multiply_bitcast_fusion.own_k), channel_id=1, source_target_pairs={{0,1},{1,0},{2,3},{3,2},{4,5},{5,4},{6,7},{7,6},{8,9},{9,8},{10,11... | collective-permute-start | bytes 6291464 | tf_op jit(solution)/shard_map/ppermute | solution.py:361
  29.0 9.4 %collective-permute-start.3 = (bf16[32,128,128]{2,1,0:T(8,128)(2,1)}, bf16[32,128,128]{2,1,0:T(8,128)(2,1)}, u32[]{:S(2)}, u32[]{:S(2)}) collective-permute-start(bf16[32,128,128]{2,1,0:T(8,128)(2,1)} %collective-permute-done.1.slot1), channel_id=1, source_target_pairs={{0,0},{2,4},{4,2},{6,6},{1,1},{3,5},{5,3},{7,7},{8,8},{10,12},{12,... | collective-permute-start | bytes 3145736 | tf_op jit(solution)/shard_map/ppermute | solution.py:362
  38.4 26.4 %collective-permute-start.4 = (bf16[32,128,128]{2,1,0:T(8,128)(2,1)}, bf16[32,128,128]{2,1,0:T(8,128)(2,1)}, u32[]{:S(2)}, u32[]{:S(2)}) collective-permute-start(bf16[32,128,128]{2,1,0:T(8,128)(2,1)} %collective-permute-done.2.mid2), channel_id=1, source_target_pairs={{0,2},{2,0},{4,6},{6,4},{1,3},{3,1},{5,7},{7,5},{8,10},{10,8},{12,... | collective-permute-start | bytes 3145736 | tf_op jit(solution)/shard_map/ppermute | solution.py:363
  38.4 47.1 %collective-permute-start.5 = (bf16[32,128,128]{2,1,0:T(8,128)(2,1)}, bf16[32,128,128]{2,1,0:T(8,128)(2,1)}, u32[]{:S(2)}, u32[]{:S(2)}) collective-permute-start(bf16[32,128,128]{2,1,0:T(8,128)(2,1)} %collective-permute-done.3.mid3), channel_id=1, source_target_pairs={{0,2},{2,0},{4,6},{6,4},{1,3},{3,1},{5,7},{7,5},{8,10},{10,8},{12,... | collective-permute-start | bytes 3145736 | tf_op jit(solution)/shard_map/ppermute | solution.py:364
  91.1 5.1 %collective-permute-start.6 = (f32[2,2,2,32,256]{4,3,2,1,0:T(8,128)S(1)}, f32[2,2,2,32,256]{4,3,2,1,0:T(8,128)S(1)}, u32[]{:S(2)}, u32[]{:S(2)}) collective-permute-start(f32[2,2,2,32,256]{4,3,2,1,0:T(8,128)S(1)} %slice.27), channel_id=1, source_target_pairs={{0,8},{8,0},{1,9},{9,1},{2,10},{10,2},{3,11},{11,3},{4,12},{12,4},... | collective-permute-start | bytes 786440 | tf_op jit(solution)/shard_map/ppermute | solution.py:377
  96.4 4.5 %collective-permute-start.7 = (f32[2,32,256]{2,1,0:T(8,128)S(1)}, f32[2,32,256]{2,1,0:T(8,128)S(1)}, u32[]{:S(2)}, u32[]{:S(2)}) collective-permute-start(f32[2,32,256]{2,1,0:T(8,128)S(1)} %get-tuple-element.15), channel_id=1, source_target_pairs={{0,16},{16,0},{1,17},{17,1},{2,18},{18,2},{3,19},{19,3},{4,20},{20... | collective-permute-start | bytes 196616 | tf_op jit(solution)/shard_map/ppermute | solution.py:378
  97.8 4.3 %collective-permute-start.8 = (f32[2,32,256]{2,1,0:T(8,128)S(1)}, f32[2,32,256]{2,1,0:T(8,128)S(1)}, u32[]{:S(2)}, u32[]{:S(2)}) collective-permute-start(f32[2,32,256]{2,1,0:T(8,128)S(1)} %get-tuple-element.14), channel_id=1, source_target_pairs={{0,1},{1,0},{2,3},{3,2},{4,5},{5,4},{6,7},{7,6},{8,9},{9,8},{10,11... | collective-permute-start | bytes 196616 | tf_op jit(solution)/shard_map/ppermute | solution.py:379
  99.3 5.2 %collective-permute-start.9 = (f32[2,32,256]{2,1,0:T(8,128)S(1)}, f32[2,32,256]{2,1,0:T(8,128)S(1)}, u32[]{:S(2)}, u32[]{:S(2)}) collective-permute-start(f32[2,32,256]{2,1,0:T(8,128)S(1)} %get-tuple-element.13), channel_id=1, source_target_pairs={{0,17},{1,16},{16,1},{17,0},{2,19},{3,18},{18,3},{19,2},{4,21},{5,... | collective-permute-start | bytes 196616 | tf_op jit(solution)/shard_map/ppermute | solution.py:380
  105.6 4.0 %collective-permute-start.10 = (bf16[2,32,256]{2,1,0:T(8,128)(2,1)S(1)}, bf16[2,32,256]{2,1,0:T(8,128)(2,1)S(1)}, u32[]{:S(2)}, u32[]{:S(2)}) collective-permute-start(bf16[2,32,256]{2,1,0:T(8,128)(2,1)S(1)} %get-tuple-element.10), channel_id=1, source_target_pairs={{0,1},{1,0},{2,3},{3,2},{4,5},{5,4},{6,7},{7,6},{8,9},{9,8},{10,11... | collective-permute-start | bytes 98312 | tf_op jit(solution)/shard_map/ppermute | solution.py:383
  106.2 5.4 %collective-permute-start.12 = (bf16[2,32,256]{2,1,0:T(8,128)(2,1)S(1)}, bf16[2,32,256]{2,1,0:T(8,128)(2,1)S(1)}, u32[]{:S(2)}, u32[]{:S(2)}) collective-permute-start(bf16[2,32,256]{2,1,0:T(8,128)(2,1)S(1)} %get-tuple-element.10), channel_id=1, source_target_pairs={{0,17},{1,16},{16,1},{17,0},{2,19},{3,18},{18,3},{19,2},{4,21},{5,... | collective-permute-start | bytes 98312 | tf_op jit(solution)/shard_map/ppermute | solution.py:384
  107.7 3.9 %collective-permute-start.11 = (bf16[2,32,256]{2,1,0:T(8,128)(2,1)S(1)}, bf16[2,32,256]{2,1,0:T(8,128)(2,1)S(1)}, u32[]{:S(2)}, u32[]{:S(2)}) collective-permute-start(bf16[2,32,256]{2,1,0:T(8,128)(2,1)S(1)} %get-tuple-element.9), channel_id=1, source_target_pairs={{0,16},{16,0},{1,17},{17,1},{2,18},{18,2},{3,19},{19,3},{4,20},{20... | collective-permute-start | bytes 98312 | tf_op jit(solution)/shard_map/ppermute | solution.py:382
  111.6 1.4 collective-permute-start.13
  117.1 26.1 %collective-permute-start.14 = (bf16[32,128,128]{2,1,0:T(8,128)(2,1)S(1)}, bf16[32,128,128]{2,1,0:T(8,128)(2,1)S(1)}, u32[]{:S(2)}, u32[]{:S(2)}) collective-permute-start(bf16[32,128,128]{2,1,0:T(8,128)(2,1)S(1)} %convert_element_type.66), channel_id=1, source_target_pairs={{0,2},{2,0},{4,6},{6,4},{1,3},{3,1},{5,7},{7,5},{8,10},{10,8},{12,... | collective-permute-start | bytes 3145736 | tf_op jit(solution)/shard_map/ppermute | solution.py:392
  121.4 43.4 %collective-permute-start.17 = (bf16[32,128,128]{2,1,0:T(8,128)(2,1)S(1)}, bf16[32,128,128]{2,1,0:T(8,128)(2,1)S(1)}, u32[]{:S(2)}, u32[]{:S(2)}) collective-permute-start(bf16[32,128,128]{2,1,0:T(8,128)(2,1)S(1)} %convert_element_type.72), channel_id=1, source_target_pairs={{0,2},{2,0},{4,6},{6,4},{1,3},{3,1},{5,7},{7,5},{8,10},{10,8},{12,... | collective-permute-start | bytes 3145736 | tf_op jit(solution)/shard_map/ppermute | solution.py:394
  143.5 22.4 %collective-permute-start.15 = (bf16[32,128,128]{2,1,0:T(8,128)(2,1)S(1)}, bf16[32,128,128]{2,1,0:T(8,128)(2,1)S(1)}, u32[]{:S(2)}, u32[]{:S(2)}) collective-permute-start(bf16[32,128,128]{2,1,0:T(8,128)(2,1)S(1)} %add_convert_fusion.2), channel_id=1, source_target_pairs={{0,0},{2,4},{4,2},{6,6},{1,1},{3,5},{5,3},{7,7},{8,8},{10,12},{12,... | collective-permute-start | bytes 3145736 | tf_op jit(solution)/shard_map/ppermute | solution.py:393
  165.1 5.5 %collective-permute-start.18 = (bf16[32,128,128]{2,1,0:T(8,128)(2,1)S(1)}, bf16[32,128,128]{2,1,0:T(8,128)(2,1)S(1)}, u32[]{:S(2)}, u32[]{:S(2)}) collective-permute-start(bf16[32,128,128]{2,1,0:T(8,128)(2,1)S(1)} %add_convert_fusion), channel_id=1, source_target_pairs={{0,0},{2,4},{4,2},{6,6},{1,1},{3,5},{5,3},{7,7},{8,8},{10,12},{12,... | collective-permute-start | bytes 3145736 | tf_op jit(solution)/shard_map/ppermute | solution.py:395
  166.3 26.6 %collective-permute-start.16 = (bf16[32,128,128]{2,1,0:T(8,128)(2,1)S(1)}, bf16[32,128,128]{2,1,0:T(8,128)(2,1)S(1)}, u32[]{:S(2)}, u32[]{:S(2)}) collective-permute-start(bf16[32,128,128]{2,1,0:T(8,128)(2,1)S(1)} %add_convert_fusion.1), channel_id=1, source_target_pairs={{0,2},{2,0},{4,6},{6,4},{1,3},{3,1},{5,7},{7,5},{8,10},{10,8},{12,... | collective-permute-start | bytes 3145736 | tf_op jit(solution)/shard_map/ppermute | solution.py:398

commit v3 on v1

v3 whole, which is shorter than its diff:
```python
import functools
import math

import jax
import jax.numpy as jnp
import ml_dtypes
import numpy as np
from jax import lax
from jax.experimental import pallas as pl
from jax.experimental.pallas import tpu as pltpu
from jax.sharding import Mesh, PartitionSpec as P

SWAP = [(0, 1), (1, 0)]
ENDS = [(0, 1), (1, 0), (2, 3), (3, 2)]
MIDS = [(1, 2), (2, 1), (5, 6), (6, 5), (0, 4), (4, 0), (3, 7), (7, 3)]
DIAG = [(0, 3), (1, 2), (2, 1), (3, 0)]
LANES = 128
PARTS = ((0, 1), (1, 2))
VMEM_LIMIT = 24 * 2**20
NT = (((1,), (1,)), ((), ()))


def cost(flops, bytes_accessed, transcendentals, times=1):
    return pl.CostEstimate(
        flops=times * flops, bytes_accessed=times * bytes_accessed, transcendentals=transcendentals
    )


def xor_chunks(rows, hi, lo):
    planes, count, cells = rows.shape
    rows = rows.reshape(planes, 2, 2, count // 4, cells)
    rows = jnp.where(hi == 1, rows[:, ::-1], rows)
    rows = jnp.where(lo == 1, rows[:, :, ::-1], rows)
    return rows.reshape(planes * count, cells)


def project(kernel_rows, sky_rows):
    out = lax.dot_general(
        kernel_rows, sky_rows, (((1,), (1,)), ((), ())), preferred_element_type=jnp.float32
    )
    base, chans = out.shape[0] // 2, out.shape[1] // 2
    real = out[:base, :chans] - out[base:, chans:]
    imag = out[:base, chans:] + out[base:, :chans]
    return jnp.stack([real, imag])


def adjoint_any(field, kernel_rows):
    total = 0.0
    for blk in range(2):
        real, imag = field[blk][0], field[blk][1]
        lhs = jnp.concatenate(
            [jnp.concatenate([real, imag], 1), jnp.concatenate([imag, -real], 1)], 0
        )
        total = total + lax.dot_general(
            lhs, kernel_rows[blk], (((0,), (0,)), ((), ())), preferred_element_type=jnp.float32
        )
    return total


def tables(channels, length):
    product = channels[:, None] * jnp.arange(length, dtype=jnp.int32)[None, :] % length
    angle = product.astype(jnp.float32) * (2.0 * math.pi / length)
    return jnp.cos(angle), jnp.sin(angle)


def mm(a, b):
    return jnp.einsum("bc,ck->bk", a, b, precision=lax.Precision.HIGHEST)


def mmt(a, b):
    return jnp.einsum("bk,ck->bc", a, b, precision=lax.Precision.HIGHEST)


def any_body(sky, kernel, data, block_tiles, length_bin, wedge_keep):
    length = data.shape[3]
    local, cells = sky.shape[1], sky.shape[3]
    base = kernel.shape[4]
    hi, lo = lax.axis_index("th"), lax.axis_index("tl")
    zpos, ypos = lax.axis_index("outer"), lax.axis_index("inner")
    depth = lax.axis_size("outer")
    tile_pos = hi * 2 + lo
    chunk = base // 4

    column = jnp.arange(block_tiles.shape[1], dtype=jnp.int32) == tile_pos
    weight = jnp.sum(jnp.where(column, block_tiles[0], 0)).astype(jnp.bfloat16)

    own_sky = sky[0].transpose(1, 0, 2).reshape(2 * local, cells)
    own_rows = xor_chunks((kernel[0, 0] * weight).transpose(0, 2, 1), hi, lo)
    kernels = [own_rows, lax.ppermute(own_rows, "inner", SWAP)]

    every = lax.all_gather(own_sky, "outer")
    order = jnp.arange(depth, dtype=jnp.int32)
    vis = [
        jnp.concatenate([project(rows, every[s]) for s in range(depth)], axis=2)
        for rows in kernels
    ]

    def channels(half):
        place = (order[:, None] * 2 + half) * local + jnp.arange(local, dtype=jnp.int32)[None, :]
        return place.reshape(-1)

    own_cos, own_sin = tables(channels(ypos), length)
    far_cos, far_sin = tables(channels(1 - ypos), length)

    count = vis[0].shape[2]
    vis = jnp.stack(vis).reshape(2, 2, 2, 2, chunk, count)
    vis = vis[:, :, :, 0] + lax.ppermute(vis[:, :, :, 1], "tl", SWAP)
    from_x = lax.ppermute(vis[0, :, 1], "th", SWAP)
    from_y = lax.ppermute(vis[1, :, 0], "inner", SWAP)
    from_d = lax.ppermute(vis[1, :, 1], ("th", "inner"), DIAG)
    own_vis = vis[0, :, 0] + from_x
    far_vis = from_y + from_d

    norm = 1.0 / math.sqrt(length)
    own_data = lax.dynamic_slice_in_dim(data[0], tile_pos * chunk, chunk, 1).astype(jnp.float32)
    own_bins = lax.dynamic_slice_in_dim(length_bin[0], tile_pos * chunk, chunk, 0)
    keep = wedge_keep[own_bins].astype(jnp.float32)
    cos_sum = [mm(own_vis[p], own_cos) + mm(far_vis[p], far_cos) for p in range(2)]
    sin_sum = [mm(own_vis[p], own_sin) + mm(far_vis[p], far_sin) for p in range(2)]
    miss_real = keep * ((cos_sum[0] + sin_sum[1]) * norm - own_data[0])
    miss_imag = keep * ((cos_sum[1] - sin_sum[0]) * norm - own_data[1])

    def back(cosine, sine):
        real = (mmt(miss_real, cosine) - mmt(miss_imag, sine)) * norm
        imag = (mmt(miss_imag, cosine) + mmt(miss_real, sine)) * norm
        return jnp.stack([real, imag]).astype(jnp.bfloat16)

    own_back, far_back = back(own_cos, own_sin), back(far_cos, far_sin)
    back_x = lax.ppermute(own_back, "th", SWAP)
    back_y = lax.ppermute(far_back, "inner", SWAP)
    back_d = lax.ppermute(far_back, ("th", "inner"), DIAG)
    half = jnp.stack([jnp.stack([own_back, back_x], 1), jnp.stack([back_y, back_d], 1)])
    other = lax.ppermute(half, "tl", SWAP)
    field = jnp.stack([half, other], 3).reshape(2, 2, base, count)

    def update(slot):
        return adjoint_any(field[..., slot * local : (slot + 1) * local], kernels)

    every = jnp.concatenate([update(s) for s in range(depth)], 0)
    gradient = lax.psum_scatter(every, "outer", scatter_dimension=0, tiled=True)
    return gradient.reshape(2, local, cells).transpose(1, 0, 2)[None]


def wide(tiles):
    return jnp.concatenate([tiles[t] for t in range(tiles.shape[0])], axis=1)


def paired(part):
    return jnp.concatenate([part[0], part[1]], axis=1)


def tall(tiles):
    return tiles.reshape(tiles.shape[0] * tiles.shape[1], tiles.shape[2])


def dot(a, b):
    return jnp.dot(a, b, preferred_element_type=jnp.float32)


def near_sum_kernel(keep, got, out):
    out[...] = (keep[...] + got[...]).astype(out.dtype)


def near_sum(keep, got):
    vmem = pl.BlockSpec(memory_space=pltpu.VMEM)
    return pl.pallas_call(
        near_sum_kernel,
        in_specs=[vmem, vmem],
        out_specs=vmem,
        out_shape=jax.ShapeDtypeStruct(keep.shape, jnp.bfloat16),
        compiler_params=pltpu.CompilerParams(vmem_limit_bytes=VMEM_LIMIT),
        cost_estimate=cost(flops=keep.size, bytes_accessed=10 * keep.size, transcendentals=0),
        name="near_sum",
    )(keep, got)


def own_sum_kernel(place, keep, got, near, mine, to_x, to_y, to_d):
    for hi, blk, out in ((0, 0, mine), (1, 0, to_x), (0, 1, to_y), (1, 1, to_d)):
        added = jnp.where(place[0] == 1, 0.0, near[hi, blk].astype(jnp.float32))
        out[...] = keep[hi, blk] + got[hi, blk] + added


def own_sum(place, keep, got, near):
    vmem = pl.BlockSpec(memory_space=pltpu.VMEM)
    shape = keep.shape[2:]
    return pl.pallas_call(
        own_sum_kernel,
        in_specs=[pl.BlockSpec(memory_space=pltpu.SMEM)] + [vmem] * 3,
        out_specs=[vmem] * 4,
        out_shape=[jax.ShapeDtypeStruct(shape, jnp.float32)] * 4,
        compiler_params=pltpu.CompilerParams(vmem_limit_bytes=VMEM_LIMIT),
        cost_estimate=cost(flops=2 * keep.size, bytes_accessed=14 * keep.size, transcendentals=0),
        name="own_sum",
    )(place, keep, got, near)


def early_kernel(place, own_k, far_k, slot0, slot1, mid2, end2, *rest):
    total = rest[-1]

    @pl.when(pl.program_id(0) == 0)
    def _():
        total[...] = jnp.zeros_like(total)

    third = jnp.where(place[0] == 1, mid2[...], end2[...])
    rows = jnp.concatenate([wide(slot0[...]), wide(slot1[...]), wide(third)], axis=0)
    for blk, part in enumerate((own_k, far_k)):
        total[blk] += dot(rows, paired(part))


def early(place, own_k, far_k, sky, r1, m1, r2, ready):
    count, rows, _ = r1.shape
    base = own_k.shape[2]
    tiles = count // 3
    k_spec = pl.BlockSpec((2, tiles * LANES, base), lambda i: (0, i, 0))
    own_spec = pl.BlockSpec((tiles, rows, LANES), lambda i: (i + 1, 0, 0))
    s_spec = pl.BlockSpec((tiles, rows, LANES), lambda i: (i, 0, 0))
    shape = (2, 3 * rows, 2 * base)
    return pl.pallas_call(
        early_kernel,
        grid=(3,),
        in_specs=[pl.BlockSpec(memory_space=pltpu.SMEM), k_spec, k_spec, own_spec]
        + [s_spec] * 3
        + [pl.BlockSpec(memory_space=pl.ANY)] * len(ready),
        out_specs=pl.BlockSpec(shape, lambda i: (0, 0, 0)),
        out_shape=jax.ShapeDtypeStruct(shape, jnp.float32),
        compiler_params=pltpu.CompilerParams(vmem_limit_bytes=VMEM_LIMIT),
        cost_estimate=cost(
            flops=12 * rows * count * LANES * 2 * base, bytes_accessed=8 * 2**20, transcendentals=0
        ),
        name="early",
    )(place, own_k, far_k, sky, r1, m1, r2, *ready)


def late_kernel(
    place, done, own_k, far_k, mid3, end3, own_a, far_a, sky_a, near_sky, peer_sky, peer_near_sky,
    near_k, near_far_k, keep, send, near_keep, near_send, total, near_total
):
    step = pl.program_id(0)
    is_mid = place[0] == 1
    done_rows = done.shape[1]
    rows = done_rows // 3

    @pl.when(step == 0)
    def _():
        total[:, :done_rows] = done[...]
        total[:, done_rows:] = jnp.zeros_like(total[:, done_rows:])

    @pl.when(step < 3)
    def _():
        last = wide(jnp.where(is_mid, mid3[...], end3[...]))
        for blk, part in enumerate((own_k, far_k)):
            total[blk, done_rows:] += dot(last, paired(part))

    @pl.when((step == 3) & is_mid)
    def _():
        tiles = sky_a.shape[0]
        sky = jnp.concatenate(
            [wide(part[...]) for part in (sky_a, near_sky, peer_sky, peer_near_sky)], axis=0
        )
        for blk, part in enumerate((own_a, far_a)):
            total[blk] += dot(sky, paired(part))
        for blk, part in enumerate((near_k, near_far_k)):
            pair = jnp.concatenate([tall(part[:tiles]), tall(part[tiles:])], axis=1)
            near_total[blk] = dot(sky, pair)

        store_visibility(place, near_total, near_keep, near_send, (1, 0, 2, 3))

    @pl.when(step == 3)
    def _():
        store_visibility(place, total, keep, send, (0, 1, 2, 3))


def store_visibility(place, total, keep, send, slots):
    base = total.shape[2] // 2
    local = total.shape[1] // 8
    chunk = base // 4
    for blk in range(2):
        for two in range(2):
            planes = [[], []]
            for slot in (slots[2 * two], slots[2 * two + 1]):
                own = total[blk, slot * 2 * local : (slot + 1) * 2 * local, :]
                planes[0].append(own[:local, :base] - own[local:, base:])
                planes[1].append(own[local:, :base] + own[:local, base:])
            turned = [jnp.concatenate(planes[p], axis=0).T for p in range(2)]
            lanes = slice(two * 2 * local, (two + 1) * 2 * local)
            for near, even, odd in ((0, keep, send), (1, send, keep)):

                @pl.when(place[2] == near)
                def _():
                    for p in range(2):
                        for n in range(4):
                            out = even if n & 1 == 0 else odd
                            out[(n >> 1) ^ place[1], blk, p, :, lanes] = turned[p][
                                n * chunk : (n + 1) * chunk
                            ]


def late(place, done, own_k, far_k, mid3, own_a, far_a, sky, r2, r3, m3, chunk):
    count, rows, _ = mid3.shape
    base = own_k.shape[2]
    tiles = count // 3
    k_spec = pl.BlockSpec((2, tiles * LANES, base), lambda i: (0, jnp.minimum(i, 2), 0))
    s_spec = pl.BlockSpec((tiles, rows, LANES), lambda i: (jnp.minimum(i, 2), 0, 0))
    a_spec = pl.BlockSpec((2, tiles * LANES, base), lambda i: (0, 0, 0))
    one = pl.BlockSpec((tiles, rows, LANES), lambda i: (0, 0, 0))
    second = pl.BlockSpec((tiles, rows, LANES), lambda i: (1, 0, 0))
    third = pl.BlockSpec((tiles, rows, LANES), lambda i: (2, 0, 0))
    two = pl.BlockSpec((2 * tiles, rows, LANES), lambda i: (0, 0, 0))
    shape = (2, 2, 2, chunk, 2 * rows)
    return pl.pallas_call(
        late_kernel,
        grid=(4,),
        in_specs=[
            pl.BlockSpec(memory_space=pltpu.SMEM),
            pl.BlockSpec(done.shape, lambda i: (0, 0, 0)),
            k_spec, k_spec, s_spec, s_spec, a_spec, a_spec, one, third, one, second, two, two,
        ],
        out_specs=[pl.BlockSpec(shape, lambda i: (0,) * 5)] * 4,
        out_shape=[jax.ShapeDtypeStruct(shape, jnp.float32)] * 4,
        scratch_shapes=[
            pltpu.VMEM((2, 4 * rows, 2 * base), jnp.float32),
            pltpu.VMEM((2, 4 * rows, 2 * base), jnp.float32),
        ],
        compiler_params=pltpu.CompilerParams(vmem_limit_bytes=VMEM_LIMIT),
        cost_estimate=cost(
            flops=10 * rows * count * LANES * 2 * base, bytes_accessed=9 * 2**20, transcendentals=0
        ),
        name="late",
    )(
        place, done, own_k, far_k, mid3, r3, own_a, far_a, sky, r2, m3, m3, r2, r3
    )


def pack_kernel(place, mid, end0, end1, out):
    is_mid = place[0] == 1
    head = end0.shape[0]

    @pl.when(is_mid)
    def _():
        out[...] = mid[...]

    @pl.when(jnp.logical_not(is_mid))
    def _():
        out[:head] = end0[...]
        out[head:] = end1[...]


def pack(place, mid, end0, end1):
    vmem = pl.BlockSpec(memory_space=pltpu.VMEM)
    return pl.pallas_call(
        pack_kernel,
        in_specs=[pl.BlockSpec(memory_space=pltpu.SMEM)] + [vmem] * 3,
        out_specs=vmem,
        out_shape=jax.ShapeDtypeStruct(mid.shape, mid.dtype),
        compiler_params=pltpu.CompilerParams(vmem_limit_bytes=VMEM_LIMIT),
        cost_estimate=cost(
            flops=0, bytes_accessed=2 * mid.size * mid.dtype.itemsize, transcendentals=0
        ),
        name="pack",
    )(place, mid, end0, end1)


def split(value):
    high = value.astype(jnp.bfloat16)
    return high, (value - high.astype(jnp.float32)).astype(jnp.bfloat16)


def times(value, high, low, dims):
    rows = value.shape[0]
    upper, lower = split(value)
    both = lax.dot_general(
        jnp.concatenate([upper, lower], axis=0), high, dims, preferred_element_type=jnp.float32
    )
    rest = lax.dot_general(upper, low, dims, preferred_element_type=jnp.float32)
    return both[:rows] + both[rows:] + rest


def delay_kernel(
    place, vis0, from_x, from_y, from_d, data, keep, turn, ch, cl, sh, sl, own_out, far_out, rows, back
):
    length = keep.shape[1]
    chunk = keep.shape[0]
    local = length // 8
    norm = 1.0 / math.sqrt(length)
    nn = (((1,), (0,)), ((), ()))
    lower = place[3] == 0
    own = vis0[...] + from_x[...]
    far = from_y[...] + from_d[...]

    def plane_of(slot):
        return pl.ds(pl.multiple_of(place[4 + slot] * 2 * local, 2 * local), 2 * local)

    for slot in range(4):
        lanes = slice(slot * local, (slot + 1) * local)
        for p in range(2):
            mine, other = own[p][:, lanes], far[p][:, lanes]
            both = jnp.where(
                lower,
                jnp.concatenate([mine, other], axis=1),
                jnp.concatenate([other, mine], axis=1),
            )
            rows[p * chunk : (p + 1) * chunk, plane_of(slot)] = both
    half = length // 2
    turn_cos, turn_sin = turn[0:1], turn[1:2]
    low_half, high_half = rows[:, :half], rows[:, half:]
    plus, minus = low_half + high_half, low_half - high_half
    odd_real = minus[:chunk] * turn_cos + minus[chunk:] * turn_sin
    odd_imag = minus[chunk:] * turn_cos - minus[:chunk] * turn_sin
    value = jnp.concatenate([plus, odd_real, odd_imag], axis=0)
    cos_sum = times(value, ch[...], cl[...], nn)
    sin_sum = times(value, sh[...], sl[...], nn)
    miss = []
    for odd in range(2):
        real, imag = (slice((2 * odd + p) * chunk, (2 * odd + p + 1) * chunk) for p in range(2))
        lanes = slice(odd * half, (odd + 1) * half)
        kept = keep[:, lanes]
        spec_real = (cos_sum[real] + sin_sum[imag]) * norm
        spec_imag = (cos_sum[imag] - sin_sum[real]) * norm
        miss.append(kept * (spec_real - data[0, :, lanes].astype(jnp.float32)))
        miss.append(kept * (spec_imag - data[1, :, lanes].astype(jnp.float32)))
    miss = jnp.concatenate(miss, axis=0)
    cos_back = times(miss, ch[...], cl[...], nn)
    sin_back = times(miss, sh[...], sl[...], nn)
    even_real, odd_real = (
        cos_back[at : at + chunk] - sin_back[at + chunk : at + 2 * chunk] for at in (0, 2 * chunk)
    )
    even_imag, odd_imag = (
        cos_back[at + chunk : at + 2 * chunk] + sin_back[at : at + chunk] for at in (0, 2 * chunk)
    )
    turned_real = odd_real * turn_cos - odd_imag * turn_sin
    turned_imag = odd_imag * turn_cos + odd_real * turn_sin
    back[:chunk, :half] = (even_real + turned_real) * norm
    back[:chunk, half:] = (even_real - turned_real) * norm
    back[chunk:, :half] = (even_imag + turned_imag) * norm
    back[chunk:, half:] = (even_imag - turned_imag) * norm
    for p in range(2):
        found = [back[p * chunk : (p + 1) * chunk, plane_of(slot)] for slot in range(4)]
        first = jnp.concatenate([f[:, :local] for f in found], axis=1)
        second = jnp.concatenate([f[:, local:] for f in found], axis=1)
        own_out[p] = jnp.where(lower, first, second).astype(jnp.bfloat16)
        far_out[p] = jnp.where(lower, second, first).astype(jnp.bfloat16)


def delay(place, *parts):
    shape = jax.ShapeDtypeStruct(parts[0].shape, jnp.bfloat16)
    chunk, length = parts[5].shape
    vmem = pl.BlockSpec(memory_space=pltpu.VMEM)
    return pl.pallas_call(
        delay_kernel,
        in_specs=[pl.BlockSpec(memory_space=pltpu.SMEM)] + [vmem] * len(parts),
        out_specs=(vmem, vmem),
        out_shape=(shape, shape),
        scratch_shapes=[pltpu.VMEM((2 * chunk, length), jnp.float32)] * 2,
        compiler_params=pltpu.CompilerParams(vmem_limit_bytes=VMEM_LIMIT),
        cost_estimate=cost(
            flops=24 * chunk * length * length, bytes_accessed=8 * length * length, transcendentals=0
        ),
        name="delay",
    )(place, *parts)


def field_rows(place, half, other, slots, out, at):
    chunk, local = half.shape[3], half.shape[4] // 4
    base = 4 * chunk
    for blk in range(2):
        for n in range(4):
            hi, lo = (n >> 1) ^ place[1], (n & 1) ^ place[2]
            planes = [
                jnp.where(
                    lo == 0,
                    half[hi, blk, p].astype(jnp.float32),
                    other[hi, blk, p].astype(jnp.float32),
                )
                for p in range(2)
            ]
            first = at + blk * 2 * base + n * chunk
            for i, s in enumerate(slots):
                real = planes[0][:, s * local : (s + 1) * local]
                imag = planes[1][:, s * local : (s + 1) * local]
                lanes = slice(i * 2 * local, (i + 1) * 2 * local)
                upper = jnp.concatenate([real, imag], axis=1)
                lower = jnp.concatenate([imag, -real], axis=1)
                out[first : first + chunk, lanes] = upper.astype(jnp.bfloat16)
                out[first + base : first + base + chunk, lanes] = lower.astype(jnp.bfloat16)


def store_tiles(sums, slot, out):
    lanes = slice(slot * LANES, (slot + 1) * LANES)
    for t in range(out.shape[0]):
        out[t] = sums[t * LANES : (t + 1) * LANES, lanes].T.astype(out.dtype)


def adjoint_kernel(slots, ends_only, place, half, other, own_k, far_k, *rest):
    outs, field = rest[:-1], rest[-1]
    step = pl.program_id(0)

    @pl.when((place[0] == 0) | (not ends_only))
    def _():
        @pl.when(step == 0)
        def _():
            field_rows(place, half, other, slots, field, 0)

        cells = jnp.concatenate([own_k[0], own_k[1], far_k[0], far_k[1]], axis=1)
        sums = dot(cells, field[...])
        for i in range(len(slots)):

            @pl.when(step == 0)
            def _():
                store_tiles(sums, i, outs[2 * i])

            @pl.when(step > 0)
            def _():
                store_tiles(sums, i, outs[2 * i + 1])


def adjoint(place, half, other, own_k, far_k, slots, dtype, ends_only=False):
    base = own_k.shape[2]
    count = own_k.shape[1] // LANES
    tiles = count // 3
    rows = half.shape[4] // 2
    k_spec = pl.BlockSpec((2, tiles * LANES, base), lambda i: (0, i, 0))
    f_spec = pl.BlockSpec(half.shape, lambda i: (0,) * 5)
    block = (tiles, rows, LANES)
    outs = pl.pallas_call(
        functools.partial(adjoint_kernel, slots, ends_only),
        grid=(3,),
        in_specs=[pl.BlockSpec(memory_space=pltpu.SMEM), f_spec, f_spec, k_spec, k_spec],
        out_specs=[
            pl.BlockSpec(block, lambda i: (0, 0, 0)),
            pl.BlockSpec(block, lambda i: (jnp.maximum(i - 1, 0), 0, 0)),
        ]
        * len(slots),
        out_shape=[
            jax.ShapeDtypeStruct((n * tiles, rows, LANES), dtype) for _ in slots for n in (1, 2)
        ],
        scratch_shapes=[pltpu.VMEM((4 * base, rows * len(slots)), jnp.bfloat16)],
        compiler_params=pltpu.CompilerParams(vmem_limit_bytes=VMEM_LIMIT),
        cost_estimate=cost(
            flops=8 * rows * len(slots) * count * LANES * base,
            bytes_accessed=(4 + 2 * len(slots)) * 2**20,
            transcendentals=0,
            times=20,
        ),
        name="adjoint",
    )(place, half, other, own_k, far_k)
    return [outs[2 * i : 2 * i + 2] for i in range(len(slots))]


def first_kernel(slot, place, half, other, own_k, far_k, out, field):
    @pl.when(place[0] == 0)
    def _():
        @pl.when(pl.program_id(0) == 0)
        def _():
            field_rows(place, half, other, (slot,), field, 0)

        cells = jnp.concatenate([own_k[0], own_k[1], far_k[0], far_k[1]], axis=1)
        store_tiles(dot(cells, field[...]), 0, out)


def first_adjoint(place, half, other, own_k, far_k, slot, begin, steps):
    base = own_k.shape[2]
    tiles = own_k.shape[1] // LANES // 3
    rows = half.shape[4] // 2
    k_spec = pl.BlockSpec((2, tiles * LANES, base), lambda i: (0, i + begin, 0))
    f_spec = pl.BlockSpec(half.shape, lambda i: (0,) * 5)
    return pl.pallas_call(
        functools.partial(first_kernel, slot),
        grid=(steps,),
        in_specs=[pl.BlockSpec(memory_space=pltpu.SMEM), f_spec, f_spec, k_spec, k_spec],
        out_specs=pl.BlockSpec((tiles, rows, LANES), lambda i: (i, 0, 0)),
        out_shape=jax.ShapeDtypeStruct((steps * tiles, rows, LANES), jnp.bfloat16),
        scratch_shapes=[pltpu.VMEM((4 * base, rows), jnp.bfloat16)],
        compiler_params=pltpu.CompilerParams(vmem_limit_bytes=VMEM_LIMIT),
        cost_estimate=cost(
            flops=8 * rows * steps * tiles * LANES * base,
            bytes_accessed=steps * 2**21,
            transcendentals=0,
            times=20,
        ),
        name="first_adjoint",
    )(place, half, other, own_k, far_k)


def near_kernel(
    place, half, other, near_half, near_other, own_a, far_a, near_k, near_far_k, send, part1, part0,
    field
):
    @pl.when(place[0] == 1)
    def _():
        field_rows(place, half, other, (3, 2, 1, 0), field, 0)
        rows = field.shape[0] // 2
        field_rows(place, near_half, near_other, (3, 2, 0, 1), field, rows)
        tiles = near_k.shape[0] // 2
        cells = jnp.concatenate(
            [own_a[0], own_a[1], far_a[0], far_a[1]]
            + [tall(part[i * tiles : (i + 1) * tiles]) for part in (near_k, near_far_k) for i in (0, 1)],
            axis=1,
        )
        sums = dot(cells, field[...])
        outs = (send.at[pl.ds(0, tiles)], send.at[pl.ds(tiles, tiles)], part1, part0)
        for i, out in enumerate(outs):
            store_tiles(sums, i, out)


def near_adjoint(place, half, other, near_half, near_other, own_a, far_a, r2, r3):
    base = own_a.shape[2]
    tiles = own_a.shape[1] // LANES
    rows = half.shape[4] // 2
    whole = lambda a: pl.BlockSpec(a.shape, lambda i: (0,) * a.ndim)
    two = pl.BlockSpec((2 * tiles, LANES, rows), lambda i: (0, 0, 0))
    one = pl.BlockSpec((tiles, LANES, rows), lambda i: (0, 0, 0))
    types = ((2, jnp.bfloat16), (1, jnp.float32), (1, jnp.float32))
    return pl.pallas_call(
        near_kernel,
        grid=(1,),
        in_specs=[pl.BlockSpec(memory_space=pltpu.SMEM)]
        + [whole(a) for a in (half, other, near_half, near_other, own_a, far_a)]
        + [two, two],
        out_specs=[two, one, one],
        out_shape=[jax.ShapeDtypeStruct((n * tiles, LANES, rows), t) for n, t in types],
        scratch_shapes=[pltpu.VMEM((8 * base, rows * 4), jnp.bfloat16)],
        compiler_params=pltpu.CompilerParams(vmem_limit_bytes=VMEM_LIMIT),
        cost_estimate=cost(
            flops=64 * rows * tiles * LANES * base,
            bytes_accessed=6 * 2**20,
            transcendentals=0,
            times=20,
        ),
        name="near_adjoint",
    )(place, half, other, near_half, near_other, own_a, far_a, r2, r3)


def final_kernel(place, part_a, peer_a, end_a, *rest):
    part_b, near_b, far_b = (rest[2 * i : 2 * i + 2] for i in range(3))
    out = rest[-1]
    step = pl.program_id(0)
    is_mid = place[0] == 1
    local = out.shape[0]

    def store(value):
        for t in range(value.shape[0]):
            lanes = slice(t * LANES, (t + 1) * LANES)
            out[:, 0, lanes] = value[t][:local]
            out[:, 1, lanes] = value[t][local:]

    @pl.when(step == 0)
    def _():
        mid = part_a[...] + peer_a[...].astype(jnp.float32)
        store(jnp.where(is_mid, mid, end_a[...].astype(jnp.float32)))

    @pl.when(step > 0)
    def _():
        def piece(parts):
            return jnp.where(step == 1, parts[0][...], parts[1][...]).astype(jnp.float32)

        store(piece(part_b) + piece(near_b) + jnp.where(is_mid, piece(far_b), 0.0))


def final(place, part_a, peer_a, end_a, part_b, near_b, far_b):
    tiles, _, rows = part_a.shape
    count = 4 * tiles
    shape = (tiles, LANES, rows)
    one = pl.BlockSpec(shape, lambda i: (0, 0, 0))
    second = pl.BlockSpec(shape, lambda i: (1, 0, 0))
    rest = pl.BlockSpec(shape, lambda i: (jnp.maximum(i - 2, 0), 0, 0))
    return pl.pallas_call(
        final_kernel,
        grid=(4,),
        in_specs=[pl.BlockSpec(memory_space=pltpu.SMEM), one, second, one] + [one, rest] * 3,
        out_specs=pl.BlockSpec((rows // 2, 2, tiles * LANES), lambda i: (0, 0, i)),
        out_shape=jax.ShapeDtypeStruct((rows // 2, 2, count * LANES), jnp.float32),
        compiler_params=pltpu.CompilerParams(vmem_limit_bytes=VMEM_LIMIT),
        cost_estimate=cost(
            flops=4 * rows * count * LANES, bytes_accessed=6 * 2**20, transcendentals=0
        ),
        name="final",
    )(place, part_a, peer_a, end_a, *part_b, *near_b, *far_b)


def table_parts(length):
    half = length // 2
    steps = np.arange(half)
    turn = steps * (2.0 * math.pi / length)
    parts = [np.stack([np.cos(turn), np.sin(turn)]).astype(np.float32)]
    angle = (steps[:, None] * steps[None, :] % half) * (2.0 * math.pi / half)
    for table in (np.cos(angle), np.sin(angle)):
        high = table.astype(ml_dtypes.bfloat16)
        parts += [high, (table - high.astype(np.float64)).astype(ml_dtypes.bfloat16)]
    return [jnp.asarray(part) for part in parts]


def line_body(sky, kernel, data, block_tiles, length_bin, wedge_keep):
    length = data.shape[3]
    local, cells = sky.shape[1], sky.shape[3]
    base = kernel.shape[4]
    hi, lo = lax.axis_index("th"), lax.axis_index("tl")
    zpos, ypos = lax.axis_index("outer"), lax.axis_index("inner")
    tile_pos = hi * 2 + lo
    chunk = base // 4
    is_mid = (zpos == 1) | (zpos == 2)
    order = jnp.array([[0, 1, 2, 3], [1, 0, 2, 3], [2, 3, 1, 0], [3, 2, 1, 0]], jnp.int32)[zpos]
    place = jnp.concatenate([jnp.stack([is_mid.astype(jnp.int32), hi, lo, ypos]), order])

    tiles = cells // LANES // 4
    cut = tiles * LANES
    own_sky = sky[0].reshape(local, 2, cells // LANES, LANES).transpose(2, 1, 0, 3)
    own_sky = own_sky.reshape(cells // LANES, 2 * local, LANES)
    sky_a, sky_b = own_sky[:tiles], own_sky[tiles:]
    def ends(*values):
        return [lax.ppermute(value, "outer", ENDS) for value in values]

    def mids(*values):
        return [lax.ppermute(value, ("tl", "outer"), MIDS) for value in values]

    def as_tiles(part):
        return part.reshape(2 * tiles, LANES, base)

    (r1,) = ends(sky_b)
    (m1,) = mids(sky_b)
    column = jnp.arange(block_tiles.shape[1], dtype=jnp.int32) == tile_pos
    weight = jnp.sum(jnp.where(column, block_tiles[0], 0)).astype(jnp.bfloat16)
    own_a = lax.optimization_barrier(kernel[0, 0, :, :cut] * weight)
    own_b = kernel[0, 0, :, cut:] * weight
    far_a = lax.ppermute(own_a, "inner", SWAP)
    (m2,) = mids(r1)
    own_b, far_a, m1 = lax.optimization_barrier((own_b, far_a, m1))
    far_b = lax.ppermute(own_b, "inner", SWAP)
    (r2,) = ends(pack(place, m1, as_tiles(own_a), sky_a))
    (r3,) = ends(pack(place, m2, as_tiles(far_a), sky_a))
    (m3,) = mids(jnp.concatenate([sky_a, r2[2 * tiles :]]))

    parts = table_parts(length)
    def by_parity(value):
        pairs = value.reshape(value.shape[:-1] + (length // 2, 2))
        return jnp.swapaxes(pairs, -1, -2).reshape(value.shape)

    own_data = by_parity(lax.dynamic_slice_in_dim(data[0], tile_pos * chunk, chunk, 1))
    own_bins = lax.dynamic_slice_in_dim(length_bin[0], tile_pos * chunk, chunk, 0)
    keep = by_parity(wedge_keep.astype(jnp.float32))[own_bins]

    done = early(place, own_b, far_b, own_sky, r1, m1, r2, (own_data, keep))
    keep_vis, send_vis, near_keep, near_send = late(
        place, done, own_b, far_b, m2, own_a, far_a, own_sky, r2, r3, m3, chunk
    )
    (near,) = ends(near_sum(near_keep, lax.ppermute(near_send, "tl", SWAP)))
    got = lax.ppermute(send_vis, "tl", SWAP)
    mine, to_x, to_y, to_d = own_sum(place, keep_vis, got, near)
    from_x = lax.ppermute(to_x, "th", SWAP)
    from_y = lax.ppermute(to_y, "inner", SWAP)
    from_d = lax.ppermute(to_d, ("th", "inner"), DIAG)
    own_back, far_back = delay(place, mine, from_x, from_y, from_d, own_data, keep, *parts)
    back_x = lax.ppermute(own_back, "th", SWAP)
    back_y = lax.ppermute(far_back, "inner", SWAP)
    back_d = lax.ppermute(far_back, ("th", "inner"), DIAG)
    half = jnp.stack([jnp.stack([own_back, back_y]), jnp.stack([back_x, back_d])])
    other = lax.ppermute(half, "tl", SWAP)
    (near_half,) = ends(half)

    low = jnp.bfloat16

    def plus(part, got):
        return (part + got.astype(jnp.float32)).astype(low)

    send3 = [first_adjoint(place, half, other, own_b, far_b, 3, *part) for part in PARTS]
    g1 = ends(*send3)
    near_half, _ = lax.optimization_barrier((near_half, send3[1]))
    near_other = lax.ppermute(near_half, "tl", SWAP)
    send_a, part1_a, part0_a = near_adjoint(
        place, half, other, near_half, near_other, own_a, far_a, r2, r3
    )
    (peer_a,) = mids(send_a)
    half, send_a = lax.optimization_barrier((half, send_a))
    part3, part2, part1, part0 = adjoint(
        place, half, other, own_b, far_b, (3, 2, 1, 0), jnp.float32
    )
    far3 = mids(*(plus(part, got) for part, got in zip(part3, g1)))
    first = jnp.where(is_mid, plus(part1_a, peer_a[:tiles]), part2[0].astype(low))
    (g2,) = ends(jnp.concatenate([first, part2[1].astype(low)]))
    far2 = mids(plus(part2[0], g2[:tiles]), plus(part2[1], g2[tiles:]))
    g3 = ends(
        *(plus(part, jnp.where(is_mid, got, jnp.zeros_like(got))) for part, got in zip(part1, far3))
    )
    return final(place, part0_a, peer_a, g2, part0, g3, far2)[None]


def body(sky, kernel, *rest):
    local, cells = sky.shape[1], sky.shape[3]
    line = lax.axis_size("outer") == 4 and 2 * local == LANES and kernel.shape[4] == LANES
    chosen = line_body if line and cells % (4 * LANES) == 0 else any_body
    return chosen(sky, kernel, *rest)


def solution(mesh):
    tiles, freqs = mesh.shape["tile"], mesh.shape["freq"]
    fine = Mesh(mesh.devices.reshape(tiles // 2, 2, freqs // 2, 2), ("th", "tl", "outer", "inner"))
    tile, freq = ("th", "tl"), ("outer", "inner")
    return jax.shard_map(
        body,
        mesh=fine,
        in_specs=(
            P(tile, freq, None, None),
            P(tile, freq, None, None, None),
            P(freq, None, None, None),
            P(freq, None),
            P(freq, None),
            P(),
        ),
        out_specs=P(tile, freq, None, None),
        check_vma=False,
    )
```

time: 266 us -> 162 us (0.61); the launches traced: 262 us -> 161 us
  matrix products: 78.4 us -> 0 us
  waiting for transfers between devices: 117 us -> 50.4 us
  starting transfers between devices: 32.8 us -> 61.5 us
  Pallas kernels: 0 us -> 27.9 us
  local copies, waits for them, and re-layouts: 24.1 us -> 14.9 us
    dot_general x36 -> x0, matrix products: 78.4 us -> none  [the longest x12 27 us: project(): lax.dot_general(kernel_rows, sky_rows, (((1,), (1,)), ((), ())), preferre...]
    ppermute x19 -> x30, waiting for transfers between devices: 117 us -> 50.4 us  [the longest x10 30.4 us: ends(): return [lax.ppermute(value, 'outer', ENDS) for value in values]]
    ppermute x19 -> x30, starting transfers between devices: 32.8 us -> 61.5 us  [the longest x10 50.1 us: ends(): return [lax.ppermute(value, 'outer', ENDS) for value in values]]
    pallas_call x0 -> x12, Pallas kernels: none -> 27.9 us  [the longest x1 5.88 us: adjoint(): pl.pallas_call(functools.partial(adjoint_kernel, slots, ends_only), grid=...]
    add x14 -> x0, local copies, waits for them, and re-layouts: 8.5 us -> none  [the longest x12 8.34 us: project(): imag = out[:base, chans:] + out[base:, :chans]]
    sub x12 -> x0, local copies, waits for them, and re-layouts: 7.06 us -> none  [project(): real = out[:base, :chans] - out[base:, chans:]]
    reshape x1, local copies, waits for them, and re-layouts: 2.94 us -> 0.05 us  [by_parity(): return jnp.swapaxes(pairs, -1, -2).reshape(value.shape)]
  transfers between devices with their start and end apart: 19 -> 30, of which waited for: 10 -> 16; matrix products, arithmetic and copies ran while one was open for 19% -> 8% of each run, Pallas kernels for 0% -> 11%
where the time goes in v3:
time: 162 us; the launch traced here: 161 us
  starting transfers between devices  61.5 us (38%)
  waiting for transfers between devices  50.4 us (31%)
  Pallas kernels  27.9 us (17%)
  local copies, waits for them, and re-layouts  14.9 us (9%)
  other arithmetic  5.03 us (3%)
    ppermute x10, starting transfers between devices, ends(): return [lax.ppermute(value, 'outer', ENDS) for value in values]  50.1 us
    ppermute x10, waiting for transfers between devices, ends(): return [lax.ppermute(value, 'outer', ENDS) for value in values]  30.4 us
    ppermute x1, waiting for transfers between devices, line_body(): far_a = lax.ppermute(own_a, 'inner', SWAP)  11.3 us
    pallas_call x1, Pallas kernels, adjoint(): pl.pallas_call(functools.partial(adjoint_kernel, slots, ends_only), grid=...  5.88 us
    unnamed x35, local copies, waits for them, and re-layouts  4.45 us
    pallas_call x1, Pallas kernels, late(): pl.pallas_call(late_kernel, grid=(4,), in_specs=[pl.BlockSpec(memory_spac...  4.28 us
    pallas_call x2, Pallas kernels, first_adjoint(): pl.pallas_call(functools.partial(first_kernel, slot), grid=(steps,), in_s...  3.95 us
    pallas_call x1, Pallas kernels, early(): pl.pallas_call(early_kernel, grid=(3,), in_specs=[pl.BlockSpec(memory_spa...  3.8 us
  transfers between devices with their start and end apart: 30, of which 16 were waited for; matrix products, arithmetic and copies ran while one was open for 8% of the time, Pallas kernels for 11%

profile of v3, /device:TPU:0, one launch (start us, length us, event | category | flops | bytes accessed | tf_op | source)
XLA Modules:
  0.0 160.8 jit_solution(985268228358031749)
XLA Ops:
  0.0 1.9 %reshape_squeeze.3 = bf16[64,2,32,128]{3,2,1,0:T(8,128)(2,1)S(1)} reshape(bf16[1,64,2,4096]{3,2,1,0:T(2,128)(2,1)} %param.12) | data formatting | bytes 2097152 | tf_op jit(solution)/shard_map/reshape;squeeze | solution.py:706
  3.5 3.0 %collective-permute-start.3 = (bf16[24,128,128]{2,1,0:T(8,128)(2,1)}, bf16[24,128,128]{2,1,0:T(8,128)(2,1)}, u32[]{:S(2)}, u32[]{:S(2)}) collective-permute-start(bf16[24,128,128]{2,1,0:T(8,128)(2,1)} %bitcast.9), channel_id=1, source_target_pairs={{0,2},{2,0},{4,6},{6,4},{1,3},{3,1},{5,7},{7,5},{8,10},{10,8},{12,... | collective-permute-start | bytes 2359304 | tf_op jit(solution)/shard_map/ppermute | solution.py:710
  9.0 1.6 collective-permute-start
  10.5 1.5 multiply_bitcast_fusion.own_k
  12.1 11.3 %collective-permute-done.far_a = bf16[2,1024,128]{2,1,0:T(8,128)(2,1)S(1)} collective-permute-done((bf16[2,1024,128]{2,1,0:T(8,128)(2,1)S(1)}, bf16[2,1024,128]{2,1,0:T(8,128)(2,1)S(1)}, u32[]{:S(2)}, u32[]{:S(2)}) %collective-permute-start) | collective-permute-done | bytes 524320 | tf_op jit(solution)/shard_map/ppermute | solution.py:724
  24.2 1.5 collective-permute-start.2
  29.4 4.9 %collective-permute-start.4 = (bf16[24,128,128]{2,1,0:T(8,128)(2,1)S(1)}, bf16[24,128,128]{2,1,0:T(8,128)(2,1)S(1)}, u32[]{:S(2)}, u32[]{:S(2)}) collective-permute-start(bf16[24,128,128]{2,1,0:T(8,128)(2,1)S(1)} %pack.2), channel_id=1, source_target_pairs={{0,2},{2,0},{4,6},{6,4},{1,3},{3,1},{5,7},{7,5},{8,10},{10,8},{12,... | collective-permute-start | bytes 2359304 | tf_op jit(solution)/shard_map/ppermute | solution.py:710
  34.4 2.2 %pack.3 = bf16[24,128,128]{2,1,0:T(8,128)(2,1)} custom-call(s32[8]{0:T(128)S(1)} %concatenate.9.place, bf16[24,128,128]{2,1,0:T(8,128)(2,1)} %collective-permute-done.5.mid.mid3, bf16[16,128,128]{2,1,0:T(8,128)(2,1)S(1)} %bitcast.53, bf16[8,128,128]{2,1,0:T(8,128)(2,1)S(1)} %bitcast.51), custom_call_target="tpu_custom_call" | custom-call | bytes 1572864 | tf_op jit(solution)/shard_map/pack/pallas_call | solution.py:350
  36.6 12.9 %collective-permute-start.6 = (bf16[24,128,128]{2,1,0:T(8,128)(2,1)}, bf16[24,128,128]{2,1,0:T(8,128)(2,1)}, u32[]{:S(2)}, u32[]{:S(2)}) collective-permute-start(bf16[24,128,128]{2,1,0:T(8,128)(2,1)} %pack.3), channel_id=1, source_target_pairs={{0,2},{2,0},{4,6},{6,4},{1,3},{3,1},{5,7},{7,5},{8,10},{10,8},{12,... | collective-permute-start | bytes 2359304 | tf_op jit(solution)/shard_map/ppermute | solution.py:710
  49.5 2.5 %collective-permute-done.4.end2.near_sky.near_k = bf16[24,128,128]{2,1,0:T(8,128)(2,1)S(1)} collective-permute-done((bf16[24,128,128]{2,1,0:T(8,128)(2,1)S(1)}, bf16[24,128,128]{2,1,0:T(8,128)(2,1)S(1)}, u32[]{:S(2)}, u32[]{:S(2)}) %collective-permute-start.4) | collective-permute-done | bytes 786464 | tf_op jit(solution)/shard_map/ppermute | solution.py:710
  61.5 3.8 %early.1.done = f32[2,384,256]{2,1,0:T(8,128)S(1)} custom-call(s32[8]{0:T(128)S(1)} %concatenate.9.place, bf16[2,3072,128]{2,1,0:T(8,128)(2,1)S(1)} %multiply_bitcast_fusion.own_k, bf16[2,3072,128]{2,1,0:T(8,128)(2,1)} %collective-permute-done.2.far_k, bf16[32,128,128]{2,1,0:T(8,128)(2,1)S(1)} %bitcast.47, ...), custom_call_target="tpu_custom_call" | custom-call | flops 1207959552 | bytes 8388608 | tf_op jit(solution)/shard_map/early/pallas_call | solution.py:218
  65.4 1.7 %collective-permute-done.6.end3.near_far_k = bf16[24,128,128]{2,1,0:T(8,128)(2,1)} collective-permute-done((bf16[24,128,128]{2,1,0:T(8,128)(2,1)}, bf16[24,128,128]{2,1,0:T(8,128)(2,1)}, u32[]{:S(2)}, u32[]{:S(2)}) %collective-permute-start.6) | collective-permute-done | bytes 786464 | tf_op jit(solution)/shard_map/ppermute | solution.py:710
  67.1 4.3 %late.1 = (f32[2,2,2,32,256]{4,3,2,1,0:T(8,128)S(1)}, f32[2,2,2,32,256]{4,3,2,1,0:T(8,128)S(1)}, f32[2,2,2,32,256]{4,3,2,1,0:T(8,128)S(1)}, f32[2,2,2,32,256]{4,3,2,1,0:T(8,128)S(1)}) custom-call(s32[8]{0:T(128)S(1)} %concatenate.9.place, f32[2,384,256]{2,1,0:T(8,128)S(1)} %early.1.done, bf16[2,3072,128]{2,1,0:T(8,128)(2,1)S(1)} %multiply_bitcast_fusion.own_k, ...), custom_call_target="tpu_custom_call" | custom-call | flops 1006632960 | bytes 9437184 | tf_op jit(solution)/shard_map/late/pallas_call | solution.py:310
  73.0 3.4 %collective-permute-start.10 = (bf16[2,2,2,32,256]{4,3,2,1,0:T(8,128)(2,1)S(1)}, bf16[2,2,2,32,256]{4,3,2,1,0:T(8,128)(2,1)S(1)}, u32[]{:S(2)}, u32[]{:S(2)}) collective-permute-start(bf16[2,2,2,32,256]{4,3,2,1,0:T(8,128)(2,1)S(1)} %near_sum.1), channel_id=1, source_target_pairs={{0,2},{2,0},{4,6},{6,4},{1,3},{3,1},{5,7},{7,5},{8,10},{10,8},{12,... | collective-permute-start | bytes 393224 | tf_op jit(solution)/shard_map/ppermute | solution.py:710
  76.5 3.8 %collective-permute-done.10.near = bf16[2,2,2,32,256]{4,3,2,1,0:T(8,128)(2,1)S(1)} collective-permute-done((bf16[2,2,2,32,256]{4,3,2,1,0:T(8,128)(2,1)S(1)}, bf16[2,2,2,32,256]{4,3,2,1,0:T(8,128)(2,1)S(1)}, u32[]{:S(2)}, u32[]{:S(2)}) %collective-permute-start.10) | collective-permute-done | bytes 131104 | tf_op jit(solution)/shard_map/ppermute | solution.py:710
  80.8 1.6 collective-permute-start.11
  82.9 1.5 collective-permute-start.13
  85.2 1.7 %collective-permute-done.12.from_y = f32[2,32,256]{2,1,0:T(8,128)S(1)} collective-permute-done((f32[2,32,256]{2,1,0:T(8,128)S(1)}, f32[2,32,256]{2,1,0:T(8,128)S(1)}, u32[]{:S(2)}, u32[]{:S(2)}) %collective-permute-start.12) | collective-permute-done | bytes 65568 | tf_op jit(solution)/shard_map/ppermute | solution.py:749
  90.1 2.4 %collective-permute-start.16 = (bf16[2,32,256]{2,1,0:T(8,128)(2,1)S(1)}, bf16[2,32,256]{2,1,0:T(8,128)(2,1)S(1)}, u32[]{:S(2)}, u32[]{:S(2)}) collective-permute-start(bf16[2,32,256]{2,1,0:T(8,128)(2,1)S(1)} %get-tuple-element.43), channel_id=1, source_target_pairs={{0,17},{1,16},{16,1},{17,0},{2,19},{3,18},{18,3},{19,2},{4,21},{5,... | collective-permute-start | bytes 98312 | tf_op jit(solution)/shard_map/ppermute | solution.py:754
  94.9 1.5 collective-permute-done.14
  96.6 1.8 %collective-permute-start.18 = (bf16[2,2,2,32,256]{4,3,2,1,0:T(8,128)(2,1)S(1)}, bf16[2,2,2,32,256]{4,3,2,1,0:T(8,128)(2,1)S(1)}, u32[]{:S(2)}, u32[]{:S(2)}) collective-permute-start(bf16[2,2,2,32,256]{4,3,2,1,0:T(8,128)(2,1)S(1)} %pad_maximum_fusion.2.half), channel_id=1, source_target_pairs={{0,2},{2,0},{4,6},{6,4},{1,3},{3,1},{5,7},{7,5},{8,10},{10,8},{12,... | collective-permute-start | bytes 393224 | tf_op jit(solution)/shard_map/ppermute | solution.py:710
  98.4 2.3 %first_adjoint.2 = bf16[16,128,128]{2,1,0:T(8,128)(2,1)S(1)} custom-call(s32[8]{0:T(128)S(1)} %concatenate.9.place, bf16[2,2,2,32,256]{4,3,2,1,0:T(8,128)(2,1)S(1)} %pad_maximum_fusion.2.half, bf16[2,2,2,32,256]{4,3,2,1,0:T(8,128)(2,1)S(1)} %collective-permute-done.17.other, bf16[2,3072,128]{2,1,0:T(8,128)(2,1)S(1)} %multiply_bitcast_fusion.own_k, ...), custom_call_target="tpu_custom_call" | custom-call | flops 5368709120 | bytes 83886080 | tf_op jit(solution)/shard_map/first_adjoint/pallas_call | solution.py:566
  102.5 1.7 %first_adjoint.3 = bf16[8,128,128]{2,1,0:T(8,128)(2,1)S(1)} custom-call(s32[8]{0:T(128)S(1)} %concatenate.9.place, bf16[2,2,2,32,256]{4,3,2,1,0:T(8,128)(2,1)S(1)} %pad_maximum_fusion.2.half, bf16[2,2,2,32,256]{4,3,2,1,0:T(8,128)(2,1)S(1)} %collective-permute-done.17.other, bf16[2,3072,128]{2,1,0:T(8,128)(2,1)S(1)} %multiply_bitcast_fusion.own_k, ...), custom_call_target="tpu_custom_call" | custom-call | flops 2684354560 | bytes 41943040 | tf_op jit(solution)/shard_map/first_adjoint/pallas_call | solution.py:566
  104.2 1.7 %collective-permute-start.22 = (bf16[8,128,128]{2,1,0:T(8,128)(2,1)S(1)}, bf16[8,128,128]{2,1,0:T(8,128)(2,1)S(1)}, u32[]{:S(2)}, u32[]{:S(2)}) collective-permute-start(bf16[8,128,128]{2,1,0:T(8,128)(2,1)S(1)} %first_adjoint.3), channel_id=1, source_target_pairs={{0,2},{2,0},{4,6},{6,4},{1,3},{3,1},{5,7},{7,5},{8,10},{10,8},{12,... | collective-permute-start | bytes 786440 | tf_op jit(solution)/shard_map/ppermute | solution.py:710
  107.4 5.9 %adjoint.1 = (f32[8,128,128]{2,1,0:T(8,128)S(1)}, f32[16,128,128]{2,1,0:T(8,128)S(1)}, f32[8,128,128]{2,1,0:T(8,128)S(1)}, f32[16,128,128]{2,1,0:T(8,128)S(1)}, ...) custom-call(s32[8]{0:T(128)S(1)} %concatenate.9.place, ...), custom_call_target="tpu_custom_call" | custom-call | flops 32212254720 | bytes 251658240 | tf_op jit(solution)/shard_map/adjoint/pallas_call | solution.py:524
  113.4 2.1 %collective-permute-done.25 = bf16[16,128,128]{2,1,0:T(8,128)(2,1)S(1)} collective-permute-done((bf16[16,128,128]{2,1,0:T(8,128)(2,1)S(1)}, bf16[16,128,128]{2,1,0:T(8,128)(2,1)S(1)}, u32[]{:S(2)}, u32[]{:S(2)}) %collective-permute-start.25) | collective-permute-done | bytes 524320 | tf_op jit(solution)/shard_map/ppermute | solution.py:710
  115.8 8.3 %collective-permute-start.21 = (bf16[24,128,128]{2,1,0:T(8,128)(2,1)S(1)}, bf16[24,128,128]{2,1,0:T(8,128)(2,1)S(1)}, u32[]{:S(2)}, u32[]{:S(2)}) collective-permute-start(bf16[24,128,128]{2,1,0:T(8,128)(2,1)S(1)} %pad_maximum_fusion), channel_id=1, source_target_pairs={{0,2},{2,0},{4,6},{6,4},{1,3},{3,1},{5,7},{7,5},{8,10},{10,8},{12,... | collective-permute-start | bytes 2359304 | tf_op jit(solution)/shard_map/ppermute | solution.py:710
  124.5 10.9 %collective-permute-start.27 = (bf16[16,128,128]{2,1,0:T(8,128)(2,1)S(1)}, bf16[16,128,128]{2,1,0:T(8,128)(2,1)S(1)}, u32[]{:S(2)}, u32[]{:S(2)}) collective-permute-start(bf16[16,128,128]{2,1,0:T(8,128)(2,1)S(1)} %add_convert_fusion.1), channel_id=1, source_target_pairs={{0,2},{2,0},{4,6},{6,4},{1,3},{3,1},{5,7},{7,5},{8,10},{10,8},{12,... | collective-permute-start | bytes 1572872 | tf_op jit(solution)/shard_map/ppermute | solution.py:710
  135.4 7.2 %collective-permute-done.21.end_a = bf16[24,128,128]{2,1,0:T(8,128)(2,1)S(1)} collective-permute-done((bf16[24,128,128]{2,1,0:T(8,128)(2,1)S(1)}, bf16[24,128,128]{2,1,0:T(8,128)(2,1)S(1)}, u32[]{:S(2)}, u32[]{:S(2)}) %collective-permute-start.21) | collective-permute-done | bytes 786464 | tf_op jit(solution)/shard_map/ppermute | solution.py:710
  143.0 2.7 %collective-permute-start.24 = (bf16[8,128,128]{2,1,0:T(8,128)(2,1)S(1)}, bf16[8,128,128]{2,1,0:T(8,128)(2,1)S(1)}, u32[]{:S(2)}, u32[]{:S(2)}) collective-permute-start(bf16[8,128,128]{2,1,0:T(8,128)(2,1)S(1)} %add_convert_fusion.4), channel_id=1, source_target_pairs={{0,2},{2,0},{4,6},{6,4},{1,3},{3,1},{5,7},{7,5},{8,10},{10,8},{12,... | collective-permute-start | bytes 786440 | tf_op jit(solution)/shard_map/ppermute | solution.py:710
  145.8 11.7 %collective-permute-done.24.rest_2_ = bf16[8,128,128]{2,1,0:T(8,128)(2,1)S(1)} collective-permute-done((bf16[8,128,128]{2,1,0:T(8,128)(2,1)S(1)}, bf16[8,128,128]{2,1,0:T(8,128)(2,1)S(1)}, u32[]{:S(2)}, u32[]{:S(2)}) %collective-permute-start.24) | collective-permute-done | bytes 262176 | tf_op jit(solution)/shard_map/ppermute | solution.py:710
  157.5 3.4 %final.1 = f32[64,2,4096]{2,1,0:T(2,128)} custom-call(s32[8]{0:T(128)S(1)} %concatenate.9.place, f32[8,128,128]{2,1,0:T(8,128)S(1)} %get-tuple-element.45.part_a, bf16[16,128,128]{2,1,0:T(8,128)(2,1)S(1)} %collective-permute-done.20.peer_a, bf16[24,128,128]{2,1,0:T(8,128)(2,1)S(1)} %collective-permute-done.21.end_a, ...), custom_call_target="tpu_custom_call" | custom-call | flops 2097152 | bytes 6291456 | tf_op jit(solution)/shard_map/final/pallas_call | solution.py:666
  (108 shorter events, 31.1 us)
Async XLA Ops:
  0.0 56.2 %copy-start = (bf16[1,2,128,512]{3,2,1,0:T(8,128)(2,1)S(1)}, bf16[1,2,128,512]{3,2,1,0:T(8,128)(2,1)}, u32[]{:S(2)}) copy-start(bf16[1,2,128,512]{3,2,1,0:T(8,128)(2,1)} %param.14) | copy-start | bytes 786436
  3.5 22.1 %collective-permute-start.3 = (bf16[24,128,128]{2,1,0:T(8,128)(2,1)}, bf16[24,128,128]{2,1,0:T(8,128)(2,1)}, u32[]{:S(2)}, u32[]{:S(2)}) collective-permute-start(bf16[24,128,128]{2,1,0:T(8,128)(2,1)} %bitcast.9), channel_id=1, source_target_pairs={{0,2},{2,0},{4,6},{6,4},{1,3},{3,1},{5,7},{7,5},{8,10},{10,8},{12,... | collective-permute-start | bytes 2359304 | tf_op jit(solution)/shard_map/ppermute | solution.py:710
  6.6 17.6 %collective-permute-start.1 = (bf16[24,128,128]{2,1,0:T(8,128)(2,1)}, bf16[24,128,128]{2,1,0:T(8,128)(2,1)}, u32[]{:S(2)}, u32[]{:S(2)}) collective-permute-start(bf16[24,128,128]{2,1,0:T(8,128)(2,1)} %bitcast.9), channel_id=1, source_target_pairs={{2,4},{4,2},{10,12},{12,10},{0,8},{8,0},{6,14},{14,6},{3,5},{5,3},... | collective-permute-start | bytes 2359304 | tf_op jit(solution)/shard_map/ppermute | solution.py:713
  9.0 14.4 %collective-permute-start = (bf16[2,1024,128]{2,1,0:T(8,128)(2,1)S(1)}, bf16[2,1024,128]{2,1,0:T(8,128)(2,1)S(1)}, u32[]{:S(2)}, u32[]{:S(2)}) collective-permute-start(bf16[2,1024,128]{2,1,0:T(8,128)(2,1)S(1)} %multiply_bitcast_fusion.1.own_a), channel_id=1, source_target_pairs={{0,1},{1,0},{2,3},{3,2},{4,5},{5,4},{6,7},{7,6},{8,9},{9,8},{10,11... | collective-permute-start | bytes 1572872 | tf_op jit(solution)/shard_map/ppermute | solution.py:724
  24.2 36.2 %collective-permute-start.2 = (bf16[2,3072,128]{2,1,0:T(8,128)(2,1)S(1)}, bf16[2,3072,128]{2,1,0:T(8,128)(2,1)}, u32[]{:S(2)}, u32[]{:S(2)}) collective-permute-start(bf16[2,3072,128]{2,1,0:T(8,128)(2,1)S(1)} %multiply_bitcast_fusion.own_k), channel_id=1, source_target_pairs={{0,1},{1,0},{2,3},{3,2},{4,5},{5,4},{6,7},{7,6},{8,9},{9,8},{10,11... | collective-permute-start | bytes 4718600 | tf_op jit(solution)/shard_map/ppermute | solution.py:727
  25.7 8.7 %collective-permute-start.5 = (bf16[24,128,128]{2,1,0:T(8,128)(2,1)}, bf16[24,128,128]{2,1,0:T(8,128)(2,1)}, u32[]{:S(2)}, u32[]{:S(2)}) collective-permute-start(bf16[24,128,128]{2,1,0:T(8,128)(2,1)} %collective-permute-done.3.slot1), channel_id=1, source_target_pairs={{2,4},{4,2},{10,12},{12,10},{0,8},{8,0},{6,14},{14,6},{3,5},{5,3},... | collective-permute-start | bytes 2359304 | tf_op jit(solution)/shard_map/ppermute | solution.py:713
  29.4 22.5 %collective-permute-start.4 = (bf16[24,128,128]{2,1,0:T(8,128)(2,1)S(1)}, bf16[24,128,128]{2,1,0:T(8,128)(2,1)S(1)}, u32[]{:S(2)}, u32[]{:S(2)}) collective-permute-start(bf16[24,128,128]{2,1,0:T(8,128)(2,1)S(1)} %pack.2), channel_id=1, source_target_pairs={{0,2},{2,0},{4,6},{6,4},{1,3},{3,1},{5,7},{7,5},{8,10},{10,8},{12,... | collective-permute-start | bytes 2359304 | tf_op jit(solution)/shard_map/ppermute | solution.py:710
  36.6 30.6 %collective-permute-start.6 = (bf16[24,128,128]{2,1,0:T(8,128)(2,1)}, bf16[24,128,128]{2,1,0:T(8,128)(2,1)}, u32[]{:S(2)}, u32[]{:S(2)}) collective-permute-start(bf16[24,128,128]{2,1,0:T(8,128)(2,1)} %pack.3), channel_id=1, source_target_pairs={{0,2},{2,0},{4,6},{6,4},{1,3},{3,1},{5,7},{7,5},{8,10},{10,8},{12,... | collective-permute-start | bytes 2359304 | tf_op jit(solution)/shard_map/ppermute | solution.py:710
  53.7 11.7 %collective-permute-start.7 = (bf16[16,128,128]{2,1,0:T(8,128)(2,1)}, bf16[16,128,128]{2,1,0:T(8,128)(2,1)}, u32[]{:S(2)}, u32[]{:S(2)}) collective-permute-start(bf16[16,128,128]{2,1,0:T(8,128)(2,1)} %pad_maximum_fusion.1), channel_id=1, source_target_pairs={{2,4},{4,2},{10,12},{12,10},{0,8},{8,0},{6,14},{14,6},{3,5},{5,3},... | collective-permute-start | bytes 1572872 | tf_op jit(solution)/shard_map/ppermute | solution.py:713
  65.3 22.7 %copy-start.9 = (bf16[256,256]{1,0:T(8,128)(2,1)S(1)}, bf16[256,256]{1,0:T(8,128)(2,1)}, u32[]{:S(2)}) copy-start(bf16[256,256]{1,0:T(8,128)(2,1)} %constant.51.clone.sl) | copy-start | bytes 393220
  71.4 1.6 collective-permute-start.9
  71.5 5.0 %collective-permute-start.8 = (f32[2,2,2,32,256]{4,3,2,1,0:T(8,128)S(1)}, f32[2,2,2,32,256]{4,3,2,1,0:T(8,128)S(1)}, u32[]{:S(2)}, u32[]{:S(2)}) collective-permute-start(f32[2,2,2,32,256]{4,3,2,1,0:T(8,128)S(1)} %get-tuple-element.35), channel_id=1, source_target_pairs={{0,8},{8,0},{1,9},{9,1},{2,10},{10,2},{3,11},{11,3},{4,12},{12,4},... | collective-permute-start | bytes 786440 | tf_op jit(solution)/shard_map/ppermute | solution.py:746
  73.0 7.2 %collective-permute-start.10 = (bf16[2,2,2,32,256]{4,3,2,1,0:T(8,128)(2,1)S(1)}, bf16[2,2,2,32,256]{4,3,2,1,0:T(8,128)(2,1)S(1)}, u32[]{:S(2)}, u32[]{:S(2)}) collective-permute-start(bf16[2,2,2,32,256]{4,3,2,1,0:T(8,128)(2,1)S(1)} %near_sum.1), channel_id=1, source_target_pairs={{0,2},{2,0},{4,6},{6,4},{1,3},{3,1},{5,7},{7,5},{8,10},{10,8},{12,... | collective-permute-start | bytes 393224 | tf_op jit(solution)/shard_map/ppermute | solution.py:710
  80.8 4.3 %collective-permute-start.11 = (f32[2,32,256]{2,1,0:T(8,128)S(1)}, f32[2,32,256]{2,1,0:T(8,128)S(1)}, u32[]{:S(2)}, u32[]{:S(2)}) collective-permute-start(f32[2,32,256]{2,1,0:T(8,128)S(1)} %get-tuple-element.39), channel_id=1, source_target_pairs={{0,16},{16,0},{1,17},{17,1},{2,18},{18,2},{3,19},{19,3},{4,20},{20... | collective-permute-start | bytes 196616 | tf_op jit(solution)/shard_map/ppermute | solution.py:748
  82.4 4.5 %collective-permute-start.12 = (f32[2,32,256]{2,1,0:T(8,128)S(1)}, f32[2,32,256]{2,1,0:T(8,128)S(1)}, u32[]{:S(2)}, u32[]{:S(2)}) collective-permute-start(f32[2,32,256]{2,1,0:T(8,128)S(1)} %get-tuple-element.40), channel_id=1, source_target_pairs={{0,1},{1,0},{2,3},{3,2},{4,5},{5,4},{6,7},{7,6},{8,9},{9,8},{10,11... | collective-permute-start | bytes 196616 | tf_op jit(solution)/shard_map/ppermute | solution.py:749
  82.9 5.2 %collective-permute-start.13 = (f32[2,32,256]{2,1,0:T(8,128)S(1)}, f32[2,32,256]{2,1,0:T(8,128)S(1)}, u32[]{:S(2)}, u32[]{:S(2)}) collective-permute-start(f32[2,32,256]{2,1,0:T(8,128)S(1)} %get-tuple-element.41), channel_id=1, source_target_pairs={{0,17},{1,16},{16,1},{17,0},{2,19},{3,18},{18,3},{19,2},{4,21},{5,... | collective-permute-start | bytes 196616 | tf_op jit(solution)/shard_map/ppermute | solution.py:750
  89.5 4.0 %collective-permute-start.15 = (bf16[2,32,256]{2,1,0:T(8,128)(2,1)S(1)}, bf16[2,32,256]{2,1,0:T(8,128)(2,1)S(1)}, u32[]{:S(2)}, u32[]{:S(2)}) collective-permute-start(bf16[2,32,256]{2,1,0:T(8,128)(2,1)S(1)} %get-tuple-element.42), channel_id=1, source_target_pairs={{0,16},{16,0},{1,17},{17,1},{2,18},{18,2},{3,19},{19,3},{4,20},{20... | collective-permute-start | bytes 98312 | tf_op jit(solution)/shard_map/ppermute | solution.py:752
  90.1 4.8 %collective-permute-start.16 = (bf16[2,32,256]{2,1,0:T(8,128)(2,1)S(1)}, bf16[2,32,256]{2,1,0:T(8,128)(2,1)S(1)}, u32[]{:S(2)}, u32[]{:S(2)}) collective-permute-start(bf16[2,32,256]{2,1,0:T(8,128)(2,1)S(1)} %get-tuple-element.43), channel_id=1, source_target_pairs={{0,17},{1,16},{16,1},{17,0},{2,19},{3,18},{18,3},{19,2},{4,21},{5,... | collective-permute-start | bytes 98312 | tf_op jit(solution)/shard_map/ppermute | solution.py:754
  92.5 3.9 %collective-permute-start.14 = (bf16[2,32,256]{2,1,0:T(8,128)(2,1)S(1)}, bf16[2,32,256]{2,1,0:T(8,128)(2,1)S(1)}, u32[]{:S(2)}, u32[]{:S(2)}) collective-permute-start(bf16[2,32,256]{2,1,0:T(8,128)(2,1)S(1)} %get-tuple-element.43), channel_id=1, source_target_pairs={{0,1},{1,0},{2,3},{3,2},{4,5},{5,4},{6,7},{7,6},{8,9},{9,8},{10,11... | collective-permute-start | bytes 98312 | tf_op jit(solution)/shard_map/ppermute | solution.py:753
  96.5 1.9 %collective-permute-start.17 = (bf16[2,2,2,32,256]{4,3,2,1,0:T(8,128)(2,1)S(1)}, bf16[2,2,2,32,256]{4,3,2,1,0:T(8,128)(2,1)S(1)}, u32[]{:S(2)}, u32[]{:S(2)}) collective-permute-start(bf16[2,2,2,32,256]{4,3,2,1,0:T(8,128)(2,1)S(1)} %pad_maximum_fusion.2.half), channel_id=1, source_target_pairs={{0,8},{8,0},{1,9},{9,1},{2,10},{10,2},{3,11},{11,3},{4,12},{12,4},... | collective-permute-start | bytes 393224 | tf_op jit(solution)/shard_map/ppermute | solution.py:756
  96.6 5.9 %collective-permute-start.18 = (bf16[2,2,2,32,256]{4,3,2,1,0:T(8,128)(2,1)S(1)}, bf16[2,2,2,32,256]{4,3,2,1,0:T(8,128)(2,1)S(1)}, u32[]{:S(2)}, u32[]{:S(2)}) collective-permute-start(bf16[2,2,2,32,256]{4,3,2,1,0:T(8,128)(2,1)S(1)} %pad_maximum_fusion.2.half), channel_id=1, source_target_pairs={{0,2},{2,0},{4,6},{6,4},{1,3},{3,1},{5,7},{7,5},{8,10},{10,8},{12,... | collective-permute-start | bytes 393224 | tf_op jit(solution)/shard_map/ppermute | solution.py:710
  100.6 14.8 %collective-permute-start.25 = (bf16[16,128,128]{2,1,0:T(8,128)(2,1)S(1)}, bf16[16,128,128]{2,1,0:T(8,128)(2,1)S(1)}, u32[]{:S(2)}, u32[]{:S(2)}) collective-permute-start(bf16[16,128,128]{2,1,0:T(8,128)(2,1)S(1)} %first_adjoint.2), channel_id=1, source_target_pairs={{0,2},{2,0},{4,6},{6,4},{1,3},{3,1},{5,7},{7,5},{8,10},{10,8},{12,... | collective-permute-start | bytes 1572872 | tf_op jit(solution)/shard_map/ppermute | solution.py:710
  102.5 3.4 %collective-permute-start.19 = (bf16[2,2,2,32,256]{4,3,2,1,0:T(8,128)(2,1)S(1)}, bf16[2,2,2,32,256]{4,3,2,1,0:T(8,128)(2,1)S(1)}, u32[]{:S(2)}, u32[]{:S(2)}) collective-permute-start(bf16[2,2,2,32,256]{4,3,2,1,0:T(8,128)(2,1)S(1)} %collective-permute-done.18.near_half), channel_id=1, source_target_pairs={{0,8},{8,0},{1,9},{9,1},{2,10},{10,2},{3,11},{11,3},{4,12},{12,4},... | collective-permute-start | bytes 393224 | tf_op jit(solution)/shard_map/ppermute | solution.py:767
  104.2 20.0 %collective-permute-start.22 = (bf16[8,128,128]{2,1,0:T(8,128)(2,1)S(1)}, bf16[8,128,128]{2,1,0:T(8,128)(2,1)S(1)}, u32[]{:S(2)}, u32[]{:S(2)}) collective-permute-start(bf16[8,128,128]{2,1,0:T(8,128)(2,1)S(1)} %first_adjoint.3), channel_id=1, source_target_pairs={{0,2},{2,0},{4,6},{6,4},{1,3},{3,1},{5,7},{7,5},{8,10},{10,8},{12,... | collective-permute-start | bytes 786440 | tf_op jit(solution)/shard_map/ppermute | solution.py:710
  107.1 8.6 %collective-permute-start.20 = (bf16[16,128,128]{2,1,0:T(8,128)(2,1)S(1)}, bf16[16,128,128]{2,1,0:T(8,128)(2,1)S(1)}, u32[]{:S(2)}, u32[]{:S(2)}) collective-permute-start(bf16[16,128,128]{2,1,0:T(8,128)(2,1)S(1)} %get-tuple-element.46), channel_id=1, source_target_pairs={{2,4},{4,2},{10,12},{12,10},{0,8},{8,0},{6,14},{14,6},{3,5},{5,3},... | collective-permute-start | bytes 1572872 | tf_op jit(solution)/shard_map/ppermute | solution.py:713
  115.6 8.7 %collective-permute-start.26 = (bf16[16,128,128]{2,1,0:T(8,128)(2,1)S(1)}, bf16[16,128,128]{2,1,0:T(8,128)(2,1)S(1)}, u32[]{:S(2)}, u32[]{:S(2)}) collective-permute-start(bf16[16,128,128]{2,1,0:T(8,128)(2,1)S(1)} %add_convert_fusion.2), channel_id=1, source_target_pairs={{2,4},{4,2},{10,12},{12,10},{0,8},{8,0},{6,14},{14,6},{3,5},{5,3},... | collective-permute-start | bytes 1572872 | tf_op jit(solution)/shard_map/ppermute | solution.py:713
  115.8 26.8 %collective-permute-start.21 = (bf16[24,128,128]{2,1,0:T(8,128)(2,1)S(1)}, bf16[24,128,128]{2,1,0:T(8,128)(2,1)S(1)}, u32[]{:S(2)}, u32[]{:S(2)}) collective-permute-start(bf16[24,128,128]{2,1,0:T(8,128)(2,1)S(1)} %pad_maximum_fusion), channel_id=1, source_target_pairs={{0,2},{2,0},{4,6},{6,4},{1,3},{3,1},{5,7},{7,5},{8,10},{10,8},{12,... | collective-permute-start | bytes 2359304 | tf_op jit(solution)/shard_map/ppermute | solution.py:710
  124.3 18.6 %collective-permute-start.23 = (bf16[8,128,128]{2,1,0:T(8,128)(2,1)S(1)}, bf16[8,128,128]{2,1,0:T(8,128)(2,1)S(1)}, u32[]{:S(2)}, u32[]{:S(2)}) collective-permute-start(bf16[8,128,128]{2,1,0:T(8,128)(2,1)S(1)} %add_convert_fusion.5), channel_id=1, source_target_pairs={{2,4},{4,2},{10,12},{12,10},{0,8},{8,0},{6,14},{14,6},{3,5},{5,3},... | collective-permute-start | bytes 786440 | tf_op jit(solution)/shard_map/ppermute | solution.py:713
  124.5 32.9 %collective-permute-start.27 = (bf16[16,128,128]{2,1,0:T(8,128)(2,1)S(1)}, bf16[16,128,128]{2,1,0:T(8,128)(2,1)S(1)}, u32[]{:S(2)}, u32[]{:S(2)}) collective-permute-start(bf16[16,128,128]{2,1,0:T(8,128)(2,1)S(1)} %add_convert_fusion.1), channel_id=1, source_target_pairs={{0,2},{2,0},{4,6},{6,4},{1,3},{3,1},{5,7},{7,5},{8,10},{10,8},{12,... | collective-permute-start | bytes 1572872 | tf_op jit(solution)/shard_map/ppermute | solution.py:710
  142.8 14.7 %collective-permute-start.29 = (bf16[16,128,128]{2,1,0:T(8,128)(2,1)S(1)}, bf16[16,128,128]{2,1,0:T(8,128)(2,1)S(1)}, u32[]{:S(2)}, u32[]{:S(2)}) collective-permute-start(bf16[16,128,128]{2,1,0:T(8,128)(2,1)S(1)} %add_convert_fusion), channel_id=1, source_target_pairs={{2,4},{4,2},{10,12},{12,10},{0,8},{8,0},{6,14},{14,6},{3,5},{5,3},... | collective-permute-start | bytes 1572872 | tf_op jit(solution)/shard_map/ppermute | solution.py:713
  143.0 14.5 %collective-permute-start.24 = (bf16[8,128,128]{2,1,0:T(8,128)(2,1)S(1)}, bf16[8,128,128]{2,1,0:T(8,128)(2,1)S(1)}, u32[]{:S(2)}, u32[]{:S(2)}) collective-permute-start(bf16[8,128,128]{2,1,0:T(8,128)(2,1)S(1)} %add_convert_fusion.4), channel_id=1, source_target_pairs={{0,2},{2,0},{4,6},{6,4},{1,3},{3,1},{5,7},{7,5},{8,10},{10,8},{12,... | collective-permute-start | bytes 786440 | tf_op jit(solution)/shard_map/ppermute | solution.py:710
  145.7 11.7 %collective-permute-start.28 = (bf16[8,128,128]{2,1,0:T(8,128)(2,1)S(1)}, bf16[8,128,128]{2,1,0:T(8,128)(2,1)S(1)}, u32[]{:S(2)}, u32[]{:S(2)}) collective-permute-start(bf16[8,128,128]{2,1,0:T(8,128)(2,1)S(1)} %add_convert_fusion.3), channel_id=1, source_target_pairs={{2,4},{4,2},{10,12},{12,10},{0,8},{8,0},{6,14},{14,6},{3,5},{5,3},... | collective-permute-start | bytes 786440 | tf_op jit(solution)/shard_map/ppermute | solution.py:713
  (15 other events, 147.6 us)

commit v4 on v3

--- a/solution.py
+++ b/solution.py
@@ -194,7 +194,7 @@
     )(place, keep, got, near)
 
 
-def early_kernel(place, own_k, far_k, slot0, slot1, mid2, end2, *rest):
+def early_kernel(place, own_k, slot0, slot1, mid2, end2, *rest):
     total = rest[-1]
 
     @pl.when(pl.program_id(0) == 0)
@@ -203,53 +203,54 @@
 
     third = jnp.where(place[0] == 1, mid2[...], end2[...])
     rows = jnp.concatenate([wide(slot0[...]), wide(slot1[...]), wide(third)], axis=0)
-    for blk, part in enumerate((own_k, far_k)):
-        total[blk] += dot(rows, paired(part))
-
-
-def early(place, own_k, far_k, sky, r1, m1, r2, ready):
+    total[...] += dot(rows, paired(own_k))
+
+
+def early(place, own_k, sky, r1, m1, r2, ready):
     count, rows, _ = r1.shape
     base = own_k.shape[2]
     tiles = count // 3
     k_spec = pl.BlockSpec((2, tiles * LANES, base), lambda i: (0, i, 0))
-    own_spec = pl.BlockSpec((tiles, rows, LANES), lambda i: (i + 1, 0, 0))
     s_spec = pl.BlockSpec((tiles, rows, LANES), lambda i: (i, 0, 0))
-    shape = (2, 3 * rows, 2 * base)
+    shape = (3 * rows, 2 * base)
     return pl.pallas_call(
         early_kernel,
         grid=(3,),
-        in_specs=[pl.BlockSpec(memory_space=pltpu.SMEM), k_spec, k_spec, own_spec]
-        + [s_spec] * 3
+        in_specs=[pl.BlockSpec(memory_space=pltpu.SMEM), k_spec]
+        + [s_spec] * 4
         + [pl.BlockSpec(memory_space=pl.ANY)] * len(ready),
-        out_specs=pl.BlockSpec(shape, lambda i: (0, 0, 0)),
+        out_specs=pl.BlockSpec(shape, lambda i: (0, 0)),
         out_shape=jax.ShapeDtypeStruct(shape, jnp.float32),
         compiler_params=pltpu.CompilerParams(vmem_limit_bytes=VMEM_LIMIT),
         cost_estimate=cost(
-            flops=12 * rows * count * LANES * 2 * base, bytes_accessed=8 * 2**20, transcendentals=0
+            flops=6 * rows * count * LANES * 2 * base, bytes_accessed=4 * 2**20, transcendentals=0
         ),
         name="early",
-    )(place, own_k, far_k, sky, r1, m1, r2, *ready)
+    )(place, own_k, sky, r1, m1, r2, *ready)
 
 
 def late_kernel(
-    place, done, own_k, far_k, mid3, end3, own_a, far_a, sky_a, near_sky, peer_sky, peer_near_sky,
+    place, done, own_k, far_k, slot0, slot1, mid2, end2, mid3, end3, own_a, far_a, sky_a, near_sky, peer_sky, peer_near_sky,
     near_k, near_far_k, keep, send, near_keep, near_send, total, near_total
 ):
     step = pl.program_id(0)
     is_mid = place[0] == 1
-    done_rows = done.shape[1]
+    done_rows = done.shape[0]
     rows = done_rows // 3
 
     @pl.when(step == 0)
     def _():
-        total[:, :done_rows] = done[...]
-        total[:, done_rows:] = jnp.zeros_like(total[:, done_rows:])
+        total[0, :done_rows] = done[...]
+        total[0, done_rows:] = jnp.zeros_like(total[0, done_rows:])
+        total[1] = jnp.zeros_like(total[1])
 
     @pl.when(step < 3)
     def _():
+        third = wide(jnp.where(is_mid, mid2[...], end2[...]))
         last = wide(jnp.where(is_mid, mid3[...], end3[...]))
-        for blk, part in enumerate((own_k, far_k)):
-            total[blk, done_rows:] += dot(last, paired(part))
+        every = jnp.concatenate([wide(slot0[...]), wide(slot1[...]), third, last], axis=0)
+        total[0, done_rows:] += dot(last, paired(own_k))
+        total[1] += dot(every, paired(far_k))
 
     @pl.when((step == 3) & is_mid)
     def _():
@@ -295,8 +296,8 @@
                             ]
 
 
-def late(place, done, own_k, far_k, mid3, own_a, far_a, sky, r2, r3, m3, chunk):
-    count, rows, _ = mid3.shape
+def late(place, done, own_k, far_k, sky_b, r1, m1, m2, own_a, far_a, sky_a, r2, r3, m3, chunk):
+    count, rows, _ = m2.shape
     base = own_k.shape[2]
     tiles = count // 3
     k_spec = pl.BlockSpec((2, tiles * LANES, base), lambda i: (0, jnp.minimum(i, 2), 0))
@@ -312,8 +313,8 @@
         grid=(4,),
         in_specs=[
             pl.BlockSpec(memory_space=pltpu.SMEM),
-            pl.BlockSpec(done.shape, lambda i: (0, 0, 0)),
-            k_spec, k_spec, s_spec, s_spec, a_spec, a_spec, one, third, one, second, two, two,
+            pl.BlockSpec(done.shape, lambda i: (0, 0)),
+            k_spec, k_spec, s_spec, s_spec, s_spec, s_spec, s_spec, s_spec, a_spec, a_spec, one, third, one, second, two, two,
         ],
         out_specs=[pl.BlockSpec(shape, lambda i: (0,) * 5)] * 4,
         out_shape=[jax.ShapeDtypeStruct(shape, jnp.float32)] * 4,
@@ -327,7 +328,7 @@
         ),
         name="late",
     )(
-        place, done, own_k, far_k, mid3, r3, own_a, far_a, sky, r2, m3, m3, r2, r3
+        place, done, own_k, far_k, sky_b, r1, m1, r2, m2, r3, own_a, far_a, sky_a, r2, m3, m3, r2, r3
     )
 
 
@@ -721,12 +722,16 @@
     weight = jnp.sum(jnp.where(column, block_tiles[0], 0)).astype(jnp.bfloat16)
     own_a = lax.optimization_barrier(kernel[0, 0, :, :cut] * weight)
     own_b = kernel[0, 0, :, cut:] * weight
+    end2 = jnp.concatenate([as_tiles(own_a), sky_a])
+    own_a, end2 = lax.optimization_barrier((own_a, end2))
     far_a = lax.ppermute(own_a, "inner", SWAP)
+    pay2 = jnp.where(is_mid, m1, end2)
+    end3 = jnp.concatenate([as_tiles(far_a), sky_a])
+    own_b, far_a, m1, end3 = lax.optimization_barrier((own_b, far_a, m1, end3))
+    (r2,) = ends(pay2)
     (m2,) = mids(r1)
-    own_b, far_a, m1 = lax.optimization_barrier((own_b, far_a, m1))
     far_b = lax.ppermute(own_b, "inner", SWAP)
-    (r2,) = ends(pack(place, m1, as_tiles(own_a), sky_a))
-    (r3,) = ends(pack(place, m2, as_tiles(far_a), sky_a))
+    (r3,) = ends(jnp.where(is_mid, m2, end3))
     (m3,) = mids(jnp.concatenate([sky_a, r2[2 * tiles :]]))
 
     parts = table_parts(length)
@@ -738,9 +743,9 @@
     own_bins = lax.dynamic_slice_in_dim(length_bin[0], tile_pos * chunk, chunk, 0)
     keep = by_parity(wedge_keep.astype(jnp.float32))[own_bins]
 
-    done = early(place, own_b, far_b, own_sky, r1, m1, r2, (own_data, keep))
+    done = early(place, own_b, sky_b, r1, m1, r2, (own_data, keep))
     keep_vis, send_vis, near_keep, near_send = late(
-        place, done, own_b, far_b, m2, own_a, far_a, own_sky, r2, r3, m3, chunk
+        place, done, own_b, far_b, sky_b, r1, m1, m2, own_a, far_a, sky_a, r2, r3, m3, chunk
     )
     (near,) = ends(near_sum(near_keep, lax.ppermute(near_send, "tl", SWAP)))
     got = lax.ppermute(send_vis, "tl", SWAP)
@@ -774,13 +779,14 @@
         place, half, other, own_b, far_b, (3, 2, 1, 0), jnp.float32
     )
     far3 = mids(*(plus(part, got) for part, got in zip(part3, g1)))
-    first = jnp.where(is_mid, plus(part1_a, peer_a[:tiles]), part2[0].astype(low))
-    (g2,) = ends(jnp.concatenate([first, part2[1].astype(low)]))
-    far2 = mids(plus(part2[0], g2[:tiles]), plus(part2[1], g2[tiles:]))
+    ready_a = jnp.where(is_mid, plus(part1_a, peer_a[:tiles]), part2[0].astype(low))
+    g2 = ends(ready_a, part2[1].astype(low))
+    g2, far3 = lax.optimization_barrier((g2, far3))
+    far2 = mids(*(plus(part, got) for part, got in zip(part2, g2)))
     g3 = ends(
         *(plus(part, jnp.where(is_mid, got, jnp.zeros_like(got))) for part, got in zip(part1, far3))
     )
-    return final(place, part0_a, peer_a, g2, part0, g3, far2)[None]
+    return final(place, part0_a, peer_a, g2[0], part0, g3, far2)[None]
 
 
 def body(sky, kernel, *rest):

time: 162 us -> 158 us (0.975)
  waiting for transfers between devices: 50.4 us -> 64.8 us
  starting transfers between devices: 61.5 us -> 47.5 us
  local copies, waits for them, and re-layouts: 14.9 us -> 10.7 us
  other arithmetic: 5.03 us -> 8.73 us
  Pallas kernels: 27.9 us -> 24.8 us
    ppermute x10 -> x11, waiting for transfers between devices: 30.4 us -> 54.5 us  [ends(): return [lax.ppermute(value, 'outer', ENDS) for value in values]]
    ppermute x10 -> x11, starting transfers between devices: 50.1 us -> 35.7 us  [ends(): return [lax.ppermute(value, 'outer', ENDS) for value in values]]
    ppermute x1, waiting for transfers between devices: 11.3 us -> 2.13 us  [line_body(): far_a = lax.ppermute(own_a, 'inner', SWAP)]
    pallas_call x2 -> x0, Pallas kernels: 3.44 us -> none  [pack(): pl.pallas_call(pack_kernel, in_specs=[pl.BlockSpec(memory_space=pltpu.SME...]
    concatenate x1 -> x2, other arithmetic: 0.07 us -> 3.18 us  [the longest x1 1.99 us: line_body(): end2 = jnp.concatenate([as_tiles(own_a), sky_a])]
    unnamed x35 -> x33, local copies, waits for them, and re-layouts: 4.45 us -> 1.84 us
  transfers between devices with their start and end apart: 30 -> 31, of which waited for: 16 -> 17; matrix products, arithmetic and copies ran while one was open for 8% -> 10% of each run, Pallas kernels for 11% -> 9%
where the time goes in v4:
time: 158 us; the launch traced here: 157 us
  waiting for transfers between devices  64.8 us (41%)
  starting transfers between devices  47.5 us (30%)
  Pallas kernels  24.8 us (16%)
  local copies, waits for them, and re-layouts  10.7 us (7%)
  other arithmetic  8.73 us (6%)
    ppermute x11, waiting for transfers between devices, ends(): return [lax.ppermute(value, 'outer', ENDS) for value in values]  54.5 us
    ppermute x11, starting transfers between devices, ends(): return [lax.ppermute(value, 'outer', ENDS) for value in values]  35.7 us
    pallas_call x1, Pallas kernels, adjoint(): pl.pallas_call(functools.partial(adjoint_kernel, slots, ends_only), grid=...  5.88 us
    pallas_call x1, Pallas kernels, late(): pl.pallas_call(late_kernel, grid=(4,), in_specs=[pl.BlockSpec(memory_spac...  5.24 us
    pallas_call x2, Pallas kernels, first_adjoint(): pl.pallas_call(functools.partial(first_kernel, slot), grid=(steps,), in_s...  3.94 us
    pallas_call x1, Pallas kernels, final(): pl.pallas_call(final_kernel, grid=(4,), in_specs=[pl.BlockSpec(memory_spa...  3.37 us
  transfers between devices with their start and end apart: 31, of which 17 were waited for; matrix products, arithmetic and copies ran while one was open for 10% of the time, Pallas kernels for 9%

profile of v4, /device:TPU:0, one launch (start us, length us, event | category | flops | bytes accessed | tf_op | source)
XLA Modules:
  0.0 157.5 jit_solution(5177217981122249473)
XLA Ops:
  0.0 1.9 %reshape_squeeze.3 = bf16[64,2,32,128]{3,2,1,0:T(8,128)(2,1)S(1)} reshape(bf16[1,64,2,4096]{3,2,1,0:T(2,128)(2,1)} %param.12) | data formatting | bytes 2097152 | tf_op jit(solution)/shard_map/reshape;squeeze | solution.py:707
  2.7 3.1 %collective-permute-start.2 = (bf16[24,128,128]{2,1,0:T(8,128)(2,1)S(1)}, bf16[24,128,128]{2,1,0:T(8,128)(2,1)}, u32[]{:S(2)}, u32[]{:S(2)}) collective-permute-start(bf16[24,128,128]{2,1,0:T(8,128)(2,1)S(1)} %bitcast.44), channel_id=1, source_target_pairs={{0,2},{2,0},{4,6},{6,4},{1,3},{3,1},{5,7},{7,5},{8,10},{10,8},{12,... | collective-permute-start | bytes 2359304 | tf_op jit(solution)/shard_map/ppermute | solution.py:711
  7.0 2.1 %multiply_bitcast_fusion.1.own_a = bf16[2,1024,128]{2,1,0:T(8,128)(2,1)} fusion(bf16[1,1,2,4096,128]{4,3,2,1,0:T(8,128)(2,1)} %param.13, bf16[]{:T(256)S(6)} %convert_element_type.55), kind=kLoop, calls=%fused_computation.15 | loop fusion | flops 262144 | bytes 1048578 | tf_op jit(solution)/shard_map/mul | solution.py:723
  9.1 2.0 %pad_maximum_fusion.1 = bf16[24,128,128]{2,1,0:T(8,128)(2,1)} fusion(bf16[8,128,128]{2,1,0:T(8,128)(2,1)S(1)} %bitcast.48, bf16[16,128,128]{2,1,0:T(8,128)(2,1)} %bitcast.8), kind=kLoop, calls=%fused_computation.7 | loop fusion | flops 393216 | bytes 1572864 | tf_op jit(solution)/shard_map/concatenate | solution.py:725
  12.6 10.9 %collective-permute-done.2.slot1 = bf16[24,128,128]{2,1,0:T(8,128)(2,1)} collective-permute-done((bf16[24,128,128]{2,1,0:T(8,128)(2,1)S(1)}, bf16[24,128,128]{2,1,0:T(8,128)(2,1)}, u32[]{:S(2)}, u32[]{:S(2)}) %collective-permute-start.2) | collective-permute-done | bytes 786464 | tf_op jit(solution)/shard_map/ppermute | solution.py:711
  23.6 2.1 %collective-permute-done.far_a = bf16[2,1024,128]{2,1,0:T(8,128)(2,1)} collective-permute-done((bf16[2,1024,128]{2,1,0:T(8,128)(2,1)}, bf16[2,1024,128]{2,1,0:T(8,128)(2,1)}, u32[]{:S(2)}, u32[]{:S(2)}) %collective-permute-start) | collective-permute-done | bytes 524320 | tf_op jit(solution)/shard_map/ppermute | solution.py:727
  26.9 1.6 %collective-permute-start.4 = (bf16[2,3072,128]{2,1,0:T(8,128)(2,1)S(1)}, bf16[2,3072,128]{2,1,0:T(8,128)(2,1)}, u32[]{:S(2)}, u32[]{:S(2)}) collective-permute-start(bf16[2,3072,128]{2,1,0:T(8,128)(2,1)S(1)} %multiply_bitcast_fusion.own_k), channel_id=1, source_target_pairs={{0,1},{1,0},{2,3},{3,2},{4,5},{5,4},{6,7},{7,6},{8,9},{9,8},{10,11... | collective-permute-start | bytes 4718600 | tf_op jit(solution)/shard_map/ppermute | solution.py:733
  28.6 2.0 %collective-permute-start.3 = (bf16[24,128,128]{2,1,0:T(8,128)(2,1)S(1)}, bf16[24,128,128]{2,1,0:T(8,128)(2,1)S(1)}, u32[]{:S(2)}, u32[]{:S(2)}) collective-permute-start(bf16[24,128,128]{2,1,0:T(8,128)(2,1)S(1)} %broadcast_select_fusion.1), channel_id=1, source_target_pairs={{0,2},{2,0},{4,6},{6,4},{1,3},{3,1},{5,7},{7,5},{8,10},{10,8},{12,... | collective-permute-start | bytes 2359304 | tf_op jit(solution)/shard_map/ppermute | solution.py:711
  31.6 14.4 %collective-permute-start.6 = (bf16[24,128,128]{2,1,0:T(8,128)(2,1)}, bf16[24,128,128]{2,1,0:T(8,128)(2,1)}, u32[]{:S(2)}, u32[]{:S(2)}) collective-permute-start(bf16[24,128,128]{2,1,0:T(8,128)(2,1)} %broadcast_select_fusion), channel_id=1, source_target_pairs={{0,2},{2,0},{4,6},{6,4},{1,3},{3,1},{5,7},{7,5},{8,10},{10,8},{12,... | collective-permute-start | bytes 2359304 | tf_op jit(solution)/shard_map/ppermute | solution.py:711
  46.0 3.2 %collective-permute-done.3.end2.near_sky.near_k = bf16[24,128,128]{2,1,0:T(8,128)(2,1)S(1)} collective-permute-done((bf16[24,128,128]{2,1,0:T(8,128)(2,1)S(1)}, bf16[24,128,128]{2,1,0:T(8,128)(2,1)S(1)}, u32[]{:S(2)}, u32[]{:S(2)}) %collective-permute-start.3) | collective-permute-done | bytes 786464 | tf_op jit(solution)/shard_map/ppermute | solution.py:711
  58.1 2.8 %early.1.done = f32[384,256]{1,0:T(8,128)S(1)} custom-call(s32[8]{0:T(128)S(1)} %concatenate.12.place, bf16[2,3072,128]{2,1,0:T(8,128)(2,1)S(1)} %multiply_bitcast_fusion.own_k, bf16[24,128,128]{2,1,0:T(8,128)(2,1)S(1)} %bitcast.46, bf16[24,128,128]{2,1,0:T(8,128)(2,1)} %collective-permute-done.2.slot1, ...), custom_call_target="tpu_custom_call" | custom-call | flops 603979776 | bytes 4194304 | tf_op jit(solution)/shard_map/early/pallas_call | solution.py:216
  61.0 3.5 %collective-permute-done.6.end3.near_far_k = bf16[24,128,128]{2,1,0:T(8,128)(2,1)} collective-permute-done((bf16[24,128,128]{2,1,0:T(8,128)(2,1)}, bf16[24,128,128]{2,1,0:T(8,128)(2,1)}, u32[]{:S(2)}, u32[]{:S(2)}) %collective-permute-start.6) | collective-permute-done | bytes 786464 | tf_op jit(solution)/shard_map/ppermute | solution.py:711
  64.5 5.2 %late.1 = (f32[2,2,2,32,256]{4,3,2,1,0:T(8,128)S(1)}, f32[2,2,2,32,256]{4,3,2,1,0:T(8,128)S(1)}, f32[2,2,2,32,256]{4,3,2,1,0:T(8,128)S(1)}, f32[2,2,2,32,256]{4,3,2,1,0:T(8,128)S(1)}) custom-call(s32[8]{0:T(128)S(1)} %concatenate.12.place, f32[384,256]{1,0:T(8,128)S(1)} %early.1.done, bf16[2,3072,128]{2,1,0:T(8,128)(2,1)S(1)} %multiply_bitcast_fusion.own_k, ...), custom_call_target="tpu_custom_call" | custom-call | flops 1006632960 | bytes 9437184 | tf_op jit(solution)/shard_map/late/pallas_call | solution.py:311
  71.4 2.2 %collective-permute-start.10 = (bf16[2,2,2,32,256]{4,3,2,1,0:T(8,128)(2,1)S(1)}, bf16[2,2,2,32,256]{4,3,2,1,0:T(8,128)(2,1)S(1)}, u32[]{:S(2)}, u32[]{:S(2)}) collective-permute-start(bf16[2,2,2,32,256]{4,3,2,1,0:T(8,128)(2,1)S(1)} %near_sum.1), channel_id=1, source_target_pairs={{0,2},{2,0},{4,6},{6,4},{1,3},{3,1},{5,7},{7,5},{8,10},{10,8},{12,... | collective-permute-start | bytes 393224 | tf_op jit(solution)/shard_map/ppermute | solution.py:711
  73.6 3.8 %collective-permute-done.10.near = bf16[2,2,2,32,256]{4,3,2,1,0:T(8,128)(2,1)S(1)} collective-permute-done((bf16[2,2,2,32,256]{4,3,2,1,0:T(8,128)(2,1)S(1)}, bf16[2,2,2,32,256]{4,3,2,1,0:T(8,128)(2,1)S(1)}, u32[]{:S(2)}, u32[]{:S(2)}) %collective-permute-start.10) | collective-permute-done | bytes 131104 | tf_op jit(solution)/shard_map/ppermute | solution.py:711
  78.0 1.6 collective-permute-start.11
  82.4 1.7 %collective-permute-done.12.from_y = f32[2,32,256]{2,1,0:T(8,128)S(1)} collective-permute-done((f32[2,32,256]{2,1,0:T(8,128)S(1)}, f32[2,32,256]{2,1,0:T(8,128)S(1)}, u32[]{:S(2)}, u32[]{:S(2)}) %collective-permute-start.12) | collective-permute-done | bytes 65568 | tf_op jit(solution)/shard_map/ppermute | solution.py:754
  87.3 2.5 %collective-permute-start.16 = (bf16[2,32,256]{2,1,0:T(8,128)(2,1)S(1)}, bf16[2,32,256]{2,1,0:T(8,128)(2,1)S(1)}, u32[]{:S(2)}, u32[]{:S(2)}) collective-permute-start(bf16[2,32,256]{2,1,0:T(8,128)(2,1)S(1)} %get-tuple-element.53), channel_id=1, source_target_pairs={{0,17},{1,16},{16,1},{17,0},{2,19},{3,18},{18,3},{19,2},{4,21},{5,... | collective-permute-start | bytes 98312 | tf_op jit(solution)/shard_map/ppermute | solution.py:759
  93.7 1.8 %collective-permute-start.18 = (bf16[2,2,2,32,256]{4,3,2,1,0:T(8,128)(2,1)S(1)}, bf16[2,2,2,32,256]{4,3,2,1,0:T(8,128)(2,1)S(1)}, u32[]{:S(2)}, u32[]{:S(2)}) collective-permute-start(bf16[2,2,2,32,256]{4,3,2,1,0:T(8,128)(2,1)S(1)} %pad_maximum_fusion.3.half), channel_id=1, source_target_pairs={{0,2},{2,0},{4,6},{6,4},{1,3},{3,1},{5,7},{7,5},{8,10},{10,8},{12,... | collective-permute-start | bytes 393224 | tf_op jit(solution)/shard_map/ppermute | solution.py:711
  95.6 2.3 %first_adjoint.2 = bf16[16,128,128]{2,1,0:T(8,128)(2,1)S(1)} custom-call(s32[8]{0:T(128)S(1)} %concatenate.12.place, bf16[2,2,2,32,256]{4,3,2,1,0:T(8,128)(2,1)S(1)} %pad_maximum_fusion.3.half, bf16[2,2,2,32,256]{4,3,2,1,0:T(8,128)(2,1)S(1)} %collective-permute-done.17.other, bf16[2,3072,128]{2,1,0:T(8,128)(2,1)S(1)} %multiply_bitcast_fusion.own_k, ...), custom_call_target="tpu_custom_call" | custom-call | flops 5368709120 | bytes 83886080 | tf_op jit(solution)/shard_map/first_adjoint/pallas_call | solution.py:567
  99.7 1.7 %first_adjoint.3 = bf16[8,128,128]{2,1,0:T(8,128)(2,1)S(1)} custom-call(s32[8]{0:T(128)S(1)} %concatenate.12.place, bf16[2,2,2,32,256]{4,3,2,1,0:T(8,128)(2,1)S(1)} %pad_maximum_fusion.3.half, bf16[2,2,2,32,256]{4,3,2,1,0:T(8,128)(2,1)S(1)} %collective-permute-done.17.other, bf16[2,3072,128]{2,1,0:T(8,128)(2,1)S(1)} %multiply_bitcast_fusion.own_k, ...), custom_call_target="tpu_custom_call" | custom-call | flops 2684354560 | bytes 41943040 | tf_op jit(solution)/shard_map/first_adjoint/pallas_call | solution.py:567
  101.4 1.7 %collective-permute-start.23 = (bf16[8,128,128]{2,1,0:T(8,128)(2,1)S(1)}, bf16[8,128,128]{2,1,0:T(8,128)(2,1)S(1)}, u32[]{:S(2)}, u32[]{:S(2)}) collective-permute-start(bf16[8,128,128]{2,1,0:T(8,128)(2,1)S(1)} %first_adjoint.3), channel_id=1, source_target_pairs={{0,2},{2,0},{4,6},{6,4},{1,3},{3,1},{5,7},{7,5},{8,10},{10,8},{12,... | collective-permute-start | bytes 786440 | tf_op jit(solution)/shard_map/ppermute | solution.py:711
  103.0 1.6 near_adjoint.1
  104.9 5.9 %adjoint.1 = (f32[8,128,128]{2,1,0:T(8,128)S(1)}, f32[16,128,128]{2,1,0:T(8,128)S(1)}, f32[8,128,128]{2,1,0:T(8,128)S(1)}, f32[16,128,128]{2,1,0:T(8,128)S(1)}, ...) custom-call(s32[8]{0:T(128)S(1)} %concatenate.12.place, ...), custom_call_target="tpu_custom_call" | custom-call | flops 32212254720 | bytes 251658240 | tf_op jit(solution)/shard_map/adjoint/pallas_call | solution.py:525
  110.9 3.3 %collective-permute-start.22 = (bf16[16,128,128]{2,1,0:T(8,128)(2,1)S(1)}, bf16[16,128,128]{2,1,0:T(8,128)(2,1)S(1)}, u32[]{:S(2)}, u32[]{:S(2)}) collective-permute-start(bf16[16,128,128]{2,1,0:T(8,128)(2,1)S(1)} %convert_element_type.60), channel_id=1, source_target_pairs={{0,2},{2,0},{4,6},{6,4},{1,3},{3,1},{5,7},{7,5},{8,10},{10,8},{12,... | collective-permute-start | bytes 1572872 | tf_op jit(solution)/shard_map/ppermute | solution.py:711
  114.1 4.1 %collective-permute-done.23 = bf16[8,128,128]{2,1,0:T(8,128)(2,1)S(1)} collective-permute-done((bf16[8,128,128]{2,1,0:T(8,128)(2,1)S(1)}, bf16[8,128,128]{2,1,0:T(8,128)(2,1)S(1)}, u32[]{:S(2)}, u32[]{:S(2)}) %collective-permute-start.23) | collective-permute-done | bytes 262176 | tf_op jit(solution)/shard_map/ppermute | solution.py:711
  119.2 2.0 %collective-permute-start.21 = (bf16[8,128,128]{2,1,0:T(8,128)(2,1)S(1)}, bf16[8,128,128]{2,1,0:T(8,128)(2,1)S(1)}, u32[]{:S(2)}, u32[]{:S(2)}) collective-permute-start(bf16[8,128,128]{2,1,0:T(8,128)(2,1)S(1)} %fusion), channel_id=1, source_target_pairs={{0,2},{2,0},{4,6},{6,4},{1,3},{3,1},{5,7},{7,5},{8,10},{10,8},{12,... | collective-permute-start | bytes 786440 | tf_op jit(solution)/shard_map/ppermute | solution.py:711
  121.2 8.3 %collective-permute-done.22 = bf16[16,128,128]{2,1,0:T(8,128)(2,1)S(1)} collective-permute-done((bf16[16,128,128]{2,1,0:T(8,128)(2,1)S(1)}, bf16[16,128,128]{2,1,0:T(8,128)(2,1)S(1)}, u32[]{:S(2)}, u32[]{:S(2)}) %collective-permute-start.22) | collective-permute-done | bytes 524320 | tf_op jit(solution)/shard_map/ppermute | solution.py:711
  129.5 4.8 %collective-permute-done.21.end_a = bf16[8,128,128]{2,1,0:T(8,128)(2,1)S(1)} collective-permute-done((bf16[8,128,128]{2,1,0:T(8,128)(2,1)S(1)}, bf16[8,128,128]{2,1,0:T(8,128)(2,1)S(1)}, u32[]{:S(2)}, u32[]{:S(2)}) %collective-permute-start.21) | collective-permute-done | bytes 262176 | tf_op jit(solution)/shard_map/ppermute | solution.py:711
  134.6 3.3 %collective-permute-start.28 = (bf16[16,128,128]{2,1,0:T(8,128)(2,1)S(1)}, bf16[16,128,128]{2,1,0:T(8,128)(2,1)S(1)}, u32[]{:S(2)}, u32[]{:S(2)}) collective-permute-start(bf16[16,128,128]{2,1,0:T(8,128)(2,1)S(1)} %add_convert_fusion.1), channel_id=1, source_target_pairs={{0,2},{2,0},{4,6},{6,4},{1,3},{3,1},{5,7},{7,5},{8,10},{10,8},{12,... | collective-permute-start | bytes 1572872 | tf_op jit(solution)/shard_map/ppermute | solution.py:711
  139.6 14.5 %collective-permute-done.27.rest_2_ = bf16[8,128,128]{2,1,0:T(8,128)(2,1)S(1)} collective-permute-done((bf16[8,128,128]{2,1,0:T(8,128)(2,1)S(1)}, bf16[8,128,128]{2,1,0:T(8,128)(2,1)S(1)}, u32[]{:S(2)}, u32[]{:S(2)}) %collective-permute-start.27) | collective-permute-done | bytes 262176 | tf_op jit(solution)/shard_map/ppermute | solution.py:711
  154.1 3.4 %final.1 = f32[64,2,4096]{2,1,0:T(2,128)} custom-call(s32[8]{0:T(128)S(1)} %concatenate.12.place, f32[8,128,128]{2,1,0:T(8,128)S(1)} %get-tuple-element.55.part_a, bf16[16,128,128]{2,1,0:T(8,128)(2,1)S(1)} %collective-permute-done.20.peer_a, bf16[8,128,128]{2,1,0:T(8,128)(2,1)S(1)} %collective-permute-done.21.end_a, ...), custom_call_target="tpu_custom_call" | custom-call | flops 2097152 | bytes 6291456 | tf_op jit(solution)/shard_map/final/pallas_call | solution.py:667
  (109 shorter events, 31.4 us)
Async XLA Ops:
  0.0 52.6 %copy-start = (bf16[1,2,128,512]{3,2,1,0:T(8,128)(2,1)S(1)}, bf16[1,2,128,512]{3,2,1,0:T(8,128)(2,1)}, u32[]{:S(2)}) copy-start(bf16[1,2,128,512]{3,2,1,0:T(8,128)(2,1)} %param.14) | copy-start | bytes 786436
  2.7 20.7 %collective-permute-start.2 = (bf16[24,128,128]{2,1,0:T(8,128)(2,1)S(1)}, bf16[24,128,128]{2,1,0:T(8,128)(2,1)}, u32[]{:S(2)}, u32[]{:S(2)}) collective-permute-start(bf16[24,128,128]{2,1,0:T(8,128)(2,1)S(1)} %bitcast.44), channel_id=1, source_target_pairs={{0,2},{2,0},{4,6},{6,4},{1,3},{3,1},{5,7},{7,5},{8,10},{10,8},{12,... | collective-permute-start | bytes 2359304 | tf_op jit(solution)/shard_map/ppermute | solution.py:711
  5.8 21.1 %collective-permute-start.1 = (bf16[24,128,128]{2,1,0:T(8,128)(2,1)S(1)}, bf16[24,128,128]{2,1,0:T(8,128)(2,1)S(1)}, u32[]{:S(2)}, u32[]{:S(2)}) collective-permute-start(bf16[24,128,128]{2,1,0:T(8,128)(2,1)S(1)} %bitcast.45), channel_id=1, source_target_pairs={{2,4},{4,2},{10,12},{12,10},{0,8},{8,0},{6,14},{14,6},{3,5},{5,3},... | collective-permute-start | bytes 2359304 | tf_op jit(solution)/shard_map/ppermute | solution.py:714
  11.1 14.7 %collective-permute-start = (bf16[2,1024,128]{2,1,0:T(8,128)(2,1)}, bf16[2,1024,128]{2,1,0:T(8,128)(2,1)}, u32[]{:S(2)}, u32[]{:S(2)}) collective-permute-start(bf16[2,1024,128]{2,1,0:T(8,128)(2,1)} %multiply_bitcast_fusion.1.own_a), channel_id=1, source_target_pairs={{0,1},{1,0},{2,3},{3,2},{4,5},{5,4},{6,7},{7,6},{8,9},{9,8},{10,11... | collective-permute-start | bytes 1572872 | tf_op jit(solution)/shard_map/ppermute | solution.py:727
  23.4 7.2 %collective-permute-start.5 = (bf16[24,128,128]{2,1,0:T(8,128)(2,1)}, bf16[24,128,128]{2,1,0:T(8,128)(2,1)}, u32[]{:S(2)}, u32[]{:S(2)}) collective-permute-start(bf16[24,128,128]{2,1,0:T(8,128)(2,1)} %collective-permute-done.2.slot1), channel_id=1, source_target_pairs={{2,4},{4,2},{10,12},{12,10},{0,8},{8,0},{6,14},{14,6},{3,5},{5,3},... | collective-permute-start | bytes 2359304 | tf_op jit(solution)/shard_map/ppermute | solution.py:714
  26.9 37.6 %collective-permute-start.4 = (bf16[2,3072,128]{2,1,0:T(8,128)(2,1)S(1)}, bf16[2,3072,128]{2,1,0:T(8,128)(2,1)}, u32[]{:S(2)}, u32[]{:S(2)}) collective-permute-start(bf16[2,3072,128]{2,1,0:T(8,128)(2,1)S(1)} %multiply_bitcast_fusion.own_k), channel_id=1, source_target_pairs={{0,1},{1,0},{2,3},{3,2},{4,5},{5,4},{6,7},{7,6},{8,9},{9,8},{10,11... | collective-permute-start | bytes 4718600 | tf_op jit(solution)/shard_map/ppermute | solution.py:733
  28.6 20.5 %collective-permute-start.3 = (bf16[24,128,128]{2,1,0:T(8,128)(2,1)S(1)}, bf16[24,128,128]{2,1,0:T(8,128)(2,1)S(1)}, u32[]{:S(2)}, u32[]{:S(2)}) collective-permute-start(bf16[24,128,128]{2,1,0:T(8,128)(2,1)S(1)} %broadcast_select_fusion.1), channel_id=1, source_target_pairs={{0,2},{2,0},{4,6},{6,4},{1,3},{3,1},{5,7},{7,5},{8,10},{10,8},{12,... | collective-permute-start | bytes 2359304 | tf_op jit(solution)/shard_map/ppermute | solution.py:711
  31.6 33.0 %collective-permute-start.6 = (bf16[24,128,128]{2,1,0:T(8,128)(2,1)}, bf16[24,128,128]{2,1,0:T(8,128)(2,1)}, u32[]{:S(2)}, u32[]{:S(2)}) collective-permute-start(bf16[24,128,128]{2,1,0:T(8,128)(2,1)} %broadcast_select_fusion), channel_id=1, source_target_pairs={{0,2},{2,0},{4,6},{6,4},{1,3},{3,1},{5,7},{7,5},{8,10},{10,8},{12,... | collective-permute-start | bytes 2359304 | tf_op jit(solution)/shard_map/ppermute | solution.py:711
  50.0 11.0 %collective-permute-start.7 = (bf16[16,128,128]{2,1,0:T(8,128)(2,1)}, bf16[16,128,128]{2,1,0:T(8,128)(2,1)}, u32[]{:S(2)}, u32[]{:S(2)}) collective-permute-start(bf16[16,128,128]{2,1,0:T(8,128)(2,1)} %pad_maximum_fusion.2), channel_id=1, source_target_pairs={{2,4},{4,2},{10,12},{12,10},{0,8},{8,0},{6,14},{14,6},{3,5},{5,3},... | collective-permute-start | bytes 1572872 | tf_op jit(solution)/shard_map/ppermute | solution.py:714
  69.8 1.6 %collective-permute-start.9 = (f32[2,2,2,32,256]{4,3,2,1,0:T(8,128)S(1)}, f32[2,2,2,32,256]{4,3,2,1,0:T(8,128)S(1)}, u32[]{:S(2)}, u32[]{:S(2)}) collective-permute-start(f32[2,2,2,32,256]{4,3,2,1,0:T(8,128)S(1)} %get-tuple-element.47), channel_id=1, source_target_pairs={{0,8},{8,0},{1,9},{9,1},{2,10},{10,2},{3,11},{11,3},{4,12},{12,4},... | collective-permute-start | bytes 786440 | tf_op jit(solution)/shard_map/ppermute | solution.py:750
  69.9 3.8 %collective-permute-start.8 = (f32[2,2,2,32,256]{4,3,2,1,0:T(8,128)S(1)}, f32[2,2,2,32,256]{4,3,2,1,0:T(8,128)S(1)}, u32[]{:S(2)}, u32[]{:S(2)}) collective-permute-start(f32[2,2,2,32,256]{4,3,2,1,0:T(8,128)S(1)} %get-tuple-element.45), channel_id=1, source_target_pairs={{0,8},{8,0},{1,9},{9,1},{2,10},{10,2},{3,11},{11,3},{4,12},{12,4},... | collective-permute-start | bytes 786440 | tf_op jit(solution)/shard_map/ppermute | solution.py:751
  71.4 6.0 %collective-permute-start.10 = (bf16[2,2,2,32,256]{4,3,2,1,0:T(8,128)(2,1)S(1)}, bf16[2,2,2,32,256]{4,3,2,1,0:T(8,128)(2,1)S(1)}, u32[]{:S(2)}, u32[]{:S(2)}) collective-permute-start(bf16[2,2,2,32,256]{4,3,2,1,0:T(8,128)(2,1)S(1)} %near_sum.1), channel_id=1, source_target_pairs={{0,2},{2,0},{4,6},{6,4},{1,3},{3,1},{5,7},{7,5},{8,10},{10,8},{12,... | collective-permute-start | bytes 393224 | tf_op jit(solution)/shard_map/ppermute | solution.py:711
  78.0 4.3 %collective-permute-start.11 = (f32[2,32,256]{2,1,0:T(8,128)S(1)}, f32[2,32,256]{2,1,0:T(8,128)S(1)}, u32[]{:S(2)}, u32[]{:S(2)}) collective-permute-start(f32[2,32,256]{2,1,0:T(8,128)S(1)} %get-tuple-element.49), channel_id=1, source_target_pairs={{0,16},{16,0},{1,17},{17,1},{2,18},{18,2},{3,19},{19,3},{4,20},{20... | collective-permute-start | bytes 196616 | tf_op jit(solution)/shard_map/ppermute | solution.py:753
  79.6 4.5 %collective-permute-start.12 = (f32[2,32,256]{2,1,0:T(8,128)S(1)}, f32[2,32,256]{2,1,0:T(8,128)S(1)}, u32[]{:S(2)}, u32[]{:S(2)}) collective-permute-start(f32[2,32,256]{2,1,0:T(8,128)S(1)} %get-tuple-element.50), channel_id=1, source_target_pairs={{0,1},{1,0},{2,3},{3,2},{4,5},{5,4},{6,7},{7,6},{8,9},{9,8},{10,11... | collective-permute-start | bytes 196616 | tf_op jit(solution)/shard_map/ppermute | solution.py:754
  80.1 5.2 %collective-permute-start.13 = (f32[2,32,256]{2,1,0:T(8,128)S(1)}, f32[2,32,256]{2,1,0:T(8,128)S(1)}, u32[]{:S(2)}, u32[]{:S(2)}) collective-permute-start(f32[2,32,256]{2,1,0:T(8,128)S(1)} %get-tuple-element.51), channel_id=1, source_target_pairs={{0,17},{1,16},{16,1},{17,0},{2,19},{3,18},{18,3},{19,2},{4,21},{5,... | collective-permute-start | bytes 196616 | tf_op jit(solution)/shard_map/ppermute | solution.py:755
  86.7 4.0 %collective-permute-start.15 = (bf16[2,32,256]{2,1,0:T(8,128)(2,1)S(1)}, bf16[2,32,256]{2,1,0:T(8,128)(2,1)S(1)}, u32[]{:S(2)}, u32[]{:S(2)}) collective-permute-start(bf16[2,32,256]{2,1,0:T(8,128)(2,1)S(1)} %get-tuple-element.52), channel_id=1, source_target_pairs={{0,16},{16,0},{1,17},{17,1},{2,18},{18,2},{3,19},{19,3},{4,20},{20... | collective-permute-start | bytes 98312 | tf_op jit(solution)/shard_map/ppermute | solution.py:757
  87.3 4.8 %collective-permute-start.16 = (bf16[2,32,256]{2,1,0:T(8,128)(2,1)S(1)}, bf16[2,32,256]{2,1,0:T(8,128)(2,1)S(1)}, u32[]{:S(2)}, u32[]{:S(2)}) collective-permute-start(bf16[2,32,256]{2,1,0:T(8,128)(2,1)S(1)} %get-tuple-element.53), channel_id=1, source_target_pairs={{0,17},{1,16},{16,1},{17,0},{2,19},{3,18},{18,3},{19,2},{4,21},{5,... | collective-permute-start | bytes 98312 | tf_op jit(solution)/shard_map/ppermute | solution.py:759
  89.7 3.9 %collective-permute-start.14 = (bf16[2,32,256]{2,1,0:T(8,128)(2,1)S(1)}, bf16[2,32,256]{2,1,0:T(8,128)(2,1)S(1)}, u32[]{:S(2)}, u32[]{:S(2)}) collective-permute-start(bf16[2,32,256]{2,1,0:T(8,128)(2,1)S(1)} %get-tuple-element.53), channel_id=1, source_target_pairs={{0,1},{1,0},{2,3},{3,2},{4,5},{5,4},{6,7},{7,6},{8,9},{9,8},{10,11... | collective-permute-start | bytes 98312 | tf_op jit(solution)/shard_map/ppermute | solution.py:758
  93.7 1.9 %collective-permute-start.17 = (bf16[2,2,2,32,256]{4,3,2,1,0:T(8,128)(2,1)S(1)}, bf16[2,2,2,32,256]{4,3,2,1,0:T(8,128)(2,1)S(1)}, u32[]{:S(2)}, u32[]{:S(2)}) collective-permute-start(bf16[2,2,2,32,256]{4,3,2,1,0:T(8,128)(2,1)S(1)} %pad_maximum_fusion.3.half), channel_id=1, source_target_pairs={{0,8},{8,0},{1,9},{9,1},{2,10},{10,2},{3,11},{11,3},{4,12},{12,4},... | collective-permute-start | bytes 393224 | tf_op jit(solution)/shard_map/ppermute | solution.py:761
  93.7 5.9 %collective-permute-start.18 = (bf16[2,2,2,32,256]{4,3,2,1,0:T(8,128)(2,1)S(1)}, bf16[2,2,2,32,256]{4,3,2,1,0:T(8,128)(2,1)S(1)}, u32[]{:S(2)}, u32[]{:S(2)}) collective-permute-start(bf16[2,2,2,32,256]{4,3,2,1,0:T(8,128)(2,1)S(1)} %pad_maximum_fusion.3.half), channel_id=1, source_target_pairs={{0,2},{2,0},{4,6},{6,4},{1,3},{3,1},{5,7},{7,5},{8,10},{10,8},{12,... | collective-permute-start | bytes 393224 | tf_op jit(solution)/shard_map/ppermute | solution.py:711
  97.8 20.6 %collective-permute-start.25 = (bf16[16,128,128]{2,1,0:T(8,128)(2,1)S(1)}, bf16[16,128,128]{2,1,0:T(8,128)(2,1)S(1)}, u32[]{:S(2)}, u32[]{:S(2)}) collective-permute-start(bf16[16,128,128]{2,1,0:T(8,128)(2,1)S(1)} %first_adjoint.2), channel_id=1, source_target_pairs={{0,2},{2,0},{4,6},{6,4},{1,3},{3,1},{5,7},{7,5},{8,10},{10,8},{12,... | collective-permute-start | bytes 1572872 | tf_op jit(solution)/shard_map/ppermute | solution.py:711
  99.7 3.4 %collective-permute-start.19 = (bf16[2,2,2,32,256]{4,3,2,1,0:T(8,128)(2,1)S(1)}, bf16[2,2,2,32,256]{4,3,2,1,0:T(8,128)(2,1)S(1)}, u32[]{:S(2)}, u32[]{:S(2)}) collective-permute-start(bf16[2,2,2,32,256]{4,3,2,1,0:T(8,128)(2,1)S(1)} %collective-permute-done.18.near_half), channel_id=1, source_target_pairs={{0,8},{8,0},{1,9},{9,1},{2,10},{10,2},{3,11},{11,3},{4,12},{12,4},... | collective-permute-start | bytes 393224 | tf_op jit(solution)/shard_map/ppermute | solution.py:772
  101.4 16.9 %collective-permute-start.23 = (bf16[8,128,128]{2,1,0:T(8,128)(2,1)S(1)}, bf16[8,128,128]{2,1,0:T(8,128)(2,1)S(1)}, u32[]{:S(2)}, u32[]{:S(2)}) collective-permute-start(bf16[8,128,128]{2,1,0:T(8,128)(2,1)S(1)} %first_adjoint.3), channel_id=1, source_target_pairs={{0,2},{2,0},{4,6},{6,4},{1,3},{3,1},{5,7},{7,5},{8,10},{10,8},{12,... | collective-permute-start | bytes 786440 | tf_op jit(solution)/shard_map/ppermute | solution.py:711
  104.6 14.5 %collective-permute-start.20 = (bf16[16,128,128]{2,1,0:T(8,128)(2,1)S(1)}, bf16[16,128,128]{2,1,0:T(8,128)(2,1)S(1)}, u32[]{:S(2)}, u32[]{:S(2)}) collective-permute-start(bf16[16,128,128]{2,1,0:T(8,128)(2,1)S(1)} %get-tuple-element.56), channel_id=1, source_target_pairs={{2,4},{4,2},{10,12},{12,10},{0,8},{8,0},{6,14},{14,6},{3,5},{5,3},... | collective-permute-start | bytes 1572872 | tf_op jit(solution)/shard_map/ppermute | solution.py:714
  110.9 18.6 %collective-permute-start.22 = (bf16[16,128,128]{2,1,0:T(8,128)(2,1)S(1)}, bf16[16,128,128]{2,1,0:T(8,128)(2,1)S(1)}, u32[]{:S(2)}, u32[]{:S(2)}) collective-permute-start(bf16[16,128,128]{2,1,0:T(8,128)(2,1)S(1)} %convert_element_type.60), channel_id=1, source_target_pairs={{0,2},{2,0},{4,6},{6,4},{1,3},{3,1},{5,7},{7,5},{8,10},{10,8},{12,... | collective-permute-start | bytes 1572872 | tf_op jit(solution)/shard_map/ppermute | solution.py:711
  118.3 2.9 %collective-permute-start.24 = (bf16[8,128,128]{2,1,0:T(8,128)(2,1)S(1)}, bf16[8,128,128]{2,1,0:T(8,128)(2,1)S(1)}, u32[]{:S(2)}, u32[]{:S(2)}) collective-permute-start(bf16[8,128,128]{2,1,0:T(8,128)(2,1)S(1)} %add_convert_fusion.5), channel_id=1, source_target_pairs={{2,4},{4,2},{10,12},{12,10},{0,8},{8,0},{6,14},{14,6},{3,5},{5,3},... | collective-permute-start | bytes 786440 | tf_op jit(solution)/shard_map/ppermute | solution.py:714
  118.5 15.8 %collective-permute-start.26 = (bf16[16,128,128]{2,1,0:T(8,128)(2,1)S(1)}, bf16[16,128,128]{2,1,0:T(8,128)(2,1)S(1)}, u32[]{:S(2)}, u32[]{:S(2)}) collective-permute-start(bf16[16,128,128]{2,1,0:T(8,128)(2,1)S(1)} %add_convert_fusion.2), channel_id=1, source_target_pairs={{2,4},{4,2},{10,12},{12,10},{0,8},{8,0},{6,14},{14,6},{3,5},{5,3},... | collective-permute-start | bytes 1572872 | tf_op jit(solution)/shard_map/ppermute | solution.py:714
  119.2 15.1 %collective-permute-start.21 = (bf16[8,128,128]{2,1,0:T(8,128)(2,1)S(1)}, bf16[8,128,128]{2,1,0:T(8,128)(2,1)S(1)}, u32[]{:S(2)}, u32[]{:S(2)}) collective-permute-start(bf16[8,128,128]{2,1,0:T(8,128)(2,1)S(1)} %fusion), channel_id=1, source_target_pairs={{0,2},{2,0},{4,6},{6,4},{1,3},{3,1},{5,7},{7,5},{8,10},{10,8},{12,... | collective-permute-start | bytes 786440 | tf_op jit(solution)/shard_map/ppermute | solution.py:711
  134.6 19.4 %collective-permute-start.28 = (bf16[16,128,128]{2,1,0:T(8,128)(2,1)S(1)}, bf16[16,128,128]{2,1,0:T(8,128)(2,1)S(1)}, u32[]{:S(2)}, u32[]{:S(2)}) collective-permute-start(bf16[16,128,128]{2,1,0:T(8,128)(2,1)S(1)} %add_convert_fusion.1), channel_id=1, source_target_pairs={{0,2},{2,0},{4,6},{6,4},{1,3},{3,1},{5,7},{7,5},{8,10},{10,8},{12,... | collective-permute-start | bytes 1572872 | tf_op jit(solution)/shard_map/ppermute | solution.py:711
  138.0 16.1 %collective-permute-start.30 = (bf16[16,128,128]{2,1,0:T(8,128)(2,1)S(1)}, bf16[16,128,128]{2,1,0:T(8,128)(2,1)S(1)}, u32[]{:S(2)}, u32[]{:S(2)}) collective-permute-start(bf16[16,128,128]{2,1,0:T(8,128)(2,1)S(1)} %add_convert_fusion), channel_id=1, source_target_pairs={{2,4},{4,2},{10,12},{12,10},{0,8},{8,0},{6,14},{14,6},{3,5},{5,3},... | collective-permute-start | bytes 1572872 | tf_op jit(solution)/shard_map/ppermute | solution.py:714
  138.1 16.0 %collective-permute-start.27 = (bf16[8,128,128]{2,1,0:T(8,128)(2,1)S(1)}, bf16[8,128,128]{2,1,0:T(8,128)(2,1)S(1)}, u32[]{:S(2)}, u32[]{:S(2)}) collective-permute-start(bf16[8,128,128]{2,1,0:T(8,128)(2,1)S(1)} %add_convert_fusion.4), channel_id=1, source_target_pairs={{0,2},{2,0},{4,6},{6,4},{1,3},{3,1},{5,7},{7,5},{8,10},{10,8},{12,... | collective-permute-start | bytes 786440 | tf_op jit(solution)/shard_map/ppermute | solution.py:711
  139.6 14.5 %collective-permute-start.29 = (bf16[8,128,128]{2,1,0:T(8,128)(2,1)S(1)}, bf16[8,128,128]{2,1,0:T(8,128)(2,1)S(1)}, u32[]{:S(2)}, u32[]{:S(2)}) collective-permute-start(bf16[8,128,128]{2,1,0:T(8,128)(2,1)S(1)} %add_convert_fusion.3), channel_id=1, source_target_pairs={{2,4},{4,2},{10,12},{12,10},{0,8},{8,0},{6,14},{14,6},{3,5},{5,3},... | collective-permute-start | bytes 786440 | tf_op jit(solution)/shard_map/ppermute | solution.py:714
  (15 other events, 227.1 us)

commit v5 on v4

--- a/solution.py
+++ b/solution.py
@@ -583,14 +583,16 @@
 
 
 def near_kernel(
-    place, half, other, near_half, near_other, own_a, far_a, near_k, near_far_k, send, part1, part0,
-    field
+    slots, place, half, other, near_half, near_other, own_a, far_a, near_k, near_far_k, *rest
 ):
+    field = rest[-1]
+
     @pl.when(place[0] == 1)
     def _():
-        field_rows(place, half, other, (3, 2, 1, 0), field, 0)
+        field_rows(place, half, other, slots, field, 0)
         rows = field.shape[0] // 2
-        field_rows(place, near_half, near_other, (3, 2, 0, 1), field, rows)
+        swapped = [(1, 0, 2, 3)[slot] for slot in slots]
+        field_rows(place, near_half, near_other, swapped, field, rows)
         tiles = near_k.shape[0] // 2
         cells = jnp.concatenate(
             [own_a[0], own_a[1], far_a[0], far_a[1]]
@@ -598,32 +600,34 @@
             axis=1,
         )
         sums = dot(cells, field[...])
-        outs = (send.at[pl.ds(0, tiles)], send.at[pl.ds(tiles, tiles)], part1, part0)
+        outs = rest[:-1]
+        if len(outs) == 1:
+            outs = (outs[0].at[pl.ds(0, tiles)], outs[0].at[pl.ds(tiles, tiles)])
         for i, out in enumerate(outs):
             store_tiles(sums, i, out)
 
 
-def near_adjoint(place, half, other, near_half, near_other, own_a, far_a, r2, r3):
+def near_adjoint(place, half, other, near_half, near_other, own_a, far_a, r2, r3, slots, dtype):
     base = own_a.shape[2]
     tiles = own_a.shape[1] // LANES
     rows = half.shape[4] // 2
     whole = lambda a: pl.BlockSpec(a.shape, lambda i: (0,) * a.ndim)
     two = pl.BlockSpec((2 * tiles, LANES, rows), lambda i: (0, 0, 0))
     one = pl.BlockSpec((tiles, LANES, rows), lambda i: (0, 0, 0))
-    types = ((2, jnp.bfloat16), (1, jnp.float32), (1, jnp.float32))
+    counts = (2,) if dtype == jnp.bfloat16 else (1, 1)
     return pl.pallas_call(
-        near_kernel,
+        functools.partial(near_kernel, slots),
         grid=(1,),
         in_specs=[pl.BlockSpec(memory_space=pltpu.SMEM)]
         + [whole(a) for a in (half, other, near_half, near_other, own_a, far_a)]
         + [two, two],
-        out_specs=[two, one, one],
-        out_shape=[jax.ShapeDtypeStruct((n * tiles, LANES, rows), t) for n, t in types],
-        scratch_shapes=[pltpu.VMEM((8 * base, rows * 4), jnp.bfloat16)],
+        out_specs=[two if n == 2 else one for n in counts],
+        out_shape=[jax.ShapeDtypeStruct((n * tiles, LANES, rows), dtype) for n in counts],
+        scratch_shapes=[pltpu.VMEM((8 * base, rows * 2), jnp.bfloat16)],
         compiler_params=pltpu.CompilerParams(vmem_limit_bytes=VMEM_LIMIT),
         cost_estimate=cost(
-            flops=64 * rows * tiles * LANES * base,
-            bytes_accessed=6 * 2**20,
+            flops=32 * rows * tiles * LANES * base,
+            bytes_accessed=5 * 2**20,
             transcendentals=0,
             times=20,
         ),
@@ -631,51 +635,59 @@
     )(place, half, other, near_half, near_other, own_a, far_a, r2, r3)
 
 
-def final_kernel(place, part_a, peer_a, end_a, *rest):
-    part_b, near_b, far_b = (rest[2 * i : 2 * i + 2] for i in range(3))
-    out = rest[-1]
-    step = pl.program_id(0)
-    is_mid = place[0] == 1
+def store_rows(out, value):
     local = out.shape[0]
-
-    def store(value):
-        for t in range(value.shape[0]):
-            lanes = slice(t * LANES, (t + 1) * LANES)
-            out[:, 0, lanes] = value[t][:local]
-            out[:, 1, lanes] = value[t][local:]
-
-    @pl.when(step == 0)
-    def _():
-        mid = part_a[...] + peer_a[...].astype(jnp.float32)
-        store(jnp.where(is_mid, mid, end_a[...].astype(jnp.float32)))
-
-    @pl.when(step > 0)
-    def _():
-        def piece(parts):
-            return jnp.where(step == 1, parts[0][...], parts[1][...]).astype(jnp.float32)
-
-        store(piece(part_b) + piece(near_b) + jnp.where(is_mid, piece(far_b), 0.0))
+    for t in range(value.shape[0]):
+        lanes = slice(t * LANES, (t + 1) * LANES)
+        out[:, 0, lanes] = value[t][:local]
+        out[:, 1, lanes] = value[t][local:]
+
+
+def final_a_kernel(place, part_a, peer_a, end_a, out):
+    mid = part_a[...] + peer_a[...].astype(jnp.float32)
+    store_rows(out, jnp.where(place[0] == 1, mid, end_a[...].astype(jnp.float32)))
+
+
+def final_b_kernel(place, part, near, far, before, out):
+    value = part[...] + near[...].astype(jnp.float32)
+    store_rows(out, value + jnp.where(place[0] == 1, far[...].astype(jnp.float32), 0.0))
 
 
 def final(place, part_a, peer_a, end_a, part_b, near_b, far_b):
-    tiles, _, rows = part_a.shape
-    count = 4 * tiles
-    shape = (tiles, LANES, rows)
+    tiles, rows, _ = part_a.shape
+    shape = (tiles, rows, LANES)
+    smem = pl.BlockSpec(memory_space=pltpu.SMEM)
     one = pl.BlockSpec(shape, lambda i: (0, 0, 0))
     second = pl.BlockSpec(shape, lambda i: (1, 0, 0))
-    rest = pl.BlockSpec(shape, lambda i: (jnp.maximum(i - 2, 0), 0, 0))
-    return pl.pallas_call(
-        final_kernel,
-        grid=(4,),
-        in_specs=[pl.BlockSpec(memory_space=pltpu.SMEM), one, second, one] + [one, rest] * 3,
-        out_specs=pl.BlockSpec((rows // 2, 2, tiles * LANES), lambda i: (0, 0, i)),
-        out_shape=jax.ShapeDtypeStruct((rows // 2, 2, count * LANES), jnp.float32),
-        compiler_params=pltpu.CompilerParams(vmem_limit_bytes=VMEM_LIMIT),
-        cost_estimate=cost(
-            flops=4 * rows * count * LANES, bytes_accessed=6 * 2**20, transcendentals=0
-        ),
-        name="final",
-    )(place, part_a, peer_a, end_a, *part_b, *near_b, *far_b)
+    block = (rows // 2, 2, tiles * LANES)
+    whole = jax.ShapeDtypeStruct((rows // 2, 2, 4 * tiles * LANES), jnp.float32)
+    params = pltpu.CompilerParams(vmem_limit_bytes=VMEM_LIMIT)
+    done = pl.pallas_call(
+        final_a_kernel,
+        grid=(1,),
+        in_specs=[smem, one, second, one],
+        out_specs=pl.BlockSpec(block, lambda i: (0, 0, 0)),
+        out_shape=whole,
+        compiler_params=params,
+        cost_estimate=cost(flops=2 * rows * tiles * LANES, bytes_accessed=2**20, transcendentals=0),
+        name="final_a",
+    )(place, part_a, peer_a, end_a)
+    for piece, begin, steps in ((1, 2, 2), (0, 1, 1)):
+        each = pl.BlockSpec(shape, lambda i: (i, 0, 0))
+        done = pl.pallas_call(
+            final_b_kernel,
+            grid=(steps,),
+            in_specs=[smem, each, each, each, pl.BlockSpec(memory_space=pl.ANY)],
+            out_specs=pl.BlockSpec(block, functools.partial(lambda start, i: (0, 0, i + start), begin)),
+            out_shape=whole,
+            input_output_aliases={4: 0},
+            compiler_params=params,
+            cost_estimate=cost(
+                flops=3 * steps * rows * tiles * LANES, bytes_accessed=2**20 * steps, transcendentals=0
+            ),
+            name="final_b",
+        )(place, part_b[piece], near_b[piece], far_b[piece], done)
+    return done
 
 
 def table_parts(length):
@@ -770,11 +782,11 @@
     g1 = ends(*send3)
     near_half, _ = lax.optimization_barrier((near_half, send3[1]))
     near_other = lax.ppermute(near_half, "tl", SWAP)
-    send_a, part1_a, part0_a = near_adjoint(
-        place, half, other, near_half, near_other, own_a, far_a, r2, r3
-    )
+    near_args = (half, other, near_half, near_other, own_a, far_a, r2, r3)
+    (send_a,) = near_adjoint(place, *near_args, (3, 2), low)
     (peer_a,) = mids(send_a)
     half, send_a = lax.optimization_barrier((half, send_a))
+    part1_a, part0_a = near_adjoint(place, half, *near_args[1:], (1, 0), jnp.float32)
     part3, part2, part1, part0 = adjoint(
         place, half, other, own_b, far_b, (3, 2, 1, 0), jnp.float32
     )

time: 158 us -> 156 us (0.987)
  waiting for transfers between devices: 64.8 us -> 60.3 us
  Pallas kernels: 24.8 us -> 28.1 us
    ppermute x11, waiting for transfers between devices: 54.5 us -> 50.1 us  [ends(): return [lax.ppermute(value, 'outer', ENDS) for value in values]]
    pallas_call x2 -> x5, Pallas kernels: 4.93 us -> 8.16 us  [the longest x2 3.74 us: final(): pl.pallas_call(final_b_kernel, grid=(steps,), in_specs=[smem, each, each,...]
  transfers between devices with their start and end apart: 31 -> 31, of which waited for: 17 -> 18; matrix products, arithmetic and copies ran while one was open for 10% -> 10% of each run, Pallas kernels for 9% -> 12%
where the time goes in v5:
time: 156 us
  waiting for transfers between devices  60.3 us (39%)
  starting transfers between devices  46.7 us (30%)
  Pallas kernels  28.1 us (18%)
  local copies, waits for them, and re-layouts  10.7 us (7%)
  other arithmetic  8.72 us (6%)
    ppermute x11, waiting for transfers between devices, ends(): return [lax.ppermute(value, 'outer', ENDS) for value in values]  50.1 us
    ppermute x11, starting transfers between devices, ends(): return [lax.ppermute(value, 'outer', ENDS) for value in values]  34.9 us
    pallas_call x1, Pallas kernels, adjoint(): pl.pallas_call(functools.partial(adjoint_kernel, slots, ends_only), grid=...  5.88 us
    pallas_call x1, Pallas kernels, late(): pl.pallas_call(late_kernel, grid=(4,), in_specs=[pl.BlockSpec(memory_spac...  5.27 us
    pallas_call x2, Pallas kernels, first_adjoint(): pl.pallas_call(functools.partial(first_kernel, slot), grid=(steps,), in_s...  3.94 us
    pallas_call x2, Pallas kernels, final(): pl.pallas_call(final_b_kernel, grid=(steps,), in_specs=[smem, each, each,...  3.74 us
  transfers between devices with their start and end apart: 31, of which 18 were waited for; matrix products, arithmetic and copies ran while one was open for 10% of the time, Pallas kernels for 12%

profile of v5, /device:TPU:0, one launch (start us, length us, event | category | flops | bytes accessed | tf_op | source)
XLA Modules:
  0.0 155.5 jit_solution(14111673069654264723)
XLA Ops:
  0.0 1.9 %reshape_squeeze.3 = bf16[64,2,32,128]{3,2,1,0:T(8,128)(2,1)S(1)} reshape(bf16[1,64,2,4096]{3,2,1,0:T(2,128)(2,1)} %param.12) | data formatting | bytes 2097152 | tf_op jit(solution)/shard_map/reshape;squeeze | solution.py:719
  2.7 3.1 %collective-permute-start.2 = (bf16[24,128,128]{2,1,0:T(8,128)(2,1)S(1)}, bf16[24,128,128]{2,1,0:T(8,128)(2,1)}, u32[]{:S(2)}, u32[]{:S(2)}) collective-permute-start(bf16[24,128,128]{2,1,0:T(8,128)(2,1)S(1)} %bitcast.44), channel_id=1, source_target_pairs={{0,2},{2,0},{4,6},{6,4},{1,3},{3,1},{5,7},{7,5},{8,10},{10,8},{12,... | collective-permute-start | bytes 2359304 | tf_op jit(solution)/shard_map/ppermute | solution.py:723
  7.0 2.1 %multiply_bitcast_fusion.1.own_a = bf16[2,1024,128]{2,1,0:T(8,128)(2,1)} fusion(bf16[1,1,2,4096,128]{4,3,2,1,0:T(8,128)(2,1)} %param.13, bf16[]{:T(256)S(6)} %convert_element_type.55), kind=kLoop, calls=%fused_computation.15 | loop fusion | flops 262144 | bytes 1048578 | tf_op jit(solution)/shard_map/mul | solution.py:735
  9.1 2.0 %pad_maximum_fusion.1 = bf16[24,128,128]{2,1,0:T(8,128)(2,1)} fusion(bf16[8,128,128]{2,1,0:T(8,128)(2,1)S(1)} %bitcast.48, bf16[16,128,128]{2,1,0:T(8,128)(2,1)} %bitcast.8), kind=kLoop, calls=%fused_computation.7 | loop fusion | flops 393216 | bytes 1572864 | tf_op jit(solution)/shard_map/concatenate | solution.py:737
  12.6 10.9 %collective-permute-done.2.slot1 = bf16[24,128,128]{2,1,0:T(8,128)(2,1)} collective-permute-done((bf16[24,128,128]{2,1,0:T(8,128)(2,1)S(1)}, bf16[24,128,128]{2,1,0:T(8,128)(2,1)}, u32[]{:S(2)}, u32[]{:S(2)}) %collective-permute-start.2) | collective-permute-done | bytes 786464 | tf_op jit(solution)/shard_map/ppermute | solution.py:723
  23.6 2.1 %collective-permute-done.far_a = bf16[2,1024,128]{2,1,0:T(8,128)(2,1)} collective-permute-done((bf16[2,1024,128]{2,1,0:T(8,128)(2,1)}, bf16[2,1024,128]{2,1,0:T(8,128)(2,1)}, u32[]{:S(2)}, u32[]{:S(2)}) %collective-permute-start) | collective-permute-done | bytes 524320 | tf_op jit(solution)/shard_map/ppermute | solution.py:739
  26.9 1.6 %collective-permute-start.4 = (bf16[2,3072,128]{2,1,0:T(8,128)(2,1)S(1)}, bf16[2,3072,128]{2,1,0:T(8,128)(2,1)}, u32[]{:S(2)}, u32[]{:S(2)}) collective-permute-start(bf16[2,3072,128]{2,1,0:T(8,128)(2,1)S(1)} %multiply_bitcast_fusion.own_k), channel_id=1, source_target_pairs={{0,1},{1,0},{2,3},{3,2},{4,5},{5,4},{6,7},{7,6},{8,9},{9,8},{10,11... | collective-permute-start | bytes 4718600 | tf_op jit(solution)/shard_map/ppermute | solution.py:745
  28.6 2.0 %collective-permute-start.3 = (bf16[24,128,128]{2,1,0:T(8,128)(2,1)S(1)}, bf16[24,128,128]{2,1,0:T(8,128)(2,1)S(1)}, u32[]{:S(2)}, u32[]{:S(2)}) collective-permute-start(bf16[24,128,128]{2,1,0:T(8,128)(2,1)S(1)} %broadcast_select_fusion.1), channel_id=1, source_target_pairs={{0,2},{2,0},{4,6},{6,4},{1,3},{3,1},{5,7},{7,5},{8,10},{10,8},{12,... | collective-permute-start | bytes 2359304 | tf_op jit(solution)/shard_map/ppermute | solution.py:723
  31.6 14.4 %collective-permute-start.6 = (bf16[24,128,128]{2,1,0:T(8,128)(2,1)}, bf16[24,128,128]{2,1,0:T(8,128)(2,1)}, u32[]{:S(2)}, u32[]{:S(2)}) collective-permute-start(bf16[24,128,128]{2,1,0:T(8,128)(2,1)} %broadcast_select_fusion), channel_id=1, source_target_pairs={{0,2},{2,0},{4,6},{6,4},{1,3},{3,1},{5,7},{7,5},{8,10},{10,8},{12,... | collective-permute-start | bytes 2359304 | tf_op jit(solution)/shard_map/ppermute | solution.py:723
  46.0 3.1 %collective-permute-done.3.end2.near_sky.near_k = bf16[24,128,128]{2,1,0:T(8,128)(2,1)S(1)} collective-permute-done((bf16[24,128,128]{2,1,0:T(8,128)(2,1)S(1)}, bf16[24,128,128]{2,1,0:T(8,128)(2,1)S(1)}, u32[]{:S(2)}, u32[]{:S(2)}) %collective-permute-start.3) | collective-permute-done | bytes 786464 | tf_op jit(solution)/shard_map/ppermute | solution.py:723
  58.1 2.8 %early.1.done = f32[384,256]{1,0:T(8,128)S(1)} custom-call(s32[8]{0:T(128)S(1)} %concatenate.12.place, bf16[2,3072,128]{2,1,0:T(8,128)(2,1)S(1)} %multiply_bitcast_fusion.own_k, bf16[24,128,128]{2,1,0:T(8,128)(2,1)S(1)} %bitcast.46, bf16[24,128,128]{2,1,0:T(8,128)(2,1)} %collective-permute-done.2.slot1, ...), custom_call_target="tpu_custom_call" | custom-call | flops 603979776 | bytes 4194304 | tf_op jit(solution)/shard_map/early/pallas_call | solution.py:216
  61.0 3.5 %collective-permute-done.6.end3.near_far_k = bf16[24,128,128]{2,1,0:T(8,128)(2,1)} collective-permute-done((bf16[24,128,128]{2,1,0:T(8,128)(2,1)}, bf16[24,128,128]{2,1,0:T(8,128)(2,1)}, u32[]{:S(2)}, u32[]{:S(2)}) %collective-permute-start.6) | collective-permute-done | bytes 786464 | tf_op jit(solution)/shard_map/ppermute | solution.py:723
  64.5 5.3 %late.1 = (f32[2,2,2,32,256]{4,3,2,1,0:T(8,128)S(1)}, f32[2,2,2,32,256]{4,3,2,1,0:T(8,128)S(1)}, f32[2,2,2,32,256]{4,3,2,1,0:T(8,128)S(1)}, f32[2,2,2,32,256]{4,3,2,1,0:T(8,128)S(1)}) custom-call(s32[8]{0:T(128)S(1)} %concatenate.12.place, f32[384,256]{1,0:T(8,128)S(1)} %early.1.done, bf16[2,3072,128]{2,1,0:T(8,128)(2,1)S(1)} %multiply_bitcast_fusion.own_k, ...), custom_call_target="tpu_custom_call" | custom-call | flops 1006632960 | bytes 9437184 | tf_op jit(solution)/shard_map/late/pallas_call | solution.py:311
  71.4 2.2 %collective-permute-start.10 = (bf16[2,2,2,32,256]{4,3,2,1,0:T(8,128)(2,1)S(1)}, bf16[2,2,2,32,256]{4,3,2,1,0:T(8,128)(2,1)S(1)}, u32[]{:S(2)}, u32[]{:S(2)}) collective-permute-start(bf16[2,2,2,32,256]{4,3,2,1,0:T(8,128)(2,1)S(1)} %near_sum.1), channel_id=1, source_target_pairs={{0,2},{2,0},{4,6},{6,4},{1,3},{3,1},{5,7},{7,5},{8,10},{10,8},{12,... | collective-permute-start | bytes 393224 | tf_op jit(solution)/shard_map/ppermute | solution.py:723
  73.7 3.8 %collective-permute-done.10.near = bf16[2,2,2,32,256]{4,3,2,1,0:T(8,128)(2,1)S(1)} collective-permute-done((bf16[2,2,2,32,256]{4,3,2,1,0:T(8,128)(2,1)S(1)}, bf16[2,2,2,32,256]{4,3,2,1,0:T(8,128)(2,1)S(1)}, u32[]{:S(2)}, u32[]{:S(2)}) %collective-permute-start.10) | collective-permute-done | bytes 131104 | tf_op jit(solution)/shard_map/ppermute | solution.py:723
  82.4 1.7 %collective-permute-done.12.from_y = f32[2,32,256]{2,1,0:T(8,128)S(1)} collective-permute-done((f32[2,32,256]{2,1,0:T(8,128)S(1)}, f32[2,32,256]{2,1,0:T(8,128)S(1)}, u32[]{:S(2)}, u32[]{:S(2)}) %collective-permute-start.12) | collective-permute-done | bytes 65568 | tf_op jit(solution)/shard_map/ppermute | solution.py:766
  87.3 2.4 %collective-permute-start.16 = (bf16[2,32,256]{2,1,0:T(8,128)(2,1)S(1)}, bf16[2,32,256]{2,1,0:T(8,128)(2,1)S(1)}, u32[]{:S(2)}, u32[]{:S(2)}) collective-permute-start(bf16[2,32,256]{2,1,0:T(8,128)(2,1)S(1)} %get-tuple-element.52), channel_id=1, source_target_pairs={{0,17},{1,16},{16,1},{17,0},{2,19},{3,18},{18,3},{19,2},{4,21},{5,... | collective-permute-start | bytes 98312 | tf_op jit(solution)/shard_map/ppermute | solution.py:771
  93.8 1.8 %collective-permute-start.18 = (bf16[2,2,2,32,256]{4,3,2,1,0:T(8,128)(2,1)S(1)}, bf16[2,2,2,32,256]{4,3,2,1,0:T(8,128)(2,1)S(1)}, u32[]{:S(2)}, u32[]{:S(2)}) collective-permute-start(bf16[2,2,2,32,256]{4,3,2,1,0:T(8,128)(2,1)S(1)} %pad_maximum_fusion.3.half), channel_id=1, source_target_pairs={{0,2},{2,0},{4,6},{6,4},{1,3},{3,1},{5,7},{7,5},{8,10},{10,8},{12,... | collective-permute-start | bytes 393224 | tf_op jit(solution)/shard_map/ppermute | solution.py:723
  95.6 2.3 %first_adjoint.2 = bf16[16,128,128]{2,1,0:T(8,128)(2,1)S(1)} custom-call(s32[8]{0:T(128)S(1)} %concatenate.12.place, bf16[2,2,2,32,256]{4,3,2,1,0:T(8,128)(2,1)S(1)} %pad_maximum_fusion.3.half, bf16[2,2,2,32,256]{4,3,2,1,0:T(8,128)(2,1)S(1)} %collective-permute-done.17.other, bf16[2,3072,128]{2,1,0:T(8,128)(2,1)S(1)} %multiply_bitcast_fusion.own_k, ...), custom_call_target="tpu_custom_call" | custom-call | flops 5368709120 | bytes 83886080 | tf_op jit(solution)/shard_map/first_adjoint/pallas_call | solution.py:567
  99.7 1.7 %first_adjoint.3 = bf16[8,128,128]{2,1,0:T(8,128)(2,1)S(1)} custom-call(s32[8]{0:T(128)S(1)} %concatenate.12.place, bf16[2,2,2,32,256]{4,3,2,1,0:T(8,128)(2,1)S(1)} %pad_maximum_fusion.3.half, bf16[2,2,2,32,256]{4,3,2,1,0:T(8,128)(2,1)S(1)} %collective-permute-done.17.other, bf16[2,3072,128]{2,1,0:T(8,128)(2,1)S(1)} %multiply_bitcast_fusion.own_k, ...), custom_call_target="tpu_custom_call" | custom-call | flops 2684354560 | bytes 41943040 | tf_op jit(solution)/shard_map/first_adjoint/pallas_call | solution.py:567
  101.4 1.7 %collective-permute-start.23 = (bf16[8,128,128]{2,1,0:T(8,128)(2,1)S(1)}, bf16[8,128,128]{2,1,0:T(8,128)(2,1)S(1)}, u32[]{:S(2)}, u32[]{:S(2)}) collective-permute-start(bf16[8,128,128]{2,1,0:T(8,128)(2,1)S(1)} %first_adjoint.3), channel_id=1, source_target_pairs={{0,2},{2,0},{4,6},{6,4},{1,3},{3,1},{5,7},{7,5},{8,10},{10,8},{12,... | collective-permute-start | bytes 786440 | tf_op jit(solution)/shard_map/ppermute | solution.py:723
  104.7 5.9 %adjoint.1 = (f32[8,128,128]{2,1,0:T(8,128)S(1)}, f32[16,128,128]{2,1,0:T(8,128)S(1)}, f32[8,128,128]{2,1,0:T(8,128)S(1)}, f32[16,128,128]{2,1,0:T(8,128)S(1)}, ...) custom-call(s32[8]{0:T(128)S(1)} %concatenate.12.place, ...), custom_call_target="tpu_custom_call" | custom-call | flops 32212254720 | bytes 251658240 | tf_op jit(solution)/shard_map/adjoint/pallas_call | solution.py:525
  110.7 2.6 %collective-permute-start.22 = (bf16[16,128,128]{2,1,0:T(8,128)(2,1)S(1)}, bf16[16,128,128]{2,1,0:T(8,128)(2,1)S(1)}, u32[]{:S(2)}, u32[]{:S(2)}) collective-permute-start(bf16[16,128,128]{2,1,0:T(8,128)(2,1)S(1)} %convert_element_type.60), channel_id=1, source_target_pairs={{0,2},{2,0},{4,6},{6,4},{1,3},{3,1},{5,7},{7,5},{8,10},{10,8},{12,... | collective-permute-start | bytes 1572872 | tf_op jit(solution)/shard_map/ppermute | solution.py:723
  114.7 3.6 %collective-permute-done.23 = bf16[8,128,128]{2,1,0:T(8,128)(2,1)S(1)} collective-permute-done((bf16[8,128,128]{2,1,0:T(8,128)(2,1)S(1)}, bf16[8,128,128]{2,1,0:T(8,128)(2,1)S(1)}, u32[]{:S(2)}, u32[]{:S(2)}) %collective-permute-start.23) | collective-permute-done | bytes 262176 | tf_op jit(solution)/shard_map/ppermute | solution.py:723
  119.2 2.0 %collective-permute-start.21 = (bf16[8,128,128]{2,1,0:T(8,128)(2,1)S(1)}, bf16[8,128,128]{2,1,0:T(8,128)(2,1)S(1)}, u32[]{:S(2)}, u32[]{:S(2)}) collective-permute-start(bf16[8,128,128]{2,1,0:T(8,128)(2,1)S(1)} %fusion), channel_id=1, source_target_pairs={{0,2},{2,0},{4,6},{6,4},{1,3},{3,1},{5,7},{7,5},{8,10},{10,8},{12,... | collective-permute-start | bytes 786440 | tf_op jit(solution)/shard_map/ppermute | solution.py:723
  121.2 8.3 %collective-permute-done.22 = bf16[16,128,128]{2,1,0:T(8,128)(2,1)S(1)} collective-permute-done((bf16[16,128,128]{2,1,0:T(8,128)(2,1)S(1)}, bf16[16,128,128]{2,1,0:T(8,128)(2,1)S(1)}, u32[]{:S(2)}, u32[]{:S(2)}) %collective-permute-start.22) | collective-permute-done | bytes 524320 | tf_op jit(solution)/shard_map/ppermute | solution.py:723
  129.5 4.8 %collective-permute-done.21.end_a = bf16[8,128,128]{2,1,0:T(8,128)(2,1)S(1)} collective-permute-done((bf16[8,128,128]{2,1,0:T(8,128)(2,1)S(1)}, bf16[8,128,128]{2,1,0:T(8,128)(2,1)S(1)}, u32[]{:S(2)}, u32[]{:S(2)}) %collective-permute-start.21) | collective-permute-done | bytes 262176 | tf_op jit(solution)/shard_map/ppermute | solution.py:723
  134.7 3.2 %collective-permute-start.29 = (bf16[16,128,128]{2,1,0:T(8,128)(2,1)S(1)}, bf16[16,128,128]{2,1,0:T(8,128)(2,1)S(1)}, u32[]{:S(2)}, u32[]{:S(2)}) collective-permute-start(bf16[16,128,128]{2,1,0:T(8,128)(2,1)S(1)} %add_convert_fusion.1), channel_id=1, source_target_pairs={{0,2},{2,0},{4,6},{6,4},{1,3},{3,1},{5,7},{7,5},{8,10},{10,8},{12,... | collective-permute-start | bytes 1572872 | tf_op jit(solution)/shard_map/ppermute | solution.py:723
  139.5 1.7 %final_a.1.before = f32[64,2,4096]{2,1,0:T(2,128)} custom-call(s32[8]{0:T(128)S(1)} %concatenate.12.place, f32[8,128,128]{2,1,0:T(8,128)S(1)} %get-tuple-element.68.part_a, bf16[16,128,128]{2,1,0:T(8,128)(2,1)S(1)} %collective-permute-done.20.peer_a, bf16[8,128,128]{2,1,0:T(8,128)(2,1)S(1)} %collective-permute-done.21.end_a), custom_call_target="tpu_custom_call" | custom-call | flops 262144 | bytes 1048576 | tf_op jit(solution)/shard_map/final_a/pallas_call | solution.py:665
  141.2 9.5 %collective-permute-done.29.near = bf16[16,128,128]{2,1,0:T(8,128)(2,1)S(1)} collective-permute-done((bf16[16,128,128]{2,1,0:T(8,128)(2,1)S(1)}, bf16[16,128,128]{2,1,0:T(8,128)(2,1)S(1)}, u32[]{:S(2)}, u32[]{:S(2)}) %collective-permute-start.29) | collective-permute-done | bytes 524320 | tf_op jit(solution)/shard_map/ppermute | solution.py:723
  150.7 2.1 %final_b.2.before = f32[64,2,4096]{2,1,0:T(2,128)} custom-call(s32[8]{0:T(128)S(1)} %concatenate.12.place, f32[16,128,128]{2,1,0:T(8,128)S(1)} %get-tuple-element.64.part, bf16[16,128,128]{2,1,0:T(8,128)(2,1)S(1)} %collective-permute-done.29.near, bf16[16,128,128]{2,1,0:T(8,128)(2,1)S(1)} %collective-permute-done.30.far, ...), custom_call_target="tpu_custom_call", output_to_operand_aliasing={{}: (4, {})} | custom-call | flops 786432 | bytes 2097152 | tf_op jit(solution)/shard_map/final_b/pallas_call | solution.py:677
  153.9 1.7 %final_b.3 = f32[64,2,4096]{2,1,0:T(2,128)} custom-call(s32[8]{0:T(128)S(1)} %concatenate.12.place, f32[8,128,128]{2,1,0:T(8,128)S(1)} %get-tuple-element.55.part, bf16[8,128,128]{2,1,0:T(8,128)(2,1)S(1)} %collective-permute-done.27.near, bf16[8,128,128]{2,1,0:T(8,128)(2,1)S(1)} %collective-permute-done.28.far, ...), custom_call_target="tpu_custom_call", output_to_operand_aliasing={{}: (4, {})} | custom-call | flops 393216 | bytes 1048576 | tf_op jit(solution)/shard_map/final_b/pallas_call | solution.py:677
  (112 shorter events, 36.9 us)
Async XLA Ops:
  0.0 52.6 %copy-start = (bf16[1,2,128,512]{3,2,1,0:T(8,128)(2,1)S(1)}, bf16[1,2,128,512]{3,2,1,0:T(8,128)(2,1)}, u32[]{:S(2)}) copy-start(bf16[1,2,128,512]{3,2,1,0:T(8,128)(2,1)} %param.14) | copy-start | bytes 786436
  2.7 20.7 %collective-permute-start.2 = (bf16[24,128,128]{2,1,0:T(8,128)(2,1)S(1)}, bf16[24,128,128]{2,1,0:T(8,128)(2,1)}, u32[]{:S(2)}, u32[]{:S(2)}) collective-permute-start(bf16[24,128,128]{2,1,0:T(8,128)(2,1)S(1)} %bitcast.44), channel_id=1, source_target_pairs={{0,2},{2,0},{4,6},{6,4},{1,3},{3,1},{5,7},{7,5},{8,10},{10,8},{12,... | collective-permute-start | bytes 2359304 | tf_op jit(solution)/shard_map/ppermute | solution.py:723
  5.8 21.1 %collective-permute-start.1 = (bf16[24,128,128]{2,1,0:T(8,128)(2,1)S(1)}, bf16[24,128,128]{2,1,0:T(8,128)(2,1)S(1)}, u32[]{:S(2)}, u32[]{:S(2)}) collective-permute-start(bf16[24,128,128]{2,1,0:T(8,128)(2,1)S(1)} %bitcast.45), channel_id=1, source_target_pairs={{2,4},{4,2},{10,12},{12,10},{0,8},{8,0},{6,14},{14,6},{3,5},{5,3},... | collective-permute-start | bytes 2359304 | tf_op jit(solution)/shard_map/ppermute | solution.py:726
  11.1 14.7 %collective-permute-start = (bf16[2,1024,128]{2,1,0:T(8,128)(2,1)}, bf16[2,1024,128]{2,1,0:T(8,128)(2,1)}, u32[]{:S(2)}, u32[]{:S(2)}) collective-permute-start(bf16[2,1024,128]{2,1,0:T(8,128)(2,1)} %multiply_bitcast_fusion.1.own_a), channel_id=1, source_target_pairs={{0,1},{1,0},{2,3},{3,2},{4,5},{5,4},{6,7},{7,6},{8,9},{9,8},{10,11... | collective-permute-start | bytes 1572872 | tf_op jit(solution)/shard_map/ppermute | solution.py:739
  23.4 7.2 %collective-permute-start.5 = (bf16[24,128,128]{2,1,0:T(8,128)(2,1)}, bf16[24,128,128]{2,1,0:T(8,128)(2,1)}, u32[]{:S(2)}, u32[]{:S(2)}) collective-permute-start(bf16[24,128,128]{2,1,0:T(8,128)(2,1)} %collective-permute-done.2.slot1), channel_id=1, source_target_pairs={{2,4},{4,2},{10,12},{12,10},{0,8},{8,0},{6,14},{14,6},{3,5},{5,3},... | collective-permute-start | bytes 2359304 | tf_op jit(solution)/shard_map/ppermute | solution.py:726
  26.9 37.6 %collective-permute-start.4 = (bf16[2,3072,128]{2,1,0:T(8,128)(2,1)S(1)}, bf16[2,3072,128]{2,1,0:T(8,128)(2,1)}, u32[]{:S(2)}, u32[]{:S(2)}) collective-permute-start(bf16[2,3072,128]{2,1,0:T(8,128)(2,1)S(1)} %multiply_bitcast_fusion.own_k), channel_id=1, source_target_pairs={{0,1},{1,0},{2,3},{3,2},{4,5},{5,4},{6,7},{7,6},{8,9},{9,8},{10,11... | collective-permute-start | bytes 4718600 | tf_op jit(solution)/shard_map/ppermute | solution.py:745
  28.6 20.5 %collective-permute-start.3 = (bf16[24,128,128]{2,1,0:T(8,128)(2,1)S(1)}, bf16[24,128,128]{2,1,0:T(8,128)(2,1)S(1)}, u32[]{:S(2)}, u32[]{:S(2)}) collective-permute-start(bf16[24,128,128]{2,1,0:T(8,128)(2,1)S(1)} %broadcast_select_fusion.1), channel_id=1, source_target_pairs={{0,2},{2,0},{4,6},{6,4},{1,3},{3,1},{5,7},{7,5},{8,10},{10,8},{12,... | collective-permute-start | bytes 2359304 | tf_op jit(solution)/shard_map/ppermute | solution.py:723
  31.6 33.0 %collective-permute-start.6 = (bf16[24,128,128]{2,1,0:T(8,128)(2,1)}, bf16[24,128,128]{2,1,0:T(8,128)(2,1)}, u32[]{:S(2)}, u32[]{:S(2)}) collective-permute-start(bf16[24,128,128]{2,1,0:T(8,128)(2,1)} %broadcast_select_fusion), channel_id=1, source_target_pairs={{0,2},{2,0},{4,6},{6,4},{1,3},{3,1},{5,7},{7,5},{8,10},{10,8},{12,... | collective-permute-start | bytes 2359304 | tf_op jit(solution)/shard_map/ppermute | solution.py:723
  50.0 11.0 %collective-permute-start.7 = (bf16[16,128,128]{2,1,0:T(8,128)(2,1)}, bf16[16,128,128]{2,1,0:T(8,128)(2,1)}, u32[]{:S(2)}, u32[]{:S(2)}) collective-permute-start(bf16[16,128,128]{2,1,0:T(8,128)(2,1)} %pad_maximum_fusion.2), channel_id=1, source_target_pairs={{2,4},{4,2},{10,12},{12,10},{0,8},{8,0},{6,14},{14,6},{3,5},{5,3},... | collective-permute-start | bytes 1572872 | tf_op jit(solution)/shard_map/ppermute | solution.py:726
  69.8 1.6 %collective-permute-start.9 = (f32[2,2,2,32,256]{4,3,2,1,0:T(8,128)S(1)}, f32[2,2,2,32,256]{4,3,2,1,0:T(8,128)S(1)}, u32[]{:S(2)}, u32[]{:S(2)}) collective-permute-start(f32[2,2,2,32,256]{4,3,2,1,0:T(8,128)S(1)} %get-tuple-element.46), channel_id=1, source_target_pairs={{0,8},{8,0},{1,9},{9,1},{2,10},{10,2},{3,11},{11,3},{4,12},{12,4},... | collective-permute-start | bytes 786440 | tf_op jit(solution)/shard_map/ppermute | solution.py:762
  69.9 3.8 %collective-permute-start.8 = (f32[2,2,2,32,256]{4,3,2,1,0:T(8,128)S(1)}, f32[2,2,2,32,256]{4,3,2,1,0:T(8,128)S(1)}, u32[]{:S(2)}, u32[]{:S(2)}) collective-permute-start(f32[2,2,2,32,256]{4,3,2,1,0:T(8,128)S(1)} %get-tuple-element.44), channel_id=1, source_target_pairs={{0,8},{8,0},{1,9},{9,1},{2,10},{10,2},{3,11},{11,3},{4,12},{12,4},... | collective-permute-start | bytes 786440 | tf_op jit(solution)/shard_map/ppermute | solution.py:763
  71.4 6.0 %collective-permute-start.10 = (bf16[2,2,2,32,256]{4,3,2,1,0:T(8,128)(2,1)S(1)}, bf16[2,2,2,32,256]{4,3,2,1,0:T(8,128)(2,1)S(1)}, u32[]{:S(2)}, u32[]{:S(2)}) collective-permute-start(bf16[2,2,2,32,256]{4,3,2,1,0:T(8,128)(2,1)S(1)} %near_sum.1), channel_id=1, source_target_pairs={{0,2},{2,0},{4,6},{6,4},{1,3},{3,1},{5,7},{7,5},{8,10},{10,8},{12,... | collective-permute-start | bytes 393224 | tf_op jit(solution)/shard_map/ppermute | solution.py:723
  78.0 4.3 %collective-permute-start.11 = (f32[2,32,256]{2,1,0:T(8,128)S(1)}, f32[2,32,256]{2,1,0:T(8,128)S(1)}, u32[]{:S(2)}, u32[]{:S(2)}) collective-permute-start(f32[2,32,256]{2,1,0:T(8,128)S(1)} %get-tuple-element.48), channel_id=1, source_target_pairs={{0,16},{16,0},{1,17},{17,1},{2,18},{18,2},{3,19},{19,3},{4,20},{20... | collective-permute-start | bytes 196616 | tf_op jit(solution)/shard_map/ppermute | solution.py:765
  79.6 4.5 %collective-permute-start.12 = (f32[2,32,256]{2,1,0:T(8,128)S(1)}, f32[2,32,256]{2,1,0:T(8,128)S(1)}, u32[]{:S(2)}, u32[]{:S(2)}) collective-permute-start(f32[2,32,256]{2,1,0:T(8,128)S(1)} %get-tuple-element.49), channel_id=1, source_target_pairs={{0,1},{1,0},{2,3},{3,2},{4,5},{5,4},{6,7},{7,6},{8,9},{9,8},{10,11... | collective-permute-start | bytes 196616 | tf_op jit(solution)/shard_map/ppermute | solution.py:766
  80.1 5.2 %collective-permute-start.13 = (f32[2,32,256]{2,1,0:T(8,128)S(1)}, f32[2,32,256]{2,1,0:T(8,128)S(1)}, u32[]{:S(2)}, u32[]{:S(2)}) collective-permute-start(f32[2,32,256]{2,1,0:T(8,128)S(1)} %get-tuple-element.50), channel_id=1, source_target_pairs={{0,17},{1,16},{16,1},{17,0},{2,19},{3,18},{18,3},{19,2},{4,21},{5,... | collective-permute-start | bytes 196616 | tf_op jit(solution)/shard_map/ppermute | solution.py:767
  86.7 4.0 %collective-permute-start.15 = (bf16[2,32,256]{2,1,0:T(8,128)(2,1)S(1)}, bf16[2,32,256]{2,1,0:T(8,128)(2,1)S(1)}, u32[]{:S(2)}, u32[]{:S(2)}) collective-permute-start(bf16[2,32,256]{2,1,0:T(8,128)(2,1)S(1)} %get-tuple-element.51), channel_id=1, source_target_pairs={{0,16},{16,0},{1,17},{17,1},{2,18},{18,2},{3,19},{19,3},{4,20},{20... | collective-permute-start | bytes 98312 | tf_op jit(solution)/shard_map/ppermute | solution.py:769
  87.3 4.8 %collective-permute-start.16 = (bf16[2,32,256]{2,1,0:T(8,128)(2,1)S(1)}, bf16[2,32,256]{2,1,0:T(8,128)(2,1)S(1)}, u32[]{:S(2)}, u32[]{:S(2)}) collective-permute-start(bf16[2,32,256]{2,1,0:T(8,128)(2,1)S(1)} %get-tuple-element.52), channel_id=1, source_target_pairs={{0,17},{1,16},{16,1},{17,0},{2,19},{3,18},{18,3},{19,2},{4,21},{5,... | collective-permute-start | bytes 98312 | tf_op jit(solution)/shard_map/ppermute | solution.py:771
  89.7 3.9 %collective-permute-start.14 = (bf16[2,32,256]{2,1,0:T(8,128)(2,1)S(1)}, bf16[2,32,256]{2,1,0:T(8,128)(2,1)S(1)}, u32[]{:S(2)}, u32[]{:S(2)}) collective-permute-start(bf16[2,32,256]{2,1,0:T(8,128)(2,1)S(1)} %get-tuple-element.52), channel_id=1, source_target_pairs={{0,1},{1,0},{2,3},{3,2},{4,5},{5,4},{6,7},{7,6},{8,9},{9,8},{10,11... | collective-permute-start | bytes 98312 | tf_op jit(solution)/shard_map/ppermute | solution.py:770
  93.7 1.9 %collective-permute-start.17 = (bf16[2,2,2,32,256]{4,3,2,1,0:T(8,128)(2,1)S(1)}, bf16[2,2,2,32,256]{4,3,2,1,0:T(8,128)(2,1)S(1)}, u32[]{:S(2)}, u32[]{:S(2)}) collective-permute-start(bf16[2,2,2,32,256]{4,3,2,1,0:T(8,128)(2,1)S(1)} %pad_maximum_fusion.3.half), channel_id=1, source_target_pairs={{0,8},{8,0},{1,9},{9,1},{2,10},{10,2},{3,11},{11,3},{4,12},{12,4},... | collective-permute-start | bytes 393224 | tf_op jit(solution)/shard_map/ppermute | solution.py:773
  93.8 5.9 %collective-permute-start.18 = (bf16[2,2,2,32,256]{4,3,2,1,0:T(8,128)(2,1)S(1)}, bf16[2,2,2,32,256]{4,3,2,1,0:T(8,128)(2,1)S(1)}, u32[]{:S(2)}, u32[]{:S(2)}) collective-permute-start(bf16[2,2,2,32,256]{4,3,2,1,0:T(8,128)(2,1)S(1)} %pad_maximum_fusion.3.half), channel_id=1, source_target_pairs={{0,2},{2,0},{4,6},{6,4},{1,3},{3,1},{5,7},{7,5},{8,10},{10,8},{12,... | collective-permute-start | bytes 393224 | tf_op jit(solution)/shard_map/ppermute | solution.py:723
  97.8 20.6 %collective-permute-start.25 = (bf16[16,128,128]{2,1,0:T(8,128)(2,1)S(1)}, bf16[16,128,128]{2,1,0:T(8,128)(2,1)S(1)}, u32[]{:S(2)}, u32[]{:S(2)}) collective-permute-start(bf16[16,128,128]{2,1,0:T(8,128)(2,1)S(1)} %first_adjoint.2), channel_id=1, source_target_pairs={{0,2},{2,0},{4,6},{6,4},{1,3},{3,1},{5,7},{7,5},{8,10},{10,8},{12,... | collective-permute-start | bytes 1572872 | tf_op jit(solution)/shard_map/ppermute | solution.py:723
  99.7 3.4 %collective-permute-start.19 = (bf16[2,2,2,32,256]{4,3,2,1,0:T(8,128)(2,1)S(1)}, bf16[2,2,2,32,256]{4,3,2,1,0:T(8,128)(2,1)S(1)}, u32[]{:S(2)}, u32[]{:S(2)}) collective-permute-start(bf16[2,2,2,32,256]{4,3,2,1,0:T(8,128)(2,1)S(1)} %collective-permute-done.18.near_half), channel_id=1, source_target_pairs={{0,8},{8,0},{1,9},{9,1},{2,10},{10,2},{3,11},{11,3},{4,12},{12,4},... | collective-permute-start | bytes 393224 | tf_op jit(solution)/shard_map/ppermute | solution.py:784
  101.4 16.9 %collective-permute-start.23 = (bf16[8,128,128]{2,1,0:T(8,128)(2,1)S(1)}, bf16[8,128,128]{2,1,0:T(8,128)(2,1)S(1)}, u32[]{:S(2)}, u32[]{:S(2)}) collective-permute-start(bf16[8,128,128]{2,1,0:T(8,128)(2,1)S(1)} %first_adjoint.3), channel_id=1, source_target_pairs={{0,2},{2,0},{4,6},{6,4},{1,3},{3,1},{5,7},{7,5},{8,10},{10,8},{12,... | collective-permute-start | bytes 786440 | tf_op jit(solution)/shard_map/ppermute | solution.py:723
  104.4 14.7 %collective-permute-start.20 = (bf16[16,128,128]{2,1,0:T(8,128)(2,1)S(1)}, bf16[16,128,128]{2,1,0:T(8,128)(2,1)S(1)}, u32[]{:S(2)}, u32[]{:S(2)}) collective-permute-start(bf16[16,128,128]{2,1,0:T(8,128)(2,1)S(1)} %near_adjoint.2), channel_id=1, source_target_pairs={{2,4},{4,2},{10,12},{12,10},{0,8},{8,0},{6,14},{14,6},{3,5},{5,3},... | collective-permute-start | bytes 1572872 | tf_op jit(solution)/shard_map/ppermute | solution.py:726
  110.7 18.8 %collective-permute-start.22 = (bf16[16,128,128]{2,1,0:T(8,128)(2,1)S(1)}, bf16[16,128,128]{2,1,0:T(8,128)(2,1)S(1)}, u32[]{:S(2)}, u32[]{:S(2)}) collective-permute-start(bf16[16,128,128]{2,1,0:T(8,128)(2,1)S(1)} %convert_element_type.60), channel_id=1, source_target_pairs={{0,2},{2,0},{4,6},{6,4},{1,3},{3,1},{5,7},{7,5},{8,10},{10,8},{12,... | collective-permute-start | bytes 1572872 | tf_op jit(solution)/shard_map/ppermute | solution.py:723
  118.3 2.9 %collective-permute-start.24 = (bf16[8,128,128]{2,1,0:T(8,128)(2,1)S(1)}, bf16[8,128,128]{2,1,0:T(8,128)(2,1)S(1)}, u32[]{:S(2)}, u32[]{:S(2)}) collective-permute-start(bf16[8,128,128]{2,1,0:T(8,128)(2,1)S(1)} %add_convert_fusion.5), channel_id=1, source_target_pairs={{2,4},{4,2},{10,12},{12,10},{0,8},{8,0},{6,14},{14,6},{3,5},{5,3},... | collective-permute-start | bytes 786440 | tf_op jit(solution)/shard_map/ppermute | solution.py:726
  118.6 15.8 %collective-permute-start.26 = (bf16[16,128,128]{2,1,0:T(8,128)(2,1)S(1)}, bf16[16,128,128]{2,1,0:T(8,128)(2,1)S(1)}, u32[]{:S(2)}, u32[]{:S(2)}) collective-permute-start(bf16[16,128,128]{2,1,0:T(8,128)(2,1)S(1)} %add_convert_fusion.2), channel_id=1, source_target_pairs={{2,4},{4,2},{10,12},{12,10},{0,8},{8,0},{6,14},{14,6},{3,5},{5,3},... | collective-permute-start | bytes 1572872 | tf_op jit(solution)/shard_map/ppermute | solution.py:726
  119.2 15.2 %collective-permute-start.21 = (bf16[8,128,128]{2,1,0:T(8,128)(2,1)S(1)}, bf16[8,128,128]{2,1,0:T(8,128)(2,1)S(1)}, u32[]{:S(2)}, u32[]{:S(2)}) collective-permute-start(bf16[8,128,128]{2,1,0:T(8,128)(2,1)S(1)} %fusion), channel_id=1, source_target_pairs={{0,2},{2,0},{4,6},{6,4},{1,3},{3,1},{5,7},{7,5},{8,10},{10,8},{12,... | collective-permute-start | bytes 786440 | tf_op jit(solution)/shard_map/ppermute | solution.py:723
  134.7 16.0 %collective-permute-start.29 = (bf16[16,128,128]{2,1,0:T(8,128)(2,1)S(1)}, bf16[16,128,128]{2,1,0:T(8,128)(2,1)S(1)}, u32[]{:S(2)}, u32[]{:S(2)}) collective-permute-start(bf16[16,128,128]{2,1,0:T(8,128)(2,1)S(1)} %add_convert_fusion.1), channel_id=1, source_target_pairs={{0,2},{2,0},{4,6},{6,4},{1,3},{3,1},{5,7},{7,5},{8,10},{10,8},{12,... | collective-permute-start | bytes 1572872 | tf_op jit(solution)/shard_map/ppermute | solution.py:723
  137.9 12.8 %collective-permute-start.30 = (bf16[16,128,128]{2,1,0:T(8,128)(2,1)S(1)}, bf16[16,128,128]{2,1,0:T(8,128)(2,1)S(1)}, u32[]{:S(2)}, u32[]{:S(2)}) collective-permute-start(bf16[16,128,128]{2,1,0:T(8,128)(2,1)S(1)} %add_convert_fusion), channel_id=1, source_target_pairs={{2,4},{4,2},{10,12},{12,10},{0,8},{8,0},{6,14},{14,6},{3,5},{5,3},... | collective-permute-start | bytes 1572872 | tf_op jit(solution)/shard_map/ppermute | solution.py:726
  138.0 15.8 %collective-permute-start.27 = (bf16[8,128,128]{2,1,0:T(8,128)(2,1)S(1)}, bf16[8,128,128]{2,1,0:T(8,128)(2,1)S(1)}, u32[]{:S(2)}, u32[]{:S(2)}) collective-permute-start(bf16[8,128,128]{2,1,0:T(8,128)(2,1)S(1)} %add_convert_fusion.4), channel_id=1, source_target_pairs={{0,2},{2,0},{4,6},{6,4},{1,3},{3,1},{5,7},{7,5},{8,10},{10,8},{12,... | collective-permute-start | bytes 786440 | tf_op jit(solution)/shard_map/ppermute | solution.py:723
  139.5 14.3 %collective-permute-start.28 = (bf16[8,128,128]{2,1,0:T(8,128)(2,1)S(1)}, bf16[8,128,128]{2,1,0:T(8,128)(2,1)S(1)}, u32[]{:S(2)}, u32[]{:S(2)}) collective-permute-start(bf16[8,128,128]{2,1,0:T(8,128)(2,1)S(1)} %add_convert_fusion.3), channel_id=1, source_target_pairs={{2,4},{4,2},{10,12},{12,10},{0,8},{8,0},{6,14},{14,6},{3,5},{5,3},... | collective-permute-start | bytes 786440 | tf_op jit(solution)/shard_map/ppermute | solution.py:726
  (15 other events, 259.7 us)

commit v6 on v5

--- a/solution.py
+++ b/solution.py
@@ -790,7 +790,8 @@
     part3, part2, part1, part0 = adjoint(
         place, half, other, own_b, far_b, (3, 2, 1, 0), jnp.float32
     )
-    far3 = mids(*(plus(part, got) for part, got in zip(part3, g1)))
+    got_0, peer_a = lax.optimization_barrier((g1[0], peer_a))
+    far3 = mids(plus(part3[0], got_0), plus(part3[1], g1[1]))
     ready_a = jnp.where(is_mid, plus(part1_a, peer_a[:tiles]), part2[0].astype(low))
     g2 = ends(ready_a, part2[1].astype(low))
     g2, far3 = lax.optimization_barrier((g2, far3))

time: 156 us -> 157 us (level)
  no operation moved by 1% of the time
where the time goes in v6:
time: 157 us; the launch traced here: 156 us
  waiting for transfers between devices  60.2 us (38%)
  starting transfers between devices  47.3 us (30%)
  Pallas kernels  28.1 us (18%)
  local copies, waits for them, and re-layouts  10.7 us (7%)
  other arithmetic  8.72 us (6%)
    ppermute x11, waiting for transfers between devices, ends(): return [lax.ppermute(value, 'outer', ENDS) for value in values]  49.9 us
    ppermute x11, starting transfers between devices, ends(): return [lax.ppermute(value, 'outer', ENDS) for value in values]  36 us
    pallas_call x1, Pallas kernels, adjoint(): pl.pallas_call(functools.partial(adjoint_kernel, slots, ends_only), grid=...  5.88 us
    pallas_call x1, Pallas kernels, late(): pl.pallas_call(late_kernel, grid=(4,), in_specs=[pl.BlockSpec(memory_spac...  5.27 us
    pallas_call x2, Pallas kernels, first_adjoint(): pl.pallas_call(functools.partial(first_kernel, slot), grid=(steps,), in_s...  3.94 us
    pallas_call x2, Pallas kernels, final(): pl.pallas_call(final_b_kernel, grid=(steps,), in_specs=[smem, each, each,...  3.74 us
  transfers between devices with their start and end apart: 31, of which 18 were waited for; matrix products, arithmetic and copies ran while one was open for 10% of the time, Pallas kernels for 12%

profile of v6, /device:TPU:0, one launch (start us, length us, event | category | flops | bytes accessed | tf_op | source)
XLA Modules:
  0.0 155.9 jit_solution(14947382023910023106)
XLA Ops:
  0.0 1.9 %reshape_squeeze.3 = bf16[64,2,32,128]{3,2,1,0:T(8,128)(2,1)S(1)} reshape(bf16[1,64,2,4096]{3,2,1,0:T(2,128)(2,1)} %param.12) | data formatting | bytes 2097152 | tf_op jit(solution)/shard_map/reshape;squeeze | solution.py:719
  2.7 3.1 %collective-permute-start.2 = (bf16[24,128,128]{2,1,0:T(8,128)(2,1)S(1)}, bf16[24,128,128]{2,1,0:T(8,128)(2,1)}, u32[]{:S(2)}, u32[]{:S(2)}) collective-permute-start(bf16[24,128,128]{2,1,0:T(8,128)(2,1)S(1)} %bitcast.44), channel_id=1, source_target_pairs={{0,2},{2,0},{4,6},{6,4},{1,3},{3,1},{5,7},{7,5},{8,10},{10,8},{12,... | collective-permute-start | bytes 2359304 | tf_op jit(solution)/shard_map/ppermute | solution.py:723
  7.0 2.1 %multiply_bitcast_fusion.1.own_a = bf16[2,1024,128]{2,1,0:T(8,128)(2,1)} fusion(bf16[1,1,2,4096,128]{4,3,2,1,0:T(8,128)(2,1)} %param.13, bf16[]{:T(256)S(6)} %convert_element_type.55), kind=kLoop, calls=%fused_computation.15 | loop fusion | flops 262144 | bytes 1048578 | tf_op jit(solution)/shard_map/mul | solution.py:735
  9.1 2.0 %pad_maximum_fusion.1 = bf16[24,128,128]{2,1,0:T(8,128)(2,1)} fusion(bf16[8,128,128]{2,1,0:T(8,128)(2,1)S(1)} %bitcast.48, bf16[16,128,128]{2,1,0:T(8,128)(2,1)} %bitcast.8), kind=kLoop, calls=%fused_computation.7 | loop fusion | flops 393216 | bytes 1572864 | tf_op jit(solution)/shard_map/concatenate | solution.py:737
  12.6 10.9 %collective-permute-done.2.slot1 = bf16[24,128,128]{2,1,0:T(8,128)(2,1)} collective-permute-done((bf16[24,128,128]{2,1,0:T(8,128)(2,1)S(1)}, bf16[24,128,128]{2,1,0:T(8,128)(2,1)}, u32[]{:S(2)}, u32[]{:S(2)}) %collective-permute-start.2) | collective-permute-done | bytes 786464 | tf_op jit(solution)/shard_map/ppermute | solution.py:723
  23.6 2.1 %collective-permute-done.far_a = bf16[2,1024,128]{2,1,0:T(8,128)(2,1)} collective-permute-done((bf16[2,1024,128]{2,1,0:T(8,128)(2,1)}, bf16[2,1024,128]{2,1,0:T(8,128)(2,1)}, u32[]{:S(2)}, u32[]{:S(2)}) %collective-permute-start) | collective-permute-done | bytes 524320 | tf_op jit(solution)/shard_map/ppermute | solution.py:739
  28.6 2.0 %collective-permute-start.3 = (bf16[24,128,128]{2,1,0:T(8,128)(2,1)S(1)}, bf16[24,128,128]{2,1,0:T(8,128)(2,1)S(1)}, u32[]{:S(2)}, u32[]{:S(2)}) collective-permute-start(bf16[24,128,128]{2,1,0:T(8,128)(2,1)S(1)} %broadcast_select_fusion.1), channel_id=1, source_target_pairs={{0,2},{2,0},{4,6},{6,4},{1,3},{3,1},{5,7},{7,5},{8,10},{10,8},{12,... | collective-permute-start | bytes 2359304 | tf_op jit(solution)/shard_map/ppermute | solution.py:723
  31.6 14.4 %collective-permute-start.6 = (bf16[24,128,128]{2,1,0:T(8,128)(2,1)}, bf16[24,128,128]{2,1,0:T(8,128)(2,1)}, u32[]{:S(2)}, u32[]{:S(2)}) collective-permute-start(bf16[24,128,128]{2,1,0:T(8,128)(2,1)} %broadcast_select_fusion), channel_id=1, source_target_pairs={{0,2},{2,0},{4,6},{6,4},{1,3},{3,1},{5,7},{7,5},{8,10},{10,8},{12,... | collective-permute-start | bytes 2359304 | tf_op jit(solution)/shard_map/ppermute | solution.py:723
  46.0 3.1 %collective-permute-done.3.end2.near_sky.near_k = bf16[24,128,128]{2,1,0:T(8,128)(2,1)S(1)} collective-permute-done((bf16[24,128,128]{2,1,0:T(8,128)(2,1)S(1)}, bf16[24,128,128]{2,1,0:T(8,128)(2,1)S(1)}, u32[]{:S(2)}, u32[]{:S(2)}) %collective-permute-start.3) | collective-permute-done | bytes 786464 | tf_op jit(solution)/shard_map/ppermute | solution.py:723
  58.1 2.8 %early.1.done = f32[384,256]{1,0:T(8,128)S(1)} custom-call(s32[8]{0:T(128)S(1)} %concatenate.12.place, bf16[2,3072,128]{2,1,0:T(8,128)(2,1)S(1)} %multiply_bitcast_fusion.own_k, bf16[24,128,128]{2,1,0:T(8,128)(2,1)S(1)} %bitcast.46, bf16[24,128,128]{2,1,0:T(8,128)(2,1)} %collective-permute-done.2.slot1, ...), custom_call_target="tpu_custom_call" | custom-call | flops 603979776 | bytes 4194304 | tf_op jit(solution)/shard_map/early/pallas_call | solution.py:216
  61.0 3.5 %collective-permute-done.6.end3.near_far_k = bf16[24,128,128]{2,1,0:T(8,128)(2,1)} collective-permute-done((bf16[24,128,128]{2,1,0:T(8,128)(2,1)}, bf16[24,128,128]{2,1,0:T(8,128)(2,1)}, u32[]{:S(2)}, u32[]{:S(2)}) %collective-permute-start.6) | collective-permute-done | bytes 786464 | tf_op jit(solution)/shard_map/ppermute | solution.py:723
  64.5 5.3 %late.1 = (f32[2,2,2,32,256]{4,3,2,1,0:T(8,128)S(1)}, f32[2,2,2,32,256]{4,3,2,1,0:T(8,128)S(1)}, f32[2,2,2,32,256]{4,3,2,1,0:T(8,128)S(1)}, f32[2,2,2,32,256]{4,3,2,1,0:T(8,128)S(1)}) custom-call(s32[8]{0:T(128)S(1)} %concatenate.12.place, f32[384,256]{1,0:T(8,128)S(1)} %early.1.done, bf16[2,3072,128]{2,1,0:T(8,128)(2,1)S(1)} %multiply_bitcast_fusion.own_k, ...), custom_call_target="tpu_custom_call" | custom-call | flops 1006632960 | bytes 9437184 | tf_op jit(solution)/shard_map/late/pallas_call | solution.py:311
  71.4 2.2 %collective-permute-start.10 = (bf16[2,2,2,32,256]{4,3,2,1,0:T(8,128)(2,1)S(1)}, bf16[2,2,2,32,256]{4,3,2,1,0:T(8,128)(2,1)S(1)}, u32[]{:S(2)}, u32[]{:S(2)}) collective-permute-start(bf16[2,2,2,32,256]{4,3,2,1,0:T(8,128)(2,1)S(1)} %near_sum.1), channel_id=1, source_target_pairs={{0,2},{2,0},{4,6},{6,4},{1,3},{3,1},{5,7},{7,5},{8,10},{10,8},{12,... | collective-permute-start | bytes 393224 | tf_op jit(solution)/shard_map/ppermute | solution.py:723
  73.7 3.8 %collective-permute-done.10.near = bf16[2,2,2,32,256]{4,3,2,1,0:T(8,128)(2,1)S(1)} collective-permute-done((bf16[2,2,2,32,256]{4,3,2,1,0:T(8,128)(2,1)S(1)}, bf16[2,2,2,32,256]{4,3,2,1,0:T(8,128)(2,1)S(1)}, u32[]{:S(2)}, u32[]{:S(2)}) %collective-permute-start.10) | collective-permute-done | bytes 131104 | tf_op jit(solution)/shard_map/ppermute | solution.py:723
  82.4 1.7 %collective-permute-done.12.from_y = f32[2,32,256]{2,1,0:T(8,128)S(1)} collective-permute-done((f32[2,32,256]{2,1,0:T(8,128)S(1)}, f32[2,32,256]{2,1,0:T(8,128)S(1)}, u32[]{:S(2)}, u32[]{:S(2)}) %collective-permute-start.12) | collective-permute-done | bytes 65568 | tf_op jit(solution)/shard_map/ppermute | solution.py:766
  87.3 2.4 %collective-permute-start.16 = (bf16[2,32,256]{2,1,0:T(8,128)(2,1)S(1)}, bf16[2,32,256]{2,1,0:T(8,128)(2,1)S(1)}, u32[]{:S(2)}, u32[]{:S(2)}) collective-permute-start(bf16[2,32,256]{2,1,0:T(8,128)(2,1)S(1)} %get-tuple-element.54), channel_id=1, source_target_pairs={{0,17},{1,16},{16,1},{17,0},{2,19},{3,18},{18,3},{19,2},{4,21},{5,... | collective-permute-start | bytes 98312 | tf_op jit(solution)/shard_map/ppermute | solution.py:771
  93.8 1.8 %collective-permute-start.18 = (bf16[2,2,2,32,256]{4,3,2,1,0:T(8,128)(2,1)S(1)}, bf16[2,2,2,32,256]{4,3,2,1,0:T(8,128)(2,1)S(1)}, u32[]{:S(2)}, u32[]{:S(2)}) collective-permute-start(bf16[2,2,2,32,256]{4,3,2,1,0:T(8,128)(2,1)S(1)} %pad_maximum_fusion.3.half), channel_id=1, source_target_pairs={{0,2},{2,0},{4,6},{6,4},{1,3},{3,1},{5,7},{7,5},{8,10},{10,8},{12,... | collective-permute-start | bytes 393224 | tf_op jit(solution)/shard_map/ppermute | solution.py:723
  95.6 2.3 %first_adjoint.2 = bf16[16,128,128]{2,1,0:T(8,128)(2,1)S(1)} custom-call(s32[8]{0:T(128)S(1)} %concatenate.12.place, bf16[2,2,2,32,256]{4,3,2,1,0:T(8,128)(2,1)S(1)} %pad_maximum_fusion.3.half, bf16[2,2,2,32,256]{4,3,2,1,0:T(8,128)(2,1)S(1)} %collective-permute-done.17.other, bf16[2,3072,128]{2,1,0:T(8,128)(2,1)S(1)} %multiply_bitcast_fusion.own_k, ...), custom_call_target="tpu_custom_call" | custom-call | flops 5368709120 | bytes 83886080 | tf_op jit(solution)/shard_map/first_adjoint/pallas_call | solution.py:567
  99.7 1.7 %first_adjoint.3 = bf16[8,128,128]{2,1,0:T(8,128)(2,1)S(1)} custom-call(s32[8]{0:T(128)S(1)} %concatenate.12.place, bf16[2,2,2,32,256]{4,3,2,1,0:T(8,128)(2,1)S(1)} %pad_maximum_fusion.3.half, bf16[2,2,2,32,256]{4,3,2,1,0:T(8,128)(2,1)S(1)} %collective-permute-done.17.other, bf16[2,3072,128]{2,1,0:T(8,128)(2,1)S(1)} %multiply_bitcast_fusion.own_k, ...), custom_call_target="tpu_custom_call" | custom-call | flops 2684354560 | bytes 41943040 | tf_op jit(solution)/shard_map/first_adjoint/pallas_call | solution.py:567
  101.4 1.7 %collective-permute-start.20 = (bf16[8,128,128]{2,1,0:T(8,128)(2,1)S(1)}, bf16[8,128,128]{2,1,0:T(8,128)(2,1)S(1)}, u32[]{:S(2)}, u32[]{:S(2)}) collective-permute-start(bf16[8,128,128]{2,1,0:T(8,128)(2,1)S(1)} %first_adjoint.3), channel_id=1, source_target_pairs={{0,2},{2,0},{4,6},{6,4},{1,3},{3,1},{5,7},{7,5},{8,10},{10,8},{12,... | collective-permute-start | bytes 786440 | tf_op jit(solution)/shard_map/ppermute | solution.py:723
  104.7 5.9 %adjoint.1 = (f32[8,128,128]{2,1,0:T(8,128)S(1)}, f32[16,128,128]{2,1,0:T(8,128)S(1)}, f32[8,128,128]{2,1,0:T(8,128)S(1)}, f32[16,128,128]{2,1,0:T(8,128)S(1)}, ...) custom-call(s32[8]{0:T(128)S(1)} %concatenate.12.place, ...), custom_call_target="tpu_custom_call" | custom-call | flops 32212254720 | bytes 251658240 | tf_op jit(solution)/shard_map/adjoint/pallas_call | solution.py:525
  110.7 2.6 %collective-permute-start.23 = (bf16[16,128,128]{2,1,0:T(8,128)(2,1)S(1)}, bf16[16,128,128]{2,1,0:T(8,128)(2,1)S(1)}, u32[]{:S(2)}, u32[]{:S(2)}) collective-permute-start(bf16[16,128,128]{2,1,0:T(8,128)(2,1)S(1)} %convert_element_type.60), channel_id=1, source_target_pairs={{0,2},{2,0},{4,6},{6,4},{1,3},{3,1},{5,7},{7,5},{8,10},{10,8},{12,... | collective-permute-start | bytes 1572872 | tf_op jit(solution)/shard_map/ppermute | solution.py:723
  114.9 3.4 %collective-permute-done.20 = bf16[8,128,128]{2,1,0:T(8,128)(2,1)S(1)} collective-permute-done((bf16[8,128,128]{2,1,0:T(8,128)(2,1)S(1)}, bf16[8,128,128]{2,1,0:T(8,128)(2,1)S(1)}, u32[]{:S(2)}, u32[]{:S(2)}) %collective-permute-start.20) | collective-permute-done | bytes 262176 | tf_op jit(solution)/shard_map/ppermute | solution.py:723
  118.5 3.8 %collective-permute-start.22 = (bf16[8,128,128]{2,1,0:T(8,128)(2,1)S(1)}, bf16[8,128,128]{2,1,0:T(8,128)(2,1)S(1)}, u32[]{:S(2)}, u32[]{:S(2)}) collective-permute-start(bf16[8,128,128]{2,1,0:T(8,128)(2,1)S(1)} %fusion), channel_id=1, source_target_pairs={{0,2},{2,0},{4,6},{6,4},{1,3},{3,1},{5,7},{7,5},{8,10},{10,8},{12,... | collective-permute-start | bytes 786440 | tf_op jit(solution)/shard_map/ppermute | solution.py:723
  122.3 7.2 %collective-permute-done.23 = bf16[16,128,128]{2,1,0:T(8,128)(2,1)S(1)} collective-permute-done((bf16[16,128,128]{2,1,0:T(8,128)(2,1)S(1)}, bf16[16,128,128]{2,1,0:T(8,128)(2,1)S(1)}, u32[]{:S(2)}, u32[]{:S(2)}) %collective-permute-start.23) | collective-permute-done | bytes 524320 | tf_op jit(solution)/shard_map/ppermute | solution.py:723
  129.5 4.8 %collective-permute-done.22.end_a = bf16[8,128,128]{2,1,0:T(8,128)(2,1)S(1)} collective-permute-done((bf16[8,128,128]{2,1,0:T(8,128)(2,1)S(1)}, bf16[8,128,128]{2,1,0:T(8,128)(2,1)S(1)}, u32[]{:S(2)}, u32[]{:S(2)}) %collective-permute-start.22) | collective-permute-done | bytes 262176 | tf_op jit(solution)/shard_map/ppermute | solution.py:723
  134.7 2.5 %collective-permute-start.29 = (bf16[16,128,128]{2,1,0:T(8,128)(2,1)S(1)}, bf16[16,128,128]{2,1,0:T(8,128)(2,1)S(1)}, u32[]{:S(2)}, u32[]{:S(2)}) collective-permute-start(bf16[16,128,128]{2,1,0:T(8,128)(2,1)S(1)} %add_convert_fusion.1), channel_id=1, source_target_pairs={{0,2},{2,0},{4,6},{6,4},{1,3},{3,1},{5,7},{7,5},{8,10},{10,8},{12,... | collective-permute-start | bytes 1572872 | tf_op jit(solution)/shard_map/ppermute | solution.py:723
  138.8 1.7 %final_a.1.before = f32[64,2,4096]{2,1,0:T(2,128)} custom-call(s32[8]{0:T(128)S(1)} %concatenate.12.place, f32[8,128,128]{2,1,0:T(8,128)S(1)} %get-tuple-element.72.part_a, bf16[16,128,128]{2,1,0:T(8,128)(2,1)S(1)} %collective-permute-done.21.peer_a, bf16[8,128,128]{2,1,0:T(8,128)(2,1)S(1)} %collective-permute-done.22.end_a), custom_call_target="tpu_custom_call" | custom-call | flops 262144 | bytes 1048576 | tf_op jit(solution)/shard_map/final_a/pallas_call | solution.py:665
  140.5 9.5 %collective-permute-done.29.near = bf16[16,128,128]{2,1,0:T(8,128)(2,1)S(1)} collective-permute-done((bf16[16,128,128]{2,1,0:T(8,128)(2,1)S(1)}, bf16[16,128,128]{2,1,0:T(8,128)(2,1)S(1)}, u32[]{:S(2)}, u32[]{:S(2)}) %collective-permute-start.29) | collective-permute-done | bytes 524320 | tf_op jit(solution)/shard_map/ppermute | solution.py:723
  150.0 2.1 %final_b.2.before = f32[64,2,4096]{2,1,0:T(2,128)} custom-call(s32[8]{0:T(128)S(1)} %concatenate.12.place, f32[16,128,128]{2,1,0:T(8,128)S(1)} %get-tuple-element.68.part, bf16[16,128,128]{2,1,0:T(8,128)(2,1)S(1)} %collective-permute-done.29.near, bf16[16,128,128]{2,1,0:T(8,128)(2,1)S(1)} %collective-permute-done.30.far, ...), custom_call_target="tpu_custom_call", output_to_operand_aliasing={{}: (4, {})} | custom-call | flops 786432 | bytes 2097152 | tf_op jit(solution)/shard_map/final_b/pallas_call | solution.py:677
  152.0 2.2 %collective-permute-done.27.near = bf16[8,128,128]{2,1,0:T(8,128)(2,1)S(1)} collective-permute-done((bf16[8,128,128]{2,1,0:T(8,128)(2,1)S(1)}, bf16[8,128,128]{2,1,0:T(8,128)(2,1)S(1)}, u32[]{:S(2)}, u32[]{:S(2)}) %collective-permute-start.27) | collective-permute-done | bytes 262176 | tf_op jit(solution)/shard_map/ppermute | solution.py:723
  154.3 1.7 %final_b.3 = f32[64,2,4096]{2,1,0:T(2,128)} custom-call(s32[8]{0:T(128)S(1)} %concatenate.12.place, f32[8,128,128]{2,1,0:T(8,128)S(1)} %get-tuple-element.57.part, bf16[8,128,128]{2,1,0:T(8,128)(2,1)S(1)} %collective-permute-done.27.near, bf16[8,128,128]{2,1,0:T(8,128)(2,1)S(1)} %collective-permute-done.28.far, ...), custom_call_target="tpu_custom_call", output_to_operand_aliasing={{}: (4, {})} | custom-call | flops 393216 | bytes 1048576 | tf_op jit(solution)/shard_map/final_b/pallas_call | solution.py:677
  (112 shorter events, 36.9 us)
Async XLA Ops:
  0.0 52.6 %copy-start = (bf16[1,2,128,512]{3,2,1,0:T(8,128)(2,1)S(1)}, bf16[1,2,128,512]{3,2,1,0:T(8,128)(2,1)}, u32[]{:S(2)}) copy-start(bf16[1,2,128,512]{3,2,1,0:T(8,128)(2,1)} %param.14) | copy-start | bytes 786436
  2.7 20.7 %collective-permute-start.2 = (bf16[24,128,128]{2,1,0:T(8,128)(2,1)S(1)}, bf16[24,128,128]{2,1,0:T(8,128)(2,1)}, u32[]{:S(2)}, u32[]{:S(2)}) collective-permute-start(bf16[24,128,128]{2,1,0:T(8,128)(2,1)S(1)} %bitcast.44), channel_id=1, source_target_pairs={{0,2},{2,0},{4,6},{6,4},{1,3},{3,1},{5,7},{7,5},{8,10},{10,8},{12,... | collective-permute-start | bytes 2359304 | tf_op jit(solution)/shard_map/ppermute | solution.py:723
  5.8 21.1 %collective-permute-start.1 = (bf16[24,128,128]{2,1,0:T(8,128)(2,1)S(1)}, bf16[24,128,128]{2,1,0:T(8,128)(2,1)S(1)}, u32[]{:S(2)}, u32[]{:S(2)}) collective-permute-start(bf16[24,128,128]{2,1,0:T(8,128)(2,1)S(1)} %bitcast.45), channel_id=1, source_target_pairs={{2,4},{4,2},{10,12},{12,10},{0,8},{8,0},{6,14},{14,6},{3,5},{5,3},... | collective-permute-start | bytes 2359304 | tf_op jit(solution)/shard_map/ppermute | solution.py:726
  11.1 14.7 %collective-permute-start = (bf16[2,1024,128]{2,1,0:T(8,128)(2,1)}, bf16[2,1024,128]{2,1,0:T(8,128)(2,1)}, u32[]{:S(2)}, u32[]{:S(2)}) collective-permute-start(bf16[2,1024,128]{2,1,0:T(8,128)(2,1)} %multiply_bitcast_fusion.1.own_a), channel_id=1, source_target_pairs={{0,1},{1,0},{2,3},{3,2},{4,5},{5,4},{6,7},{7,6},{8,9},{9,8},{10,11... | collective-permute-start | bytes 1572872 | tf_op jit(solution)/shard_map/ppermute | solution.py:739
  23.4 7.2 %collective-permute-start.5 = (bf16[24,128,128]{2,1,0:T(8,128)(2,1)}, bf16[24,128,128]{2,1,0:T(8,128)(2,1)}, u32[]{:S(2)}, u32[]{:S(2)}) collective-permute-start(bf16[24,128,128]{2,1,0:T(8,128)(2,1)} %collective-permute-done.2.slot1), channel_id=1, source_target_pairs={{2,4},{4,2},{10,12},{12,10},{0,8},{8,0},{6,14},{14,6},{3,5},{5,3},... | collective-permute-start | bytes 2359304 | tf_op jit(solution)/shard_map/ppermute | solution.py:726
  26.9 37.6 %collective-permute-start.4 = (bf16[2,3072,128]{2,1,0:T(8,128)(2,1)S(1)}, bf16[2,3072,128]{2,1,0:T(8,128)(2,1)}, u32[]{:S(2)}, u32[]{:S(2)}) collective-permute-start(bf16[2,3072,128]{2,1,0:T(8,128)(2,1)S(1)} %multiply_bitcast_fusion.own_k), channel_id=1, source_target_pairs={{0,1},{1,0},{2,3},{3,2},{4,5},{5,4},{6,7},{7,6},{8,9},{9,8},{10,11... | collective-permute-start | bytes 4718600 | tf_op jit(solution)/shard_map/ppermute | solution.py:745
  28.6 20.5 %collective-permute-start.3 = (bf16[24,128,128]{2,1,0:T(8,128)(2,1)S(1)}, bf16[24,128,128]{2,1,0:T(8,128)(2,1)S(1)}, u32[]{:S(2)}, u32[]{:S(2)}) collective-permute-start(bf16[24,128,128]{2,1,0:T(8,128)(2,1)S(1)} %broadcast_select_fusion.1), channel_id=1, source_target_pairs={{0,2},{2,0},{4,6},{6,4},{1,3},{3,1},{5,7},{7,5},{8,10},{10,8},{12,... | collective-permute-start | bytes 2359304 | tf_op jit(solution)/shard_map/ppermute | solution.py:723
  31.6 33.0 %collective-permute-start.6 = (bf16[24,128,128]{2,1,0:T(8,128)(2,1)}, bf16[24,128,128]{2,1,0:T(8,128)(2,1)}, u32[]{:S(2)}, u32[]{:S(2)}) collective-permute-start(bf16[24,128,128]{2,1,0:T(8,128)(2,1)} %broadcast_select_fusion), channel_id=1, source_target_pairs={{0,2},{2,0},{4,6},{6,4},{1,3},{3,1},{5,7},{7,5},{8,10},{10,8},{12,... | collective-permute-start | bytes 2359304 | tf_op jit(solution)/shard_map/ppermute | solution.py:723
  50.0 11.0 %collective-permute-start.7 = (bf16[16,128,128]{2,1,0:T(8,128)(2,1)}, bf16[16,128,128]{2,1,0:T(8,128)(2,1)}, u32[]{:S(2)}, u32[]{:S(2)}) collective-permute-start(bf16[16,128,128]{2,1,0:T(8,128)(2,1)} %pad_maximum_fusion.2), channel_id=1, source_target_pairs={{2,4},{4,2},{10,12},{12,10},{0,8},{8,0},{6,14},{14,6},{3,5},{5,3},... | collective-permute-start | bytes 1572872 | tf_op jit(solution)/shard_map/ppermute | solution.py:726
  69.8 1.6 %collective-permute-start.9 = (f32[2,2,2,32,256]{4,3,2,1,0:T(8,128)S(1)}, f32[2,2,2,32,256]{4,3,2,1,0:T(8,128)S(1)}, u32[]{:S(2)}, u32[]{:S(2)}) collective-permute-start(f32[2,2,2,32,256]{4,3,2,1,0:T(8,128)S(1)} %get-tuple-element.48), channel_id=1, source_target_pairs={{0,8},{8,0},{1,9},{9,1},{2,10},{10,2},{3,11},{11,3},{4,12},{12,4},... | collective-permute-start | bytes 786440 | tf_op jit(solution)/shard_map/ppermute | solution.py:762
  69.9 3.8 %collective-permute-start.8 = (f32[2,2,2,32,256]{4,3,2,1,0:T(8,128)S(1)}, f32[2,2,2,32,256]{4,3,2,1,0:T(8,128)S(1)}, u32[]{:S(2)}, u32[]{:S(2)}) collective-permute-start(f32[2,2,2,32,256]{4,3,2,1,0:T(8,128)S(1)} %get-tuple-element.46), channel_id=1, source_target_pairs={{0,8},{8,0},{1,9},{9,1},{2,10},{10,2},{3,11},{11,3},{4,12},{12,4},... | collective-permute-start | bytes 786440 | tf_op jit(solution)/shard_map/ppermute | solution.py:763
  71.4 6.0 %collective-permute-start.10 = (bf16[2,2,2,32,256]{4,3,2,1,0:T(8,128)(2,1)S(1)}, bf16[2,2,2,32,256]{4,3,2,1,0:T(8,128)(2,1)S(1)}, u32[]{:S(2)}, u32[]{:S(2)}) collective-permute-start(bf16[2,2,2,32,256]{4,3,2,1,0:T(8,128)(2,1)S(1)} %near_sum.1), channel_id=1, source_target_pairs={{0,2},{2,0},{4,6},{6,4},{1,3},{3,1},{5,7},{7,5},{8,10},{10,8},{12,... | collective-permute-start | bytes 393224 | tf_op jit(solution)/shard_map/ppermute | solution.py:723
  78.0 4.3 %collective-permute-start.11 = (f32[2,32,256]{2,1,0:T(8,128)S(1)}, f32[2,32,256]{2,1,0:T(8,128)S(1)}, u32[]{:S(2)}, u32[]{:S(2)}) collective-permute-start(f32[2,32,256]{2,1,0:T(8,128)S(1)} %get-tuple-element.50), channel_id=1, source_target_pairs={{0,16},{16,0},{1,17},{17,1},{2,18},{18,2},{3,19},{19,3},{4,20},{20... | collective-permute-start | bytes 196616 | tf_op jit(solution)/shard_map/ppermute | solution.py:765
  79.6 4.5 %collective-permute-start.12 = (f32[2,32,256]{2,1,0:T(8,128)S(1)}, f32[2,32,256]{2,1,0:T(8,128)S(1)}, u32[]{:S(2)}, u32[]{:S(2)}) collective-permute-start(f32[2,32,256]{2,1,0:T(8,128)S(1)} %get-tuple-element.51), channel_id=1, source_target_pairs={{0,1},{1,0},{2,3},{3,2},{4,5},{5,4},{6,7},{7,6},{8,9},{9,8},{10,11... | collective-permute-start | bytes 196616 | tf_op jit(solution)/shard_map/ppermute | solution.py:766
  80.1 5.2 %collective-permute-start.13 = (f32[2,32,256]{2,1,0:T(8,128)S(1)}, f32[2,32,256]{2,1,0:T(8,128)S(1)}, u32[]{:S(2)}, u32[]{:S(2)}) collective-permute-start(f32[2,32,256]{2,1,0:T(8,128)S(1)} %get-tuple-element.52), channel_id=1, source_target_pairs={{0,17},{1,16},{16,1},{17,0},{2,19},{3,18},{18,3},{19,2},{4,21},{5,... | collective-permute-start | bytes 196616 | tf_op jit(solution)/shard_map/ppermute | solution.py:767
  86.7 4.0 %collective-permute-start.15 = (bf16[2,32,256]{2,1,0:T(8,128)(2,1)S(1)}, bf16[2,32,256]{2,1,0:T(8,128)(2,1)S(1)}, u32[]{:S(2)}, u32[]{:S(2)}) collective-permute-start(bf16[2,32,256]{2,1,0:T(8,128)(2,1)S(1)} %get-tuple-element.53), channel_id=1, source_target_pairs={{0,16},{16,0},{1,17},{17,1},{2,18},{18,2},{3,19},{19,3},{4,20},{20... | collective-permute-start | bytes 98312 | tf_op jit(solution)/shard_map/ppermute | solution.py:769
  87.3 4.8 %collective-permute-start.16 = (bf16[2,32,256]{2,1,0:T(8,128)(2,1)S(1)}, bf16[2,32,256]{2,1,0:T(8,128)(2,1)S(1)}, u32[]{:S(2)}, u32[]{:S(2)}) collective-permute-start(bf16[2,32,256]{2,1,0:T(8,128)(2,1)S(1)} %get-tuple-element.54), channel_id=1, source_target_pairs={{0,17},{1,16},{16,1},{17,0},{2,19},{3,18},{18,3},{19,2},{4,21},{5,... | collective-permute-start | bytes 98312 | tf_op jit(solution)/shard_map/ppermute | solution.py:771
  89.7 3.9 %collective-permute-start.14 = (bf16[2,32,256]{2,1,0:T(8,128)(2,1)S(1)}, bf16[2,32,256]{2,1,0:T(8,128)(2,1)S(1)}, u32[]{:S(2)}, u32[]{:S(2)}) collective-permute-start(bf16[2,32,256]{2,1,0:T(8,128)(2,1)S(1)} %get-tuple-element.54), channel_id=1, source_target_pairs={{0,1},{1,0},{2,3},{3,2},{4,5},{5,4},{6,7},{7,6},{8,9},{9,8},{10,11... | collective-permute-start | bytes 98312 | tf_op jit(solution)/shard_map/ppermute | solution.py:770
  93.7 1.9 %collective-permute-start.17 = (bf16[2,2,2,32,256]{4,3,2,1,0:T(8,128)(2,1)S(1)}, bf16[2,2,2,32,256]{4,3,2,1,0:T(8,128)(2,1)S(1)}, u32[]{:S(2)}, u32[]{:S(2)}) collective-permute-start(bf16[2,2,2,32,256]{4,3,2,1,0:T(8,128)(2,1)S(1)} %pad_maximum_fusion.3.half), channel_id=1, source_target_pairs={{0,8},{8,0},{1,9},{9,1},{2,10},{10,2},{3,11},{11,3},{4,12},{12,4},... | collective-permute-start | bytes 393224 | tf_op jit(solution)/shard_map/ppermute | solution.py:773
  93.8 5.9 %collective-permute-start.18 = (bf16[2,2,2,32,256]{4,3,2,1,0:T(8,128)(2,1)S(1)}, bf16[2,2,2,32,256]{4,3,2,1,0:T(8,128)(2,1)S(1)}, u32[]{:S(2)}, u32[]{:S(2)}) collective-permute-start(bf16[2,2,2,32,256]{4,3,2,1,0:T(8,128)(2,1)S(1)} %pad_maximum_fusion.3.half), channel_id=1, source_target_pairs={{0,2},{2,0},{4,6},{6,4},{1,3},{3,1},{5,7},{7,5},{8,10},{10,8},{12,... | collective-permute-start | bytes 393224 | tf_op jit(solution)/shard_map/ppermute | solution.py:723
  97.8 16.9 %collective-permute-start.25 = (bf16[16,128,128]{2,1,0:T(8,128)(2,1)S(1)}, bf16[16,128,128]{2,1,0:T(8,128)(2,1)S(1)}, u32[]{:S(2)}, u32[]{:S(2)}) collective-permute-start(bf16[16,128,128]{2,1,0:T(8,128)(2,1)S(1)} %first_adjoint.2), channel_id=1, source_target_pairs={{0,2},{2,0},{4,6},{6,4},{1,3},{3,1},{5,7},{7,5},{8,10},{10,8},{12,... | collective-permute-start | bytes 1572872 | tf_op jit(solution)/shard_map/ppermute | solution.py:723
  99.7 3.4 %collective-permute-start.19 = (bf16[2,2,2,32,256]{4,3,2,1,0:T(8,128)(2,1)S(1)}, bf16[2,2,2,32,256]{4,3,2,1,0:T(8,128)(2,1)S(1)}, u32[]{:S(2)}, u32[]{:S(2)}) collective-permute-start(bf16[2,2,2,32,256]{4,3,2,1,0:T(8,128)(2,1)S(1)} %collective-permute-done.18.near_half), channel_id=1, source_target_pairs={{0,8},{8,0},{1,9},{9,1},{2,10},{10,2},{3,11},{11,3},{4,12},{12,4},... | collective-permute-start | bytes 393224 | tf_op jit(solution)/shard_map/ppermute | solution.py:784
  101.4 16.9 %collective-permute-start.20 = (bf16[8,128,128]{2,1,0:T(8,128)(2,1)S(1)}, bf16[8,128,128]{2,1,0:T(8,128)(2,1)S(1)}, u32[]{:S(2)}, u32[]{:S(2)}) collective-permute-start(bf16[8,128,128]{2,1,0:T(8,128)(2,1)S(1)} %first_adjoint.3), channel_id=1, source_target_pairs={{0,2},{2,0},{4,6},{6,4},{1,3},{3,1},{5,7},{7,5},{8,10},{10,8},{12,... | collective-permute-start | bytes 786440 | tf_op jit(solution)/shard_map/ppermute | solution.py:723
  104.4 13.9 %collective-permute-start.21 = (bf16[16,128,128]{2,1,0:T(8,128)(2,1)S(1)}, bf16[16,128,128]{2,1,0:T(8,128)(2,1)S(1)}, u32[]{:S(2)}, u32[]{:S(2)}) collective-permute-start(bf16[16,128,128]{2,1,0:T(8,128)(2,1)S(1)} %near_adjoint.2), channel_id=1, source_target_pairs={{2,4},{4,2},{10,12},{12,10},{0,8},{8,0},{6,14},{14,6},{3,5},{5,3},... | collective-permute-start | bytes 1572872 | tf_op jit(solution)/shard_map/ppermute | solution.py:726
  110.7 18.8 %collective-permute-start.23 = (bf16[16,128,128]{2,1,0:T(8,128)(2,1)S(1)}, bf16[16,128,128]{2,1,0:T(8,128)(2,1)S(1)}, u32[]{:S(2)}, u32[]{:S(2)}) collective-permute-start(bf16[16,128,128]{2,1,0:T(8,128)(2,1)S(1)} %convert_element_type.60), channel_id=1, source_target_pairs={{0,2},{2,0},{4,6},{6,4},{1,3},{3,1},{5,7},{7,5},{8,10},{10,8},{12,... | collective-permute-start | bytes 1572872 | tf_op jit(solution)/shard_map/ppermute | solution.py:723
  114.8 19.5 %collective-permute-start.26 = (bf16[16,128,128]{2,1,0:T(8,128)(2,1)S(1)}, bf16[16,128,128]{2,1,0:T(8,128)(2,1)S(1)}, u32[]{:S(2)}, u32[]{:S(2)}) collective-permute-start(bf16[16,128,128]{2,1,0:T(8,128)(2,1)S(1)} %add_convert_fusion.2), channel_id=1, source_target_pairs={{2,4},{4,2},{10,12},{12,10},{0,8},{8,0},{6,14},{14,6},{3,5},{5,3},... | collective-permute-start | bytes 1572872 | tf_op jit(solution)/shard_map/ppermute | solution.py:726
  118.3 11.2 %collective-permute-start.24 = (bf16[8,128,128]{2,1,0:T(8,128)(2,1)S(1)}, bf16[8,128,128]{2,1,0:T(8,128)(2,1)S(1)}, u32[]{:S(2)}, u32[]{:S(2)}) collective-permute-start(bf16[8,128,128]{2,1,0:T(8,128)(2,1)S(1)} %add_convert_fusion.5), channel_id=1, source_target_pairs={{2,4},{4,2},{10,12},{12,10},{0,8},{8,0},{6,14},{14,6},{3,5},{5,3},... | collective-permute-start | bytes 786440 | tf_op jit(solution)/shard_map/ppermute | solution.py:726
  118.5 15.9 %collective-permute-start.22 = (bf16[8,128,128]{2,1,0:T(8,128)(2,1)S(1)}, bf16[8,128,128]{2,1,0:T(8,128)(2,1)S(1)}, u32[]{:S(2)}, u32[]{:S(2)}) collective-permute-start(bf16[8,128,128]{2,1,0:T(8,128)(2,1)S(1)} %fusion), channel_id=1, source_target_pairs={{0,2},{2,0},{4,6},{6,4},{1,3},{3,1},{5,7},{7,5},{8,10},{10,8},{12,... | collective-permute-start | bytes 786440 | tf_op jit(solution)/shard_map/ppermute | solution.py:723
  134.7 15.3 %collective-permute-start.29 = (bf16[16,128,128]{2,1,0:T(8,128)(2,1)S(1)}, bf16[16,128,128]{2,1,0:T(8,128)(2,1)S(1)}, u32[]{:S(2)}, u32[]{:S(2)}) collective-permute-start(bf16[16,128,128]{2,1,0:T(8,128)(2,1)S(1)} %add_convert_fusion.1), channel_id=1, source_target_pairs={{0,2},{2,0},{4,6},{6,4},{1,3},{3,1},{5,7},{7,5},{8,10},{10,8},{12,... | collective-permute-start | bytes 1572872 | tf_op jit(solution)/shard_map/ppermute | solution.py:723
  137.1 12.8 %collective-permute-start.30 = (bf16[16,128,128]{2,1,0:T(8,128)(2,1)S(1)}, bf16[16,128,128]{2,1,0:T(8,128)(2,1)S(1)}, u32[]{:S(2)}, u32[]{:S(2)}) collective-permute-start(bf16[16,128,128]{2,1,0:T(8,128)(2,1)S(1)} %add_convert_fusion), channel_id=1, source_target_pairs={{2,4},{4,2},{10,12},{12,10},{0,8},{8,0},{6,14},{14,6},{3,5},{5,3},... | collective-permute-start | bytes 1572872 | tf_op jit(solution)/shard_map/ppermute | solution.py:726
  137.3 17.0 %collective-permute-start.27 = (bf16[8,128,128]{2,1,0:T(8,128)(2,1)S(1)}, bf16[8,128,128]{2,1,0:T(8,128)(2,1)S(1)}, u32[]{:S(2)}, u32[]{:S(2)}) collective-permute-start(bf16[8,128,128]{2,1,0:T(8,128)(2,1)S(1)} %add_convert_fusion.4), channel_id=1, source_target_pairs={{0,2},{2,0},{4,6},{6,4},{1,3},{3,1},{5,7},{7,5},{8,10},{10,8},{12,... | collective-permute-start | bytes 786440 | tf_op jit(solution)/shard_map/ppermute | solution.py:723
  138.8 15.4 %collective-permute-start.28 = (bf16[8,128,128]{2,1,0:T(8,128)(2,1)S(1)}, bf16[8,128,128]{2,1,0:T(8,128)(2,1)S(1)}, u32[]{:S(2)}, u32[]{:S(2)}) collective-permute-start(bf16[8,128,128]{2,1,0:T(8,128)(2,1)S(1)} %add_convert_fusion.3), channel_id=1, source_target_pairs={{2,4},{4,2},{10,12},{12,10},{0,8},{8,0},{6,14},{14,6},{3,5},{5,3},... | collective-permute-start | bytes 786440 | tf_op jit(solution)/shard_map/ppermute | solution.py:726
  (15 other events, 259.7 us)

commit v7 on v5

--- a/solution.py
+++ b/solution.py
@@ -739,7 +739,7 @@
     far_a = lax.ppermute(own_a, "inner", SWAP)
     pay2 = jnp.where(is_mid, m1, end2)
     end3 = jnp.concatenate([as_tiles(far_a), sky_a])
-    own_b, far_a, m1, end3 = lax.optimization_barrier((own_b, far_a, m1, end3))
+    own_b, far_a, end3 = lax.optimization_barrier((own_b, far_a, end3))
     (r2,) = ends(pay2)
     (m2,) = mids(r1)
     far_b = lax.ppermute(own_b, "inner", SWAP)

time: 156 us -> 156 us (level)
    ppermute x1, waiting for transfers between devices: 0.01 us -> 2.11 us  [line_body(): far_b = lax.ppermute(own_b, 'inner', SWAP)]
    ppermute x11, waiting for transfers between devices: 50.1 us -> 48 us  [ends(): return [lax.ppermute(value, 'outer', ENDS) for value in values]]
  transfers between devices with their start and end apart: 31 -> 31, of which waited for: 18 -> 19; matrix products, arithmetic and copies ran while one was open for 10% -> 10% of each run, Pallas kernels for 12% -> 12%
where the time goes in v7:
time: 156 us
  waiting for transfers between devices  60.3 us (39%)
  starting transfers between devices  46.7 us (30%)
  Pallas kernels  28.1 us (18%)
  local copies, waits for them, and re-layouts  10.7 us (7%)
  other arithmetic  8.72 us (6%)
    ppermute x11, waiting for transfers between devices, ends(): return [lax.ppermute(value, 'outer', ENDS) for value in values]  48 us
    ppermute x11, starting transfers between devices, ends(): return [lax.ppermute(value, 'outer', ENDS) for value in values]  34.9 us
    pallas_call x1, Pallas kernels, adjoint(): pl.pallas_call(functools.partial(adjoint_kernel, slots, ends_only), grid=...  5.88 us
    pallas_call x1, Pallas kernels, late(): pl.pallas_call(late_kernel, grid=(4,), in_specs=[pl.BlockSpec(memory_spac...  5.27 us
    pallas_call x2, Pallas kernels, first_adjoint(): pl.pallas_call(functools.partial(first_kernel, slot), grid=(steps,), in_s...  3.94 us
    pallas_call x2, Pallas kernels, final(): pl.pallas_call(final_b_kernel, grid=(steps,), in_specs=[smem, each, each,...  3.74 us
  transfers between devices with their start and end apart: 31, of which 19 were waited for; matrix products, arithmetic and copies ran while one was open for 10% of the time, Pallas kernels for 12%

profile of v7, /device:TPU:0, one launch (start us, length us, event | category | flops | bytes accessed | tf_op | source)
XLA Modules:
  0.0 155.5 jit_solution(11491085618672190371)
XLA Ops:
  0.0 1.9 %reshape_squeeze.3 = bf16[64,2,32,128]{3,2,1,0:T(8,128)(2,1)S(1)} reshape(bf16[1,64,2,4096]{3,2,1,0:T(2,128)(2,1)} %param.12) | data formatting | bytes 2097152 | tf_op jit(solution)/shard_map/reshape;squeeze | solution.py:719
  2.7 3.1 %collective-permute-start.1 = (bf16[24,128,128]{2,1,0:T(8,128)(2,1)S(1)}, bf16[24,128,128]{2,1,0:T(8,128)(2,1)}, u32[]{:S(2)}, u32[]{:S(2)}) collective-permute-start(bf16[24,128,128]{2,1,0:T(8,128)(2,1)S(1)} %bitcast.44), channel_id=1, source_target_pairs={{0,2},{2,0},{4,6},{6,4},{1,3},{3,1},{5,7},{7,5},{8,10},{10,8},{12,... | collective-permute-start | bytes 2359304 | tf_op jit(solution)/shard_map/ppermute | solution.py:723
  7.0 2.1 %multiply_bitcast_fusion.1.own_a = bf16[2,1024,128]{2,1,0:T(8,128)(2,1)} fusion(bf16[1,1,2,4096,128]{4,3,2,1,0:T(8,128)(2,1)} %param.13, bf16[]{:T(256)S(6)} %convert_element_type.55), kind=kLoop, calls=%fused_computation.15 | loop fusion | flops 262144 | bytes 1048578 | tf_op jit(solution)/shard_map/mul | solution.py:735
  9.1 2.0 %pad_maximum_fusion.1 = bf16[24,128,128]{2,1,0:T(8,128)(2,1)} fusion(bf16[8,128,128]{2,1,0:T(8,128)(2,1)S(1)} %bitcast.48, bf16[16,128,128]{2,1,0:T(8,128)(2,1)} %bitcast.8), kind=kLoop, calls=%fused_computation.7 | loop fusion | flops 393216 | bytes 1572864 | tf_op jit(solution)/shard_map/concatenate | solution.py:737
  12.6 10.9 %collective-permute-done.1.slot1 = bf16[24,128,128]{2,1,0:T(8,128)(2,1)} collective-permute-done((bf16[24,128,128]{2,1,0:T(8,128)(2,1)S(1)}, bf16[24,128,128]{2,1,0:T(8,128)(2,1)}, u32[]{:S(2)}, u32[]{:S(2)}) %collective-permute-start.1) | collective-permute-done | bytes 786464 | tf_op jit(solution)/shard_map/ppermute | solution.py:723
  23.6 2.1 %collective-permute-done.far_a = bf16[2,1024,128]{2,1,0:T(8,128)(2,1)} collective-permute-done((bf16[2,1024,128]{2,1,0:T(8,128)(2,1)}, bf16[2,1024,128]{2,1,0:T(8,128)(2,1)}, u32[]{:S(2)}, u32[]{:S(2)}) %collective-permute-start) | collective-permute-done | bytes 524320 | tf_op jit(solution)/shard_map/ppermute | solution.py:739
  26.9 1.6 %collective-permute-start.4 = (bf16[2,3072,128]{2,1,0:T(8,128)(2,1)S(1)}, bf16[2,3072,128]{2,1,0:T(8,128)(2,1)}, u32[]{:S(2)}, u32[]{:S(2)}) collective-permute-start(bf16[2,3072,128]{2,1,0:T(8,128)(2,1)S(1)} %multiply_bitcast_fusion.own_k), channel_id=1, source_target_pairs={{0,1},{1,0},{2,3},{3,2},{4,5},{5,4},{6,7},{7,6},{8,9},{9,8},{10,11... | collective-permute-start | bytes 4718600 | tf_op jit(solution)/shard_map/ppermute | solution.py:745
  28.6 2.0 %collective-permute-start.3 = (bf16[24,128,128]{2,1,0:T(8,128)(2,1)S(1)}, bf16[24,128,128]{2,1,0:T(8,128)(2,1)S(1)}, u32[]{:S(2)}, u32[]{:S(2)}) collective-permute-start(bf16[24,128,128]{2,1,0:T(8,128)(2,1)S(1)} %broadcast_select_fusion.1), channel_id=1, source_target_pairs={{0,2},{2,0},{4,6},{6,4},{1,3},{3,1},{5,7},{7,5},{8,10},{10,8},{12,... | collective-permute-start | bytes 2359304 | tf_op jit(solution)/shard_map/ppermute | solution.py:723
  31.6 14.4 %collective-permute-start.6 = (bf16[24,128,128]{2,1,0:T(8,128)(2,1)}, bf16[24,128,128]{2,1,0:T(8,128)(2,1)}, u32[]{:S(2)}, u32[]{:S(2)}) collective-permute-start(bf16[24,128,128]{2,1,0:T(8,128)(2,1)} %broadcast_select_fusion), channel_id=1, source_target_pairs={{0,2},{2,0},{4,6},{6,4},{1,3},{3,1},{5,7},{7,5},{8,10},{10,8},{12,... | collective-permute-start | bytes 2359304 | tf_op jit(solution)/shard_map/ppermute | solution.py:723
  46.0 3.1 %collective-permute-done.3.end2.near_sky.near_k = bf16[24,128,128]{2,1,0:T(8,128)(2,1)S(1)} collective-permute-done((bf16[24,128,128]{2,1,0:T(8,128)(2,1)S(1)}, bf16[24,128,128]{2,1,0:T(8,128)(2,1)S(1)}, u32[]{:S(2)}, u32[]{:S(2)}) %collective-permute-start.3) | collective-permute-done | bytes 786464 | tf_op jit(solution)/shard_map/ppermute | solution.py:723
  58.1 2.8 %early.1.done = f32[384,256]{1,0:T(8,128)S(1)} custom-call(s32[8]{0:T(128)S(1)} %concatenate.12.place, bf16[2,3072,128]{2,1,0:T(8,128)(2,1)S(1)} %multiply_bitcast_fusion.own_k, bf16[24,128,128]{2,1,0:T(8,128)(2,1)S(1)} %bitcast.46, bf16[24,128,128]{2,1,0:T(8,128)(2,1)} %collective-permute-done.1.slot1, ...), custom_call_target="tpu_custom_call" | custom-call | flops 603979776 | bytes 4194304 | tf_op jit(solution)/shard_map/early/pallas_call | solution.py:216
  61.0 2.1 %collective-permute-done.4.far_k = bf16[2,3072,128]{2,1,0:T(8,128)(2,1)} collective-permute-done((bf16[2,3072,128]{2,1,0:T(8,128)(2,1)S(1)}, bf16[2,3072,128]{2,1,0:T(8,128)(2,1)}, u32[]{:S(2)}, u32[]{:S(2)}) %collective-permute-start.4) | collective-permute-done | bytes 1572896 | tf_op jit(solution)/shard_map/ppermute | solution.py:745
  64.5 5.3 %late.1 = (f32[2,2,2,32,256]{4,3,2,1,0:T(8,128)S(1)}, f32[2,2,2,32,256]{4,3,2,1,0:T(8,128)S(1)}, f32[2,2,2,32,256]{4,3,2,1,0:T(8,128)S(1)}, f32[2,2,2,32,256]{4,3,2,1,0:T(8,128)S(1)}) custom-call(s32[8]{0:T(128)S(1)} %concatenate.12.place, f32[384,256]{1,0:T(8,128)S(1)} %early.1.done, bf16[2,3072,128]{2,1,0:T(8,128)(2,1)S(1)} %multiply_bitcast_fusion.own_k, ...), custom_call_target="tpu_custom_call" | custom-call | flops 1006632960 | bytes 9437184 | tf_op jit(solution)/shard_map/late/pallas_call | solution.py:311
  71.4 2.2 %collective-permute-start.10 = (bf16[2,2,2,32,256]{4,3,2,1,0:T(8,128)(2,1)S(1)}, bf16[2,2,2,32,256]{4,3,2,1,0:T(8,128)(2,1)S(1)}, u32[]{:S(2)}, u32[]{:S(2)}) collective-permute-start(bf16[2,2,2,32,256]{4,3,2,1,0:T(8,128)(2,1)S(1)} %near_sum.1), channel_id=1, source_target_pairs={{0,2},{2,0},{4,6},{6,4},{1,3},{3,1},{5,7},{7,5},{8,10},{10,8},{12,... | collective-permute-start | bytes 393224 | tf_op jit(solution)/shard_map/ppermute | solution.py:723
  73.6 3.8 %collective-permute-done.10.near = bf16[2,2,2,32,256]{4,3,2,1,0:T(8,128)(2,1)S(1)} collective-permute-done((bf16[2,2,2,32,256]{4,3,2,1,0:T(8,128)(2,1)S(1)}, bf16[2,2,2,32,256]{4,3,2,1,0:T(8,128)(2,1)S(1)}, u32[]{:S(2)}, u32[]{:S(2)}) %collective-permute-start.10) | collective-permute-done | bytes 131104 | tf_op jit(solution)/shard_map/ppermute | solution.py:723
  82.4 1.7 %collective-permute-done.12.from_y = f32[2,32,256]{2,1,0:T(8,128)S(1)} collective-permute-done((f32[2,32,256]{2,1,0:T(8,128)S(1)}, f32[2,32,256]{2,1,0:T(8,128)S(1)}, u32[]{:S(2)}, u32[]{:S(2)}) %collective-permute-start.12) | collective-permute-done | bytes 65568 | tf_op jit(solution)/shard_map/ppermute | solution.py:766
  87.3 2.5 %collective-permute-start.16 = (bf16[2,32,256]{2,1,0:T(8,128)(2,1)S(1)}, bf16[2,32,256]{2,1,0:T(8,128)(2,1)S(1)}, u32[]{:S(2)}, u32[]{:S(2)}) collective-permute-start(bf16[2,32,256]{2,1,0:T(8,128)(2,1)S(1)} %get-tuple-element.50), channel_id=1, source_target_pairs={{0,17},{1,16},{16,1},{17,0},{2,19},{3,18},{18,3},{19,2},{4,21},{5,... | collective-permute-start | bytes 98312 | tf_op jit(solution)/shard_map/ppermute | solution.py:771
  93.8 1.8 %collective-permute-start.18 = (bf16[2,2,2,32,256]{4,3,2,1,0:T(8,128)(2,1)S(1)}, bf16[2,2,2,32,256]{4,3,2,1,0:T(8,128)(2,1)S(1)}, u32[]{:S(2)}, u32[]{:S(2)}) collective-permute-start(bf16[2,2,2,32,256]{4,3,2,1,0:T(8,128)(2,1)S(1)} %pad_maximum_fusion.3.half), channel_id=1, source_target_pairs={{0,2},{2,0},{4,6},{6,4},{1,3},{3,1},{5,7},{7,5},{8,10},{10,8},{12,... | collective-permute-start | bytes 393224 | tf_op jit(solution)/shard_map/ppermute | solution.py:723
  95.6 2.3 %first_adjoint.2 = bf16[16,128,128]{2,1,0:T(8,128)(2,1)S(1)} custom-call(s32[8]{0:T(128)S(1)} %concatenate.12.place, bf16[2,2,2,32,256]{4,3,2,1,0:T(8,128)(2,1)S(1)} %pad_maximum_fusion.3.half, bf16[2,2,2,32,256]{4,3,2,1,0:T(8,128)(2,1)S(1)} %collective-permute-done.17.other, bf16[2,3072,128]{2,1,0:T(8,128)(2,1)S(1)} %multiply_bitcast_fusion.own_k, ...), custom_call_target="tpu_custom_call" | custom-call | flops 5368709120 | bytes 83886080 | tf_op jit(solution)/shard_map/first_adjoint/pallas_call | solution.py:567
  99.7 1.7 %first_adjoint.3 = bf16[8,128,128]{2,1,0:T(8,128)(2,1)S(1)} custom-call(s32[8]{0:T(128)S(1)} %concatenate.12.place, bf16[2,2,2,32,256]{4,3,2,1,0:T(8,128)(2,1)S(1)} %pad_maximum_fusion.3.half, bf16[2,2,2,32,256]{4,3,2,1,0:T(8,128)(2,1)S(1)} %collective-permute-done.17.other, bf16[2,3072,128]{2,1,0:T(8,128)(2,1)S(1)} %multiply_bitcast_fusion.own_k, ...), custom_call_target="tpu_custom_call" | custom-call | flops 2684354560 | bytes 41943040 | tf_op jit(solution)/shard_map/first_adjoint/pallas_call | solution.py:567
  101.4 1.7 %collective-permute-start.23 = (bf16[8,128,128]{2,1,0:T(8,128)(2,1)S(1)}, bf16[8,128,128]{2,1,0:T(8,128)(2,1)S(1)}, u32[]{:S(2)}, u32[]{:S(2)}) collective-permute-start(bf16[8,128,128]{2,1,0:T(8,128)(2,1)S(1)} %first_adjoint.3), channel_id=1, source_target_pairs={{0,2},{2,0},{4,6},{6,4},{1,3},{3,1},{5,7},{7,5},{8,10},{10,8},{12,... | collective-permute-start | bytes 786440 | tf_op jit(solution)/shard_map/ppermute | solution.py:723
  104.7 5.9 %adjoint.1 = (f32[8,128,128]{2,1,0:T(8,128)S(1)}, f32[16,128,128]{2,1,0:T(8,128)S(1)}, f32[8,128,128]{2,1,0:T(8,128)S(1)}, f32[16,128,128]{2,1,0:T(8,128)S(1)}, ...) custom-call(s32[8]{0:T(128)S(1)} %concatenate.12.place, ...), custom_call_target="tpu_custom_call" | custom-call | flops 32212254720 | bytes 251658240 | tf_op jit(solution)/shard_map/adjoint/pallas_call | solution.py:525
  110.7 2.6 %collective-permute-start.22 = (bf16[16,128,128]{2,1,0:T(8,128)(2,1)S(1)}, bf16[16,128,128]{2,1,0:T(8,128)(2,1)S(1)}, u32[]{:S(2)}, u32[]{:S(2)}) collective-permute-start(bf16[16,128,128]{2,1,0:T(8,128)(2,1)S(1)} %convert_element_type.60), channel_id=1, source_target_pairs={{0,2},{2,0},{4,6},{6,4},{1,3},{3,1},{5,7},{7,5},{8,10},{10,8},{12,... | collective-permute-start | bytes 1572872 | tf_op jit(solution)/shard_map/ppermute | solution.py:723
  114.7 3.6 %collective-permute-done.23 = bf16[8,128,128]{2,1,0:T(8,128)(2,1)S(1)} collective-permute-done((bf16[8,128,128]{2,1,0:T(8,128)(2,1)S(1)}, bf16[8,128,128]{2,1,0:T(8,128)(2,1)S(1)}, u32[]{:S(2)}, u32[]{:S(2)}) %collective-permute-start.23) | collective-permute-done | bytes 262176 | tf_op jit(solution)/shard_map/ppermute | solution.py:723
  119.2 2.0 %collective-permute-start.21 = (bf16[8,128,128]{2,1,0:T(8,128)(2,1)S(1)}, bf16[8,128,128]{2,1,0:T(8,128)(2,1)S(1)}, u32[]{:S(2)}, u32[]{:S(2)}) collective-permute-start(bf16[8,128,128]{2,1,0:T(8,128)(2,1)S(1)} %fusion), channel_id=1, source_target_pairs={{0,2},{2,0},{4,6},{6,4},{1,3},{3,1},{5,7},{7,5},{8,10},{10,8},{12,... | collective-permute-start | bytes 786440 | tf_op jit(solution)/shard_map/ppermute | solution.py:723
  121.2 8.3 %collective-permute-done.22 = bf16[16,128,128]{2,1,0:T(8,128)(2,1)S(1)} collective-permute-done((bf16[16,128,128]{2,1,0:T(8,128)(2,1)S(1)}, bf16[16,128,128]{2,1,0:T(8,128)(2,1)S(1)}, u32[]{:S(2)}, u32[]{:S(2)}) %collective-permute-start.22) | collective-permute-done | bytes 524320 | tf_op jit(solution)/shard_map/ppermute | solution.py:723
  129.5 4.8 %collective-permute-done.21.end_a = bf16[8,128,128]{2,1,0:T(8,128)(2,1)S(1)} collective-permute-done((bf16[8,128,128]{2,1,0:T(8,128)(2,1)S(1)}, bf16[8,128,128]{2,1,0:T(8,128)(2,1)S(1)}, u32[]{:S(2)}, u32[]{:S(2)}) %collective-permute-start.21) | collective-permute-done | bytes 262176 | tf_op jit(solution)/shard_map/ppermute | solution.py:723
  134.7 3.2 %collective-permute-start.29 = (bf16[16,128,128]{2,1,0:T(8,128)(2,1)S(1)}, bf16[16,128,128]{2,1,0:T(8,128)(2,1)S(1)}, u32[]{:S(2)}, u32[]{:S(2)}) collective-permute-start(bf16[16,128,128]{2,1,0:T(8,128)(2,1)S(1)} %add_convert_fusion.1), channel_id=1, source_target_pairs={{0,2},{2,0},{4,6},{6,4},{1,3},{3,1},{5,7},{7,5},{8,10},{10,8},{12,... | collective-permute-start | bytes 1572872 | tf_op jit(solution)/shard_map/ppermute | solution.py:723
  139.5 1.7 %final_a.1.before = f32[64,2,4096]{2,1,0:T(2,128)} custom-call(s32[8]{0:T(128)S(1)} %concatenate.12.place, f32[8,128,128]{2,1,0:T(8,128)S(1)} %get-tuple-element.66.part_a, bf16[16,128,128]{2,1,0:T(8,128)(2,1)S(1)} %collective-permute-done.20.peer_a, bf16[8,128,128]{2,1,0:T(8,128)(2,1)S(1)} %collective-permute-done.21.end_a), custom_call_target="tpu_custom_call" | custom-call | flops 262144 | bytes 1048576 | tf_op jit(solution)/shard_map/final_a/pallas_call | solution.py:665
  141.2 9.5 %collective-permute-done.29.near = bf16[16,128,128]{2,1,0:T(8,128)(2,1)S(1)} collective-permute-done((bf16[16,128,128]{2,1,0:T(8,128)(2,1)S(1)}, bf16[16,128,128]{2,1,0:T(8,128)(2,1)S(1)}, u32[]{:S(2)}, u32[]{:S(2)}) %collective-permute-start.29) | collective-permute-done | bytes 524320 | tf_op jit(solution)/shard_map/ppermute | solution.py:723
  150.7 2.1 %final_b.2.before = f32[64,2,4096]{2,1,0:T(2,128)} custom-call(s32[8]{0:T(128)S(1)} %concatenate.12.place, f32[16,128,128]{2,1,0:T(8,128)S(1)} %get-tuple-element.62.part, bf16[16,128,128]{2,1,0:T(8,128)(2,1)S(1)} %collective-permute-done.29.near, bf16[16,128,128]{2,1,0:T(8,128)(2,1)S(1)} %collective-permute-done.30.far, ...), custom_call_target="tpu_custom_call", output_to_operand_aliasing={{}: (4, {})} | custom-call | flops 786432 | bytes 2097152 | tf_op jit(solution)/shard_map/final_b/pallas_call | solution.py:677
  153.9 1.7 %final_b.3 = f32[64,2,4096]{2,1,0:T(2,128)} custom-call(s32[8]{0:T(128)S(1)} %concatenate.12.place, f32[8,128,128]{2,1,0:T(8,128)S(1)} %get-tuple-element.53.part, bf16[8,128,128]{2,1,0:T(8,128)(2,1)S(1)} %collective-permute-done.27.near, bf16[8,128,128]{2,1,0:T(8,128)(2,1)S(1)} %collective-permute-done.28.far, ...), custom_call_target="tpu_custom_call", output_to_operand_aliasing={{}: (4, {})} | custom-call | flops 393216 | bytes 1048576 | tf_op jit(solution)/shard_map/final_b/pallas_call | solution.py:677
  (112 shorter events, 38.3 us)
Async XLA Ops:
  0.0 52.5 %copy-start = (bf16[1,2,128,512]{3,2,1,0:T(8,128)(2,1)S(1)}, bf16[1,2,128,512]{3,2,1,0:T(8,128)(2,1)}, u32[]{:S(2)}) copy-start(bf16[1,2,128,512]{3,2,1,0:T(8,128)(2,1)} %param.14) | copy-start | bytes 786436
  2.7 20.7 %collective-permute-start.1 = (bf16[24,128,128]{2,1,0:T(8,128)(2,1)S(1)}, bf16[24,128,128]{2,1,0:T(8,128)(2,1)}, u32[]{:S(2)}, u32[]{:S(2)}) collective-permute-start(bf16[24,128,128]{2,1,0:T(8,128)(2,1)S(1)} %bitcast.44), channel_id=1, source_target_pairs={{0,2},{2,0},{4,6},{6,4},{1,3},{3,1},{5,7},{7,5},{8,10},{10,8},{12,... | collective-permute-start | bytes 2359304 | tf_op jit(solution)/shard_map/ppermute | solution.py:723
  5.8 22.7 %collective-permute-start.2 = (bf16[24,128,128]{2,1,0:T(8,128)(2,1)S(1)}, bf16[24,128,128]{2,1,0:T(8,128)(2,1)S(1)}, u32[]{:S(2)}, u32[]{:S(2)}) collective-permute-start(bf16[24,128,128]{2,1,0:T(8,128)(2,1)S(1)} %bitcast.45), channel_id=1, source_target_pairs={{2,4},{4,2},{10,12},{12,10},{0,8},{8,0},{6,14},{14,6},{3,5},{5,3},... | collective-permute-start | bytes 2359304 | tf_op jit(solution)/shard_map/ppermute | solution.py:726
  11.1 14.7 %collective-permute-start = (bf16[2,1024,128]{2,1,0:T(8,128)(2,1)}, bf16[2,1024,128]{2,1,0:T(8,128)(2,1)}, u32[]{:S(2)}, u32[]{:S(2)}) collective-permute-start(bf16[2,1024,128]{2,1,0:T(8,128)(2,1)} %multiply_bitcast_fusion.1.own_a), channel_id=1, source_target_pairs={{0,1},{1,0},{2,3},{3,2},{4,5},{5,4},{6,7},{7,6},{8,9},{9,8},{10,11... | collective-permute-start | bytes 1572872 | tf_op jit(solution)/shard_map/ppermute | solution.py:739
  23.4 7.2 %collective-permute-start.5 = (bf16[24,128,128]{2,1,0:T(8,128)(2,1)}, bf16[24,128,128]{2,1,0:T(8,128)(2,1)}, u32[]{:S(2)}, u32[]{:S(2)}) collective-permute-start(bf16[24,128,128]{2,1,0:T(8,128)(2,1)} %collective-permute-done.1.slot1), channel_id=1, source_target_pairs={{2,4},{4,2},{10,12},{12,10},{0,8},{8,0},{6,14},{14,6},{3,5},{5,3},... | collective-permute-start | bytes 2359304 | tf_op jit(solution)/shard_map/ppermute | solution.py:726
  26.9 36.2 %collective-permute-start.4 = (bf16[2,3072,128]{2,1,0:T(8,128)(2,1)S(1)}, bf16[2,3072,128]{2,1,0:T(8,128)(2,1)}, u32[]{:S(2)}, u32[]{:S(2)}) collective-permute-start(bf16[2,3072,128]{2,1,0:T(8,128)(2,1)S(1)} %multiply_bitcast_fusion.own_k), channel_id=1, source_target_pairs={{0,1},{1,0},{2,3},{3,2},{4,5},{5,4},{6,7},{7,6},{8,9},{9,8},{10,11... | collective-permute-start | bytes 4718600 | tf_op jit(solution)/shard_map/ppermute | solution.py:745
  28.6 20.5 %collective-permute-start.3 = (bf16[24,128,128]{2,1,0:T(8,128)(2,1)S(1)}, bf16[24,128,128]{2,1,0:T(8,128)(2,1)S(1)}, u32[]{:S(2)}, u32[]{:S(2)}) collective-permute-start(bf16[24,128,128]{2,1,0:T(8,128)(2,1)S(1)} %broadcast_select_fusion.1), channel_id=1, source_target_pairs={{0,2},{2,0},{4,6},{6,4},{1,3},{3,1},{5,7},{7,5},{8,10},{10,8},{12,... | collective-permute-start | bytes 2359304 | tf_op jit(solution)/shard_map/ppermute | solution.py:723
  31.6 33.0 %collective-permute-start.6 = (bf16[24,128,128]{2,1,0:T(8,128)(2,1)}, bf16[24,128,128]{2,1,0:T(8,128)(2,1)}, u32[]{:S(2)}, u32[]{:S(2)}) collective-permute-start(bf16[24,128,128]{2,1,0:T(8,128)(2,1)} %broadcast_select_fusion), channel_id=1, source_target_pairs={{0,2},{2,0},{4,6},{6,4},{1,3},{3,1},{5,7},{7,5},{8,10},{10,8},{12,... | collective-permute-start | bytes 2359304 | tf_op jit(solution)/shard_map/ppermute | solution.py:723
  50.0 11.0 %collective-permute-start.7 = (bf16[16,128,128]{2,1,0:T(8,128)(2,1)}, bf16[16,128,128]{2,1,0:T(8,128)(2,1)}, u32[]{:S(2)}, u32[]{:S(2)}) collective-permute-start(bf16[16,128,128]{2,1,0:T(8,128)(2,1)} %pad_maximum_fusion.2), channel_id=1, source_target_pairs={{2,4},{4,2},{10,12},{12,10},{0,8},{8,0},{6,14},{14,6},{3,5},{5,3},... | collective-permute-start | bytes 1572872 | tf_op jit(solution)/shard_map/ppermute | solution.py:726
  69.8 1.6 %collective-permute-start.9 = (f32[2,2,2,32,256]{4,3,2,1,0:T(8,128)S(1)}, f32[2,2,2,32,256]{4,3,2,1,0:T(8,128)S(1)}, u32[]{:S(2)}, u32[]{:S(2)}) collective-permute-start(f32[2,2,2,32,256]{4,3,2,1,0:T(8,128)S(1)} %get-tuple-element.44), channel_id=1, source_target_pairs={{0,8},{8,0},{1,9},{9,1},{2,10},{10,2},{3,11},{11,3},{4,12},{12,4},... | collective-permute-start | bytes 786440 | tf_op jit(solution)/shard_map/ppermute | solution.py:762
  69.9 3.8 %collective-permute-start.8 = (f32[2,2,2,32,256]{4,3,2,1,0:T(8,128)S(1)}, f32[2,2,2,32,256]{4,3,2,1,0:T(8,128)S(1)}, u32[]{:S(2)}, u32[]{:S(2)}) collective-permute-start(f32[2,2,2,32,256]{4,3,2,1,0:T(8,128)S(1)} %get-tuple-element.42), channel_id=1, source_target_pairs={{0,8},{8,0},{1,9},{9,1},{2,10},{10,2},{3,11},{11,3},{4,12},{12,4},... | collective-permute-start | bytes 786440 | tf_op jit(solution)/shard_map/ppermute | solution.py:763
  71.4 6.0 %collective-permute-start.10 = (bf16[2,2,2,32,256]{4,3,2,1,0:T(8,128)(2,1)S(1)}, bf16[2,2,2,32,256]{4,3,2,1,0:T(8,128)(2,1)S(1)}, u32[]{:S(2)}, u32[]{:S(2)}) collective-permute-start(bf16[2,2,2,32,256]{4,3,2,1,0:T(8,128)(2,1)S(1)} %near_sum.1), channel_id=1, source_target_pairs={{0,2},{2,0},{4,6},{6,4},{1,3},{3,1},{5,7},{7,5},{8,10},{10,8},{12,... | collective-permute-start | bytes 393224 | tf_op jit(solution)/shard_map/ppermute | solution.py:723
  78.0 4.3 %collective-permute-start.11 = (f32[2,32,256]{2,1,0:T(8,128)S(1)}, f32[2,32,256]{2,1,0:T(8,128)S(1)}, u32[]{:S(2)}, u32[]{:S(2)}) collective-permute-start(f32[2,32,256]{2,1,0:T(8,128)S(1)} %get-tuple-element.46), channel_id=1, source_target_pairs={{0,16},{16,0},{1,17},{17,1},{2,18},{18,2},{3,19},{19,3},{4,20},{20... | collective-permute-start | bytes 196616 | tf_op jit(solution)/shard_map/ppermute | solution.py:765
  79.6 4.5 %collective-permute-start.12 = (f32[2,32,256]{2,1,0:T(8,128)S(1)}, f32[2,32,256]{2,1,0:T(8,128)S(1)}, u32[]{:S(2)}, u32[]{:S(2)}) collective-permute-start(f32[2,32,256]{2,1,0:T(8,128)S(1)} %get-tuple-element.47), channel_id=1, source_target_pairs={{0,1},{1,0},{2,3},{3,2},{4,5},{5,4},{6,7},{7,6},{8,9},{9,8},{10,11... | collective-permute-start | bytes 196616 | tf_op jit(solution)/shard_map/ppermute | solution.py:766
  80.1 5.2 %collective-permute-start.13 = (f32[2,32,256]{2,1,0:T(8,128)S(1)}, f32[2,32,256]{2,1,0:T(8,128)S(1)}, u32[]{:S(2)}, u32[]{:S(2)}) collective-permute-start(f32[2,32,256]{2,1,0:T(8,128)S(1)} %get-tuple-element.48), channel_id=1, source_target_pairs={{0,17},{1,16},{16,1},{17,0},{2,19},{3,18},{18,3},{19,2},{4,21},{5,... | collective-permute-start | bytes 196616 | tf_op jit(solution)/shard_map/ppermute | solution.py:767
  86.7 4.0 %collective-permute-start.15 = (bf16[2,32,256]{2,1,0:T(8,128)(2,1)S(1)}, bf16[2,32,256]{2,1,0:T(8,128)(2,1)S(1)}, u32[]{:S(2)}, u32[]{:S(2)}) collective-permute-start(bf16[2,32,256]{2,1,0:T(8,128)(2,1)S(1)} %get-tuple-element.49), channel_id=1, source_target_pairs={{0,16},{16,0},{1,17},{17,1},{2,18},{18,2},{3,19},{19,3},{4,20},{20... | collective-permute-start | bytes 98312 | tf_op jit(solution)/shard_map/ppermute | solution.py:769
  87.3 4.8 %collective-permute-start.16 = (bf16[2,32,256]{2,1,0:T(8,128)(2,1)S(1)}, bf16[2,32,256]{2,1,0:T(8,128)(2,1)S(1)}, u32[]{:S(2)}, u32[]{:S(2)}) collective-permute-start(bf16[2,32,256]{2,1,0:T(8,128)(2,1)S(1)} %get-tuple-element.50), channel_id=1, source_target_pairs={{0,17},{1,16},{16,1},{17,0},{2,19},{3,18},{18,3},{19,2},{4,21},{5,... | collective-permute-start | bytes 98312 | tf_op jit(solution)/shard_map/ppermute | solution.py:771
  89.7 3.9 %collective-permute-start.14 = (bf16[2,32,256]{2,1,0:T(8,128)(2,1)S(1)}, bf16[2,32,256]{2,1,0:T(8,128)(2,1)S(1)}, u32[]{:S(2)}, u32[]{:S(2)}) collective-permute-start(bf16[2,32,256]{2,1,0:T(8,128)(2,1)S(1)} %get-tuple-element.50), channel_id=1, source_target_pairs={{0,1},{1,0},{2,3},{3,2},{4,5},{5,4},{6,7},{7,6},{8,9},{9,8},{10,11... | collective-permute-start | bytes 98312 | tf_op jit(solution)/shard_map/ppermute | solution.py:770
  93.7 1.9 %collective-permute-start.17 = (bf16[2,2,2,32,256]{4,3,2,1,0:T(8,128)(2,1)S(1)}, bf16[2,2,2,32,256]{4,3,2,1,0:T(8,128)(2,1)S(1)}, u32[]{:S(2)}, u32[]{:S(2)}) collective-permute-start(bf16[2,2,2,32,256]{4,3,2,1,0:T(8,128)(2,1)S(1)} %pad_maximum_fusion.3.half), channel_id=1, source_target_pairs={{0,8},{8,0},{1,9},{9,1},{2,10},{10,2},{3,11},{11,3},{4,12},{12,4},... | collective-permute-start | bytes 393224 | tf_op jit(solution)/shard_map/ppermute | solution.py:773
  93.8 5.9 %collective-permute-start.18 = (bf16[2,2,2,32,256]{4,3,2,1,0:T(8,128)(2,1)S(1)}, bf16[2,2,2,32,256]{4,3,2,1,0:T(8,128)(2,1)S(1)}, u32[]{:S(2)}, u32[]{:S(2)}) collective-permute-start(bf16[2,2,2,32,256]{4,3,2,1,0:T(8,128)(2,1)S(1)} %pad_maximum_fusion.3.half), channel_id=1, source_target_pairs={{0,2},{2,0},{4,6},{6,4},{1,3},{3,1},{5,7},{7,5},{8,10},{10,8},{12,... | collective-permute-start | bytes 393224 | tf_op jit(solution)/shard_map/ppermute | solution.py:723
  97.8 20.6 %collective-permute-start.25 = (bf16[16,128,128]{2,1,0:T(8,128)(2,1)S(1)}, bf16[16,128,128]{2,1,0:T(8,128)(2,1)S(1)}, u32[]{:S(2)}, u32[]{:S(2)}) collective-permute-start(bf16[16,128,128]{2,1,0:T(8,128)(2,1)S(1)} %first_adjoint.2), channel_id=1, source_target_pairs={{0,2},{2,0},{4,6},{6,4},{1,3},{3,1},{5,7},{7,5},{8,10},{10,8},{12,... | collective-permute-start | bytes 1572872 | tf_op jit(solution)/shard_map/ppermute | solution.py:723
  99.7 3.4 %collective-permute-start.19 = (bf16[2,2,2,32,256]{4,3,2,1,0:T(8,128)(2,1)S(1)}, bf16[2,2,2,32,256]{4,3,2,1,0:T(8,128)(2,1)S(1)}, u32[]{:S(2)}, u32[]{:S(2)}) collective-permute-start(bf16[2,2,2,32,256]{4,3,2,1,0:T(8,128)(2,1)S(1)} %collective-permute-done.18.near_half), channel_id=1, source_target_pairs={{0,8},{8,0},{1,9},{9,1},{2,10},{10,2},{3,11},{11,3},{4,12},{12,4},... | collective-permute-start | bytes 393224 | tf_op jit(solution)/shard_map/ppermute | solution.py:784
  101.4 16.9 %collective-permute-start.23 = (bf16[8,128,128]{2,1,0:T(8,128)(2,1)S(1)}, bf16[8,128,128]{2,1,0:T(8,128)(2,1)S(1)}, u32[]{:S(2)}, u32[]{:S(2)}) collective-permute-start(bf16[8,128,128]{2,1,0:T(8,128)(2,1)S(1)} %first_adjoint.3), channel_id=1, source_target_pairs={{0,2},{2,0},{4,6},{6,4},{1,3},{3,1},{5,7},{7,5},{8,10},{10,8},{12,... | collective-permute-start | bytes 786440 | tf_op jit(solution)/shard_map/ppermute | solution.py:723
  104.4 14.7 %collective-permute-start.20 = (bf16[16,128,128]{2,1,0:T(8,128)(2,1)S(1)}, bf16[16,128,128]{2,1,0:T(8,128)(2,1)S(1)}, u32[]{:S(2)}, u32[]{:S(2)}) collective-permute-start(bf16[16,128,128]{2,1,0:T(8,128)(2,1)S(1)} %near_adjoint.2), channel_id=1, source_target_pairs={{2,4},{4,2},{10,12},{12,10},{0,8},{8,0},{6,14},{14,6},{3,5},{5,3},... | collective-permute-start | bytes 1572872 | tf_op jit(solution)/shard_map/ppermute | solution.py:726
  110.7 18.8 %collective-permute-start.22 = (bf16[16,128,128]{2,1,0:T(8,128)(2,1)S(1)}, bf16[16,128,128]{2,1,0:T(8,128)(2,1)S(1)}, u32[]{:S(2)}, u32[]{:S(2)}) collective-permute-start(bf16[16,128,128]{2,1,0:T(8,128)(2,1)S(1)} %convert_element_type.60), channel_id=1, source_target_pairs={{0,2},{2,0},{4,6},{6,4},{1,3},{3,1},{5,7},{7,5},{8,10},{10,8},{12,... | collective-permute-start | bytes 1572872 | tf_op jit(solution)/shard_map/ppermute | solution.py:723
  118.3 2.9 %collective-permute-start.24 = (bf16[8,128,128]{2,1,0:T(8,128)(2,1)S(1)}, bf16[8,128,128]{2,1,0:T(8,128)(2,1)S(1)}, u32[]{:S(2)}, u32[]{:S(2)}) collective-permute-start(bf16[8,128,128]{2,1,0:T(8,128)(2,1)S(1)} %add_convert_fusion.5), channel_id=1, source_target_pairs={{2,4},{4,2},{10,12},{12,10},{0,8},{8,0},{6,14},{14,6},{3,5},{5,3},... | collective-permute-start | bytes 786440 | tf_op jit(solution)/shard_map/ppermute | solution.py:726
  118.6 15.8 %collective-permute-start.26 = (bf16[16,128,128]{2,1,0:T(8,128)(2,1)S(1)}, bf16[16,128,128]{2,1,0:T(8,128)(2,1)S(1)}, u32[]{:S(2)}, u32[]{:S(2)}) collective-permute-start(bf16[16,128,128]{2,1,0:T(8,128)(2,1)S(1)} %add_convert_fusion.2), channel_id=1, source_target_pairs={{2,4},{4,2},{10,12},{12,10},{0,8},{8,0},{6,14},{14,6},{3,5},{5,3},... | collective-permute-start | bytes 1572872 | tf_op jit(solution)/shard_map/ppermute | solution.py:726
  119.2 15.2 %collective-permute-start.21 = (bf16[8,128,128]{2,1,0:T(8,128)(2,1)S(1)}, bf16[8,128,128]{2,1,0:T(8,128)(2,1)S(1)}, u32[]{:S(2)}, u32[]{:S(2)}) collective-permute-start(bf16[8,128,128]{2,1,0:T(8,128)(2,1)S(1)} %fusion), channel_id=1, source_target_pairs={{0,2},{2,0},{4,6},{6,4},{1,3},{3,1},{5,7},{7,5},{8,10},{10,8},{12,... | collective-permute-start | bytes 786440 | tf_op jit(solution)/shard_map/ppermute | solution.py:723
  134.7 16.0 %collective-permute-start.29 = (bf16[16,128,128]{2,1,0:T(8,128)(2,1)S(1)}, bf16[16,128,128]{2,1,0:T(8,128)(2,1)S(1)}, u32[]{:S(2)}, u32[]{:S(2)}) collective-permute-start(bf16[16,128,128]{2,1,0:T(8,128)(2,1)S(1)} %add_convert_fusion.1), channel_id=1, source_target_pairs={{0,2},{2,0},{4,6},{6,4},{1,3},{3,1},{5,7},{7,5},{8,10},{10,8},{12,... | collective-permute-start | bytes 1572872 | tf_op jit(solution)/shard_map/ppermute | solution.py:723
  137.9 12.8 %collective-permute-start.30 = (bf16[16,128,128]{2,1,0:T(8,128)(2,1)S(1)}, bf16[16,128,128]{2,1,0:T(8,128)(2,1)S(1)}, u32[]{:S(2)}, u32[]{:S(2)}) collective-permute-start(bf16[16,128,128]{2,1,0:T(8,128)(2,1)S(1)} %add_convert_fusion), channel_id=1, source_target_pairs={{2,4},{4,2},{10,12},{12,10},{0,8},{8,0},{6,14},{14,6},{3,5},{5,3},... | collective-permute-start | bytes 1572872 | tf_op jit(solution)/shard_map/ppermute | solution.py:726
  138.0 15.8 %collective-permute-start.27 = (bf16[8,128,128]{2,1,0:T(8,128)(2,1)S(1)}, bf16[8,128,128]{2,1,0:T(8,128)(2,1)S(1)}, u32[]{:S(2)}, u32[]{:S(2)}) collective-permute-start(bf16[8,128,128]{2,1,0:T(8,128)(2,1)S(1)} %add_convert_fusion.4), channel_id=1, source_target_pairs={{0,2},{2,0},{4,6},{6,4},{1,3},{3,1},{5,7},{7,5},{8,10},{10,8},{12,... | collective-permute-start | bytes 786440 | tf_op jit(solution)/shard_map/ppermute | solution.py:723
  139.5 14.3 %collective-permute-start.28 = (bf16[8,128,128]{2,1,0:T(8,128)(2,1)S(1)}, bf16[8,128,128]{2,1,0:T(8,128)(2,1)S(1)}, u32[]{:S(2)}, u32[]{:S(2)}) collective-permute-start(bf16[8,128,128]{2,1,0:T(8,128)(2,1)S(1)} %add_convert_fusion.3), channel_id=1, source_target_pairs={{2,4},{4,2},{10,12},{12,10},{0,8},{8,0},{6,14},{14,6},{3,5},{5,3},... | collective-permute-start | bytes 786440 | tf_op jit(solution)/shard_map/ppermute | solution.py:726
  (15 other events, 259.7 us)
